TPU v7x, 32 devices: a whole 2x2x4 slice. The times are simulated.
32 devices in a mesh: groups: 2 (over y), brick: 16 (over z, x, core).
Axes of the slice: x: 2, y: 2, z: 4, core: 2. Of those that a mesh axis runs over, the one named last changes fastest.
Arguments:
- ct_win: bfloat16 [64, 128, 768], P(('groups', 'brick')), parts along dimension 0, may hold values from -8 to 8
- pet_win: bfloat16 [64, 128, 768], P(('groups', 'brick')), parts along dimension 0, may hold values from -8 to 8
- placed_anchor: int32 [64], P('groups'), parts along dimension 0, may hold values from 0 to 12, as said below
- placed_count: int32 [64], P('groups'), parts along dimension 0, may hold values from 0 to 256, as said below
- norm_ct: float32 [768], replicated, may hold values from 0.1 to 1.9
- norm_pet: float32 [768], replicated, may hold values from 0.1 to 1.9
- norm_ffn: float32 [768], replicated, may hold values from 0.1 to 1.9
- w_query: bfloat16 [768, 768], replicated, may hold values from -2 to 2
- w_key: bfloat16 [768, 768], replicated, may hold values from -2 to 2
- w_value: bfloat16 [768, 768], replicated, may hold values from -0.21875 to 0.21875
- w_out: bfloat16 [768, 768], replicated, may hold values from -0.21875 to 0.21875
- w_up: bfloat16 [768, 1536], replicated, may hold values from -0.21875 to 0.21875
- w_down: bfloat16 [1536, 768], replicated, may hold values from -0.15625 to 0.15625
- w_upconv: bfloat16 [768, 1024], replicated, may hold values from -0.21875 to 0.21875
- w_conv: bfloat16 [3456, 128], replicated, may hold values from -0.109375 to 0.109375
Outputs:
- volume: bfloat16 [64, 8, 16, 128], P(('groups', 'brick')), parts along dimension 0
There are 2 independent parts, one for each index of `groups`. A program takes and returns all parts, laid end to end along the dimension named above; an argument that names none is the same for every part. Nothing has to cross between parts.
Inputs may be any that keep to these rules, and one draw needn't show every extreme that they name: `placed_anchor`: windows may lie anywhere in depth, whichever device holds them. `placed_count`: on each device the live slots (count above 0) are its first slots, at least one; in every draw some device has all 2 slots live and some device only one; a live window's count is 1 to 256, and 256 occurs in every draw.
All inputs are finite; a program needn't handle non-finite values.
Results may differ from a plain program's by a relative error of at most 0.012.
The roundings to bfloat16 on the way count: a program that leaves them out, or rounds other values in their place, can miss the bound.
Values may be sent and summed in bfloat16 or wider, within the bound.
No kernel may reach another device: no remote copies, remote signals or barrier semaphores. Data moves between devices by JAX's collectives and lax.ppermute only.
A program may use at most 128 MiB of HBM per device.

v0:
```python
import jax
import jax.numpy as jnp
from jax import lax
from jax.sharding import PartitionSpec as P

DH = 64
PY = 4
PX = 8
WDEP = 4


epsilon = 1e-06


def with_halo(cells, sides, width):
    for axis, dim in sides:
        count = lax.axis_size(axis)
        ends = count - 1
        head = lax.slice_in_dim(cells, 0, width, axis=dim)
        tail = lax.slice_in_dim(cells, cells.shape[dim] - width, cells.shape[dim], axis=dim)
        cells = jnp.concatenate(
            [
                lax.ppermute(tail, axis, [(i, (i + 1) % count) for i in range(ends)]),
                cells,
                lax.ppermute(head, axis, [((i + 1) % count, i) for i in range(ends)]),
            ],
            axis=dim,
        )
    return cells


def rms_scale(inputs, gain_vec):
    inputs = inputs.astype(jnp.float32)
    mean_square = jnp.mean(inputs * inputs, axis=-1, keepdims=True)
    return (inputs * lax.rsqrt(mean_square + epsilon) * gain_vec).astype(jnp.bfloat16)


def project(normed, weight):
    return jnp.dot(normed, weight, preferred_element_type=jnp.float32).astype(jnp.bfloat16)


def attend(queries, key_rows, value_rows, head_count):
    slot_total, row_total, model_width = queries.shape
    head_size = model_width // head_count
    query_heads = queries.reshape(slot_total, row_total, head_count, head_size)
    key_heads = key_rows.reshape(slot_total, row_total, head_count, head_size)
    value_heads = value_rows.reshape(slot_total, row_total, head_count, head_size)
    scores = (
        jnp.einsum("swhd,svhd->shwv", query_heads, key_heads, preferred_element_type=jnp.float32)
        / head_size**0.5
    )
    row_max = jnp.max(scores, axis=-1, keepdims=True)
    exp_scores = jnp.exp(scores - row_max)
    attn_probs = (exp_scores / jnp.sum(exp_scores, axis=-1, keepdims=True)).astype(jnp.bfloat16)
    mixed_out = jnp.einsum(
        "shwv,svhd->swhd", attn_probs, value_heads, preferred_element_type=jnp.float32
    )
    return mixed_out.reshape(slot_total, row_total, model_width).astype(jnp.bfloat16)


def feed_forward(middle, norm_ffn, w_up, w_down):
    normed = rms_scale(middle, norm_ffn)
    hidden = jax.nn.gelu(
        jnp.dot(normed, w_up, preferred_element_type=jnp.float32), approximate=True
    ).astype(jnp.bfloat16)
    return middle + jnp.dot(hidden, w_down, preferred_element_type=jnp.float32)


def window_layer(ct_rows, pet_rows, params):
    norm_ct, norm_pet, norm_ffn, w_query, w_key, w_value, w_out, w_up, w_down = params
    head_count = ct_rows.shape[-1] // DH
    normed_ct = rms_scale(ct_rows, norm_ct)
    normed_pet = rms_scale(pet_rows, norm_pet)
    mixed_ct = attend(
        project(normed_ct, w_query),
        project(normed_pet, w_key),
        project(normed_pet, w_value),
        head_count,
    )
    mixed_pet = attend(
        project(normed_pet, w_query),
        project(normed_ct, w_key),
        project(normed_ct, w_value),
        head_count,
    )
    mid_ct = ct_rows.astype(jnp.float32) + jnp.dot(
        mixed_ct, w_out, preferred_element_type=jnp.float32
    )
    mid_pet = pet_rows.astype(jnp.float32) + jnp.dot(
        mixed_pet, w_out, preferred_element_type=jnp.float32
    )
    return feed_forward(mid_ct, norm_ffn, w_up, w_down) + feed_forward(
        mid_pet, norm_ffn, w_up, w_down
    )


def on_device(
    ct_win,
    pet_win,
    placed_anchor,
    placed_count,
    norm_ct,
    norm_pet,
    norm_ffn,
    w_query,
    w_key,
    w_value,
    w_out,
    w_up,
    w_down,
    w_upconv,
    w_conv,
):
    slot_total, token_total, model_width = ct_win.shape
    window_depth = WDEP
    plane_cells = token_total // window_depth
    channels = w_conv.shape[1]
    brick_total = lax.axis_size("brick")
    position = lax.axis_index("brick")
    params = (norm_ct, norm_pet, norm_ffn, w_query, w_key, w_value, w_out, w_up, w_down)
    anchor_local = lax.dynamic_slice_in_dim(placed_anchor, position * slot_total, slot_total)
    count_local = lax.dynamic_slice_in_dim(placed_count, position * slot_total, slot_total)
    joined = window_layer(ct_win, pet_win, params)
    offsets = jnp.arange(window_depth, dtype=jnp.float32) - (window_depth - 1) / 2.0
    spread_width = window_depth / 4.0
    bell_curve = jnp.exp(-offsets * offsets / (2.0 * spread_width * spread_width))
    factor = count_local.astype(jnp.float32) / (2.0 * token_total)
    flat_terms = (
        joined.reshape(slot_total, window_depth, plane_cells * model_width)
        * (factor[:, None] * bell_curve[None, :])[:, :, None]
    ).reshape(slot_total * window_depth, plane_cells * model_width)
    target = (anchor_local[:, None] + jnp.arange(window_depth, dtype=jnp.int32)[None, :]).reshape(
        slot_total * window_depth
    )
    row_ids = jnp.arange(brick_total, dtype=jnp.int32)
    one_hot = (row_ids[:, None] == target[None, :]).astype(jnp.float32)
    pieces = lax.all_to_all(
        jnp.dot(
            one_hot, flat_terms, precision=lax.Precision.HIGHEST, preferred_element_type=jnp.float32
        ).astype(jnp.bfloat16),
        "brick",
        split_axis=0,
        concat_axis=0,
        tiled=True,
    )
    numerator = jnp.sum(pieces.astype(jnp.float32), axis=0)
    inside = (position >= placed_anchor) & (position < placed_anchor + window_depth)
    shifted = (position - placed_anchor).astype(jnp.float32) - (window_depth - 1) / 2.0
    all_factor = placed_count.astype(jnp.float32) / (2.0 * token_total)
    denominator = jnp.sum(
        jnp.where(
            inside,
            all_factor * jnp.exp(-shifted * shifted / (2.0 * spread_width * spread_width)),
            0.0,
        )
    )
    feature = (
        (numerator / jnp.maximum(denominator, 1.0))
        .astype(jnp.bfloat16)
        .reshape(plane_cells, model_width)
    )
    up_rows = jnp.dot(feature, w_upconv, preferred_element_type=jnp.float32)
    up_rows = up_rows.reshape(PY, PX, 2, 2, 2, channels).transpose(2, 0, 3, 1, 4, 5)
    upsampled = up_rows.reshape(2, 2 * PY, 2 * PX, channels).astype(jnp.bfloat16)
    active = jnp.maximum(upsampled, jnp.zeros((), jnp.bfloat16))
    padded = with_halo(active, (("brick", 0),), 1)
    padded = jnp.pad(padded, ((0, 0), (1, 1), (1, 1), (0, 0)))
    patches = jnp.concatenate(
        [
            padded[shift_z : shift_z + 2, shift_y : shift_y + 2 * PY, shift_x : shift_x + 2 * PX, :]
            for shift_z in range(3)
            for shift_y in range(3)
            for shift_x in range(3)
        ],
        axis=-1,
    )
    conv_out = jnp.dot(
        patches.reshape(2 * 2 * PY * 2 * PX, 27 * channels),
        w_conv,
        preferred_element_type=jnp.float32,
    )
    conv_out = conv_out.reshape(2, 2 * PY, 2 * PX, channels)
    return (upsampled.astype(jnp.float32) + conv_out).astype(jnp.bfloat16)


def solution(mesh):
    return jax.shard_map(
        on_device,
        mesh=mesh,
        in_specs=(
            P(("groups", "brick"), None, None),
            P(("groups", "brick"), None, None),
            P("groups"),
            P("groups"),
            P(),
            P(),
            P(),
            P(),
            P(),
            P(),
            P(),
            P(),
            P(),
            P(),
            P(),
        ),
        out_specs=P(("groups", "brick"), None, None, None),
        check_vma=False,
    )
```

profile of v0, /device:TPU:16, one launch (start us, length us, event | category | flops | bytes accessed | tf_op | source)
XLA Modules:
  0.0 95.1 jit_solution(1412790497110214119)
XLA Ops:
  3.1 2.7 %convolution_convert_fusion.6 = bf16[2,128,768]{2,1,0:T(8,128)(2,1)} fusion(bf16[768,768]{1,0:T(8,128)(2,1)} %param.23, bf16[2,128,768]{2,1,0:T(8,128)(2,1)} %param.16, f32[768]{0:T(1024)} %param.20, f32[2,128]{1,0:T(2,128)S(1)} %add_rsqrt_fusion.3), kind=kOutput, calls=%fused_computation.49 | convolution fusion | flops 302972928 | bytes 1970176 | tf_op jit(solution)/shard_map/dot_general | solution.py:39
  12.4 1.9 %copy.44 = bf16[2,128,768]{1,2,0:T(8,128)(2,1)} copy(bf16[2,128,768]{2,1,0:T(8,128)(2,1)} %convolution_convert_fusion.6) | data formatting | bytes 786432 | tf_op jit(solution)/shard_map/convert_element_type | solution.py:39
  14.3 1.9 %copy.48 = bf16[2,128,768]{1,2,0:T(8,128)(2,1)} copy(bf16[2,128,768]{2,1,0:T(8,128)(2,1)} %convolution_convert_fusion.3) | data formatting | bytes 786432 | tf_op jit(solution)/shard_map/convert_element_type | solution.py:39
  16.2 1.9 %copy.42 = bf16[2,128,768]{1,2,0:T(8,128)(2,1)} copy(bf16[2,128,768]{2,1,0:T(8,128)(2,1)} %convolution_convert_fusion.8) | data formatting | bytes 786432 | tf_op jit(solution)/shard_map/convert_element_type | solution.py:39
  20.2 3.5 %fusion.122 = (f32[2,12,128]{2,1,0:T(8,128)}, f32[2,12,128,128]{2,3,1,0:T(8,128)}) fusion(bf16[2,128,12,64]{1,3,2,0:T(8,128)(2,1)S(1)} %bitcast.114, bf16[2,128,12,64]{1,3,2,0:T(8,128)(2,1)} %bitcast.112), kind=kOutput, calls=%fused_computation.168 | convolution fusion | flops 51511424 | bytes 2371584 | tf_op jit(solution)/shard_map/sub | solution.py:53
  23.7 1.9 %convolution_convert_fusion.5 = bf16[2,12,64,128]{3,2,1,0:T(8,128)(2,1)S(1)} fusion(bf16[2,128,12,64]{1,3,2,0:T(8,128)(2,1)} %bitcast.113, f32[2,12,128,128]{2,3,1,0:T(8,128)} %get-tuple-element.14, f32[2,12,128]{2,1,0:T(8,128)} %get-tuple-element.13), kind=kOutput, calls=%fused_computation.48 | convolution fusion | flops 51314688 | bytes 2371584 | tf_op jit(solution)/shard_map/shwv,svhd->swhd/dot_general | solution.py:55
  25.7 1.4 %multiply_reduce_fusion.1 = (f32[2,128]{1,0:T(2,128)S(1)}, f32[2,128,768]{2,1,0:T(8,128)}) fusion(bf16[2,128,768]{1,2,0:T(8,128)(2,1)S(1)} %bitcast.107, bf16[768,768]{1,0:T(8,128)(2,1)S(1)} %copy-done.1, bf16[2,128,768]{2,1,0:T(8,128)(2,1)S(1)} %copy-done.3), kind=kOutput, calls=%fused_computation.86 | convolution fusion | flops 302776064 | bytes 2753536 | tf_op jit(solution)/shard_map/dot_general | solution.py:86
  27.1 3.6 %fusion.121 = (f32[2,12,128]{2,1,0:T(8,128)}, f32[2,12,128,128]{2,3,1,0:T(8,128)}) fusion(bf16[2,128,12,64]{1,3,2,0:T(8,128)(2,1)} %bitcast.109, bf16[2,128,12,64]{1,3,2,0:T(8,128)(2,1)} %bitcast.111), kind=kOutput, calls=%fused_computation.167 | convolution fusion | flops 51511424 | bytes 2371584 | tf_op jit(solution)/shard_map/sub | solution.py:53
  30.6 1.9 %convolution_convert_fusion.1 = bf16[2,12,64,128]{3,2,1,0:T(8,128)(2,1)S(1)} fusion(bf16[2,128,12,64]{1,3,2,0:T(8,128)(2,1)} %bitcast.110, f32[2,12,128,128]{2,3,1,0:T(8,128)} %get-tuple-element.10, f32[2,12,128]{2,1,0:T(8,128)} %get-tuple-element.9), kind=kOutput, calls=%fused_computation.44 | convolution fusion | flops 51314688 | bytes 2371584 | tf_op jit(solution)/shard_map/shwv,svhd->swhd/dot_general | solution.py:55
  32.5 1.4 %multiply_reduce_fusion = (f32[2,128]{1,0:T(2,128)S(1)}, f32[2,128,768]{2,1,0:T(8,128)}) fusion(bf16[2,128,768]{1,2,0:T(8,128)(2,1)S(1)} %bitcast.108, bf16[768,768]{1,0:T(8,128)(2,1)S(1)} %copy-done.1, bf16[2,128,768]{2,1,0:T(8,128)(2,1)S(1)} %copy-done.5), kind=kOutput, calls=%fused_computation.76 | convolution fusion | flops 302776064 | bytes 2753536 | tf_op jit(solution)/shard_map/dot_general | solution.py:89
  33.9 4.7 %fusion.45 = f32[2,128,768]{2,1,0:T(8,128)} fusion(f32[2,128,768]{2,1,0:T(8,128)} %get-tuple-element.12, bf16[1536,768]{1,0:T(8,128)(2,1)S(1)} %copy-done, bf16[768,1536]{1,0:T(8,128)(2,1)} %param.26, f32[2,128]{1,0:T(2,128)S(1)} %add_rsqrt_fusion, f32[768]{0:T(1024)} %param.21), kind=kOutput, calls=%fused_computation.41 | convolution fusion | flops 1212284928 | bytes 6295552 | tf_op jit(solution)/shard_map/dot_general | solution.py:66
  38.6 4.3 %fusion.42 = f32[2,128,768]{2,1,0:T(8,128)} fusion(f32[2,128,768]{2,1,0:T(8,128)} %fusion.45, f32[2,128,768]{2,1,0:T(8,128)S(1)} %copy-done.7, bf16[1536,768]{1,0:T(8,128)(2,1)S(1)} %copy-done, bf16[768,1536]{1,0:T(8,128)(2,1)} %param.26, f32[768]{0:T(1024)S(1)} %copy-done.15, f32[2,128]{1,0:T(2,128)S(1)} %add_rsqrt_fusion.1), kind=kOutput, calls=%fused_computation.40 | convolution fusion | flops 1212481536 | bytes 7081984 | tf_op jit(solution)/shard_map/dot_general | solution.py:66
  44.3 1.7 %fusion.2 = bf16[16,1,24576]{2,0,1:T(8,128)(2,1)} fusion(f32[8,24576]{1,0:T(8,128)S(1)} %reshape.149, f32[8]{0:T(128)S(1)} %mul.178, s32[8]{0:T(128)S(1)} %add.104), kind=kOutput, calls=%fused_computation.3 | convolution fusion | flops 38338688 | bytes 1572928 | tf_op jit(solution)/shard_map/dot_general | solution.py:138
  46.5 2.4 %reduce.1 = bf16[16,24576]{1,0:T(8,128)(2,1)S(1)} reduce(bf16[16,1,24576]{2,0,1:T(8,128)(2,1)} %fusion.2, bf16[]{:T(256)} %broadcast.228), dimensions={1}, to_apply=%copy.52.reduce_sub_computation | reduce | bytes 1572866 | tf_op jit(solution)/shard_map/all_to_all | solution.py:137
  48.9 1.5 %reshape.161 = bf16[16,2,12288]{2,1,0:T(2,128)(2,1)} reshape(bf16[16,24576]{1,0:T(8,128)(2,1)S(1)} %reduce.1) | data formatting | bytes 1572864
  50.3 6.2 %all-to-all-start = ((bf16[16,2,12288]{2,1,0:T(2,128)(2,1)}), bf16[16,2,12288]{2,1,0:T(2,128)(2,1)S(1)}, u32[]{:S(2)}, u32[]{:S(2)}) async-start(bf16[16,2,12288]{2,1,0:T(2,128)(2,1)} %reshape.161), calls=%async_computation | async-start | bytes 1572864 | tf_op jit(solution)/shard_map/all_to_all | solution.py:137
  56.5 2.6 %copy.64 = bf16[1024,768]{1,0:T(8,128)(2,1)} copy(bf16[1024,768]{0,1:T(8,128)(2,1)} %bitcast.104) | data formatting | bytes 3145728 | tf_op jit(solution)/shard_map/dot_general | solution.py:162
  60.4 15.7 %all-to-all-done = bf16[16,2,12288]{2,1,0:T(2,128)(2,1)S(1)} async-done(((bf16[16,2,12288]{2,1,0:T(2,128)(2,1)}), bf16[16,2,12288]{2,1,0:T(2,128)(2,1)S(1)}, u32[]{:S(2)}, u32[]{:S(2)}) %all-to-all-start) | async-done | bytes 786464 | tf_op jit(solution)/shard_map/all_to_all | solution.py:137
  76.1 2.1 %reshape.162 = bf16[16,1,24576]{2,1,0:T(2,128)(2,1)} reshape(bf16[16,2,12288]{2,1,0:T(2,128)(2,1)S(1)} %all-to-all-done) | data formatting | bytes 1572864
  78.1 3.3 %convert_reduce_fusion = f32[24576]{0:T(1024)S(1)} fusion(bf16[16,1,24576]{2,1,0:T(2,128)(2,1)} %reshape.162), kind=kLoop, calls=%fused_computation.32 | loop fusion | flops 761856 | bytes 884736 | tf_op jit(solution)/shard_map/reduce_sum | solution.py:146
  81.6 2.0 %maximum_bitcast_fusion = (bf16[2,4,2,8,2,128]{5,3,4,2,0,1:T(8,128)(2,1)S(1)}, f32[2,4,2,8,2,128]{5,3,4,2,0,1:T(8,128)S(1)}) fusion(bf16[2,2,2,128,768,1]{4,3,2,1,0,5:T(8,128)(2,1)} %bitcast.105, bf16[4,8,768,1,1,1]{2,1,0,3,4,5:T(8,128)(2,1)S(1)} %reshape.157), kind=kOutput, calls=%fused_computation.134 | convolution fusion | flops 50429952 | bytes 1818624 | tf_op jit(solution)/shard_map/dot_general | solution.py:162
  83.6 2.8 %collective-permute-start.1 = (bf16[1,8,16,128]{3,2,1,0:T(8,128)(2,1)S(1)}, bf16[1,8,16,128]{3,2,1,0:T(8,128)(2,1)S(1)}, u32[]{:S(2)}, u32[]{:S(2)}) collective-permute-start(bf16[1,8,16,128]{3,2,1,0:T(8,128)(2,1)S(1)} %bitcast.116), channel_id=1, source_target_pairs={{1,0},{2,1},{3,2},{4,3},{5,4},{6,5},{7,6},{8,7},{9,8},{10,9},{11,1... | collective-permute-start | bytes 98312 | tf_op jit(solution)/shard_map/ppermute | solution.py:25
  86.4 1.9 %collective-permute-start = (bf16[1,8,16,128]{3,2,1,0:T(8,128)(2,1)S(1)}, bf16[1,8,16,128]{3,2,1,0:T(8,128)(2,1)S(1)}, u32[]{:S(2)}, u32[]{:S(2)}) collective-permute-start(bf16[1,8,16,128]{3,2,1,0:T(8,128)(2,1)S(1)} %bitcast.115), channel_id=1, source_target_pairs={{0,1},{1,2},{2,3},{3,4},{4,5},{5,6},{6,7},{7,8},{8,9},{9,10},{10,1... | collective-permute-start | bytes 98312 | tf_op jit(solution)/shard_map/ppermute | solution.py:23
  88.5 4.1 %collective-permute-done = bf16[1,8,16,128]{3,2,1,0:T(8,128)(2,1)S(1)} collective-permute-done((bf16[1,8,16,128]{3,2,1,0:T(8,128)(2,1)S(1)}, bf16[1,8,16,128]{3,2,1,0:T(8,128)(2,1)S(1)}, u32[]{:S(2)}, u32[]{:S(2)}) %collective-permute-start) | collective-permute-done | bytes 32800 | tf_op jit(solution)/shard_map/ppermute | solution.py:23
  (100 shorter events, 16.8 us)
Async XLA Ops:
  0.0 33.9 %copy-start = (bf16[1536,768]{1,0:T(8,128)(2,1)S(1)}, bf16[1536,768]{1,0:T(8,128)(2,1)}, u32[]{:S(2)}) copy-start(bf16[1536,768]{1,0:T(8,128)(2,1)} %param.27) | copy-start | bytes 7077892
  0.0 5.8 %copy-start.4 = (bf16[2,128,768]{2,1,0:T(8,128)(2,1)S(1)}, bf16[2,128,768]{2,1,0:T(8,128)(2,1)}, u32[]{:S(2)}) copy-start(bf16[2,128,768]{2,1,0:T(8,128)(2,1)} %param.16) | copy-start | bytes 1179652
  0.0 5.8 %copy-start.13 = (f32[768]{0:T(1024)S(1)}, f32[768]{0:T(1024)}, u32[]{:S(2)}) copy-start(f32[768]{0:T(1024)} %param.20) | copy-start | bytes 9220
  0.0 5.8 %copy-start.10 = (bf16[768,768]{1,0:T(8,128)(2,1)S(1)}, bf16[768,768]{1,0:T(8,128)(2,1)}, u32[]{:S(2)}) copy-start(bf16[768,768]{1,0:T(8,128)(2,1)} %param.24) | copy-start | bytes 3538948
  3.0 4.0 %copy-start.2 = (bf16[2,128,768]{2,1,0:T(8,128)(2,1)S(1)}, bf16[2,128,768]{2,1,0:T(8,128)(2,1)}, u32[]{:S(2)}) copy-start(bf16[2,128,768]{2,1,0:T(8,128)(2,1)} %param.15) | copy-start | bytes 1179652
  3.0 4.0 %copy-start.14 = (f32[768]{0:T(1024)S(1)}, f32[768]{0:T(1024)}, u32[]{:S(2)}) copy-start(f32[768]{0:T(1024)} %param.19) | copy-start | bytes 9220
  5.8 1.8 %copy-start.11 = (bf16[768,768]{1,0:T(8,128)(2,1)S(1)}, bf16[768,768]{1,0:T(8,128)(2,1)}, u32[]{:S(2)}) copy-start(bf16[768,768]{1,0:T(8,128)(2,1)} %param.23) | copy-start | bytes 3538948
  7.1 1.3 %copy-start.12 = (bf16[768,768]{1,0:T(8,128)(2,1)S(1)}, bf16[768,768]{1,0:T(8,128)(2,1)}, u32[]{:S(2)}) copy-start(bf16[768,768]{1,0:T(8,128)(2,1)} %param.22) | copy-start | bytes 3538948
  8.4 1.9 %copy-start.9 = (s32[32]{0:T(128)S(1)}, s32[32]{0:T(128)}, u32[]{:S(2)}) copy-start(s32[32]{0:T(128)} %param.17) | copy-start | bytes 388
  8.4 1.9 %copy-start.8 = (s32[32]{0:T(128)S(1)}, s32[32]{0:T(128)}, u32[]{:S(2)}) copy-start(s32[32]{0:T(128)} %param.18) | copy-start | bytes 388
  23.7 1.9 %copy-start.1 = (bf16[768,768]{1,0:T(8,128)(2,1)S(1)}, bf16[768,768]{1,0:T(8,128)(2,1)}, u32[]{:S(2)}) copy-start(bf16[768,768]{1,0:T(8,128)(2,1)} %param.25) | copy-start | bytes 3538948
  23.7 2.0 %copy-start.3 = (bf16[2,128,768]{2,1,0:T(8,128)(2,1)S(1)}, bf16[2,128,768]{2,1,0:T(8,128)(2,1)}, u32[]{:S(2)}) copy-start(bf16[2,128,768]{2,1,0:T(8,128)(2,1)} %param.15) | copy-start | bytes 1179652
  30.6 1.9 %copy-start.5 = (bf16[2,128,768]{2,1,0:T(8,128)(2,1)S(1)}, bf16[2,128,768]{2,1,0:T(8,128)(2,1)}, u32[]{:S(2)}) copy-start(bf16[2,128,768]{2,1,0:T(8,128)(2,1)} %param.16) | copy-start | bytes 1179652
  33.9 4.7 %copy-start.7 = (f32[2,128,768]{2,1,0:T(8,128)S(1)}, f32[2,128,768]{2,1,0:T(8,128)}, u32[]{:S(2)}) copy-start(f32[2,128,768]{2,1,0:T(8,128)} %get-tuple-element.16) | copy-start | bytes 2359300
  33.9 4.7 %copy-start.15 = (f32[768]{0:T(1024)S(1)}, f32[768]{0:T(1024)}, u32[]{:S(2)}) copy-start(f32[768]{0:T(1024)} %param.21) | copy-start | bytes 9220
  38.6 5.6 %copy-start.16 = (f32[8]{0:T(128)S(1)}, f32[8]{0:T(128)}, u32[]{:S(2)}) copy-start(f32[8]{0:T(128)} %mul.174) | copy-start | bytes 100
  38.6 5.6 %copy-start.17 = (f32[8]{0:T(128)S(1)}, f32[8]{0:T(128)}, u32[]{:S(2)}) copy-start(f32[8]{0:T(128)} %mul.177) | copy-start | bytes 100
  50.3 25.7 %all-to-all-start = ((bf16[16,2,12288]{2,1,0:T(2,128)(2,1)}), bf16[16,2,12288]{2,1,0:T(2,128)(2,1)S(1)}, u32[]{:S(2)}, u32[]{:S(2)}) async-start(bf16[16,2,12288]{2,1,0:T(2,128)(2,1)} %reshape.161), calls=%async_computation | async-start | bytes 1572864 | tf_op jit(solution)/shard_map/all_to_all | solution.py:137
  83.6 4.9 %collective-permute-start.1 = (bf16[1,8,16,128]{3,2,1,0:T(8,128)(2,1)S(1)}, bf16[1,8,16,128]{3,2,1,0:T(8,128)(2,1)S(1)}, u32[]{:S(2)}, u32[]{:S(2)}) collective-permute-start(bf16[1,8,16,128]{3,2,1,0:T(8,128)(2,1)S(1)} %bitcast.116), channel_id=1, source_target_pairs={{1,0},{2,1},{3,2},{4,3},{5,4},{6,5},{7,6},{8,7},{9,8},{10,9},{11,1... | collective-permute-start | bytes 98312 | tf_op jit(solution)/shard_map/ppermute | solution.py:25
  86.4 6.1 %collective-permute-start = (bf16[1,8,16,128]{3,2,1,0:T(8,128)(2,1)S(1)}, bf16[1,8,16,128]{3,2,1,0:T(8,128)(2,1)S(1)}, u32[]{:S(2)}, u32[]{:S(2)}) collective-permute-start(bf16[1,8,16,128]{3,2,1,0:T(8,128)(2,1)S(1)} %bitcast.115), channel_id=1, source_target_pairs={{0,1},{1,2},{2,3},{3,4},{4,5},{5,6},{6,7},{7,8},{8,9},{9,10},{10,1... | collective-permute-start | bytes 98312 | tf_op jit(solution)/shard_map/ppermute | solution.py:23
  92.7 1.2 %copy-start.6 = (bf16[3456,128]{1,0:T(8,128)(2,1)S(1)}, bf16[3456,128]{1,0:T(8,128)(2,1)}, u32[]{:S(2)}) copy-start(bf16[3456,128]{1,0:T(8,128)(2,1)} %param.29) | copy-start | bytes 2654212
where the time goes:
time: 95.9 us; the launch traced here: 95.1 us
  matrix products  34.4 us (36%)
  waiting for transfers between devices  19.7 us (21%)
  local copies, waits for them, and re-layouts  19.3 us (20%)
  starting transfers between devices  10.9 us (11%)
  other arithmetic  9.62 us (10%)
  between operations  1.06 us (1%)
    all_to_all x1, waiting for transfers between devices, on_device(): lax.all_to_all(jnp.dot(one_hot, flat_terms, precision=lax.Precision.HIGHE...  15.7 us
    dot_general x2, matrix products, feed_forward(): return middle + jnp.dot(hidden, w_down, preferred_element_type=jnp.float32)  9 us
    convert_element_type x6, local copies, waits for them, and re-layouts, project(): jnp.dot(normed, weight, preferred_element_type=jnp.float32)  7.81 us
    sub x2, matrix products, attend(): exp_scores = jnp.exp(scores - row_max)  7.01 us
    dot_general x6, matrix products, project(): jnp.dot(normed, weight, preferred_element_type=jnp.float32)  6.89 us
    all_to_all x1, starting transfers between devices, on_device(): lax.all_to_all(jnp.dot(one_hot, flat_terms, precision=lax.Precision.HIGHE...  6.16 us
    unnamed x62, local copies, waits for them, and re-layouts  4.81 us
    ppermute x1, waiting for transfers between devices, with_halo(): lax.ppermute(tail, axis, [(i, (i + 1) % count) for i in range(ends)])  4.06 us
  transfers between devices with their start and end apart: 3, of which 2 were waited for; matrix products, arithmetic and copies ran while one was open for 4% of the time, Pallas kernels for 0%

commit v1 on v0

v1 whole, which is shorter than its diff:
```python
import functools
import math

import jax
import jax.numpy as jnp
from jax import lax
from jax.experimental import pallas as pl
from jax.experimental.pallas import tpu as pltpu
from jax.sharding import PartitionSpec as P

DH = 64
PY = 4
PX = 8
WDEP = 4
LANES = 128

epsilon = 1e-06

VMEM = pl.BlockSpec(memory_space=pltpu.VMEM)
SMEM = pl.BlockSpec(memory_space=pltpu.SMEM)
ANY = pl.BlockSpec(memory_space=pl.ANY)

BELL = [
    math.exp(-((i - (WDEP - 1) / 2.0) ** 2) / (2.0 * (WDEP / 4.0) ** 2)) for i in range(WDEP)
]


def rms_scale(inputs, gain_vec):
    mean_square = jnp.mean(inputs * inputs, axis=-1, keepdims=True)
    return (inputs * lax.rsqrt(mean_square + epsilon) * gain_vec).astype(jnp.bfloat16)


def dot(left, right):
    return jnp.dot(left, right, preferred_element_type=jnp.float32)


def bell_at(depth):
    value = jnp.float32(BELL[0])
    for i in range(1, WDEP):
        value = jnp.where(depth == i, jnp.float32(BELL[i]), value)
    return value


def window_kernel(
    anchor_ref,
    count_ref,
    place_ref,
    gain_ct,
    gain_pet,
    gain_ffn,
    ct_hbm,
    pet_hbm,
    wq_hbm,
    wk_hbm,
    wv_hbm,
    wo_hbm,
    wu_hbm,
    wd_hbm,
    *rest,
):
    outs = rest[:WDEP]
    tok, wq, wk, wv, wo, wu, wd, normed, q_all, k_all, v_all, mixed, sems = rest[WDEP:]
    slots, tokens, width = ct_hbm.shape
    rows = slots * tokens
    cells = tokens // WDEP
    sources = [
        (ct_hbm, tok.at[0]),
        (pet_hbm, tok.at[1]),
        (wq_hbm, wq),
        (wk_hbm, wk),
        (wv_hbm, wv),
        (wo_hbm, wo),
        (wu_hbm, wu),
        (wd_hbm, wd),
    ]
    copies = [pltpu.make_async_copy(src, dst, sems.at[i]) for i, (src, dst) in enumerate(sources)]
    for copy in copies:
        copy.start()
    position = place_ref[0]
    residue = lax.rem(position, WDEP)

    gains = (gain_ct, gain_pet)
    for m in range(2):
        copies[m].wait()
        for s in range(slots):
            start = m * rows + s * tokens
            normed[start : start + tokens, :] = rms_scale(
                tok[m, s].astype(jnp.float32), gains[m][...]
            )
    for i, (weight, result) in enumerate(((wq, q_all), (wk, k_all), (wv, v_all))):
        copies[2 + i].wait()
        result[...] = dot(normed[...], weight[...]).astype(jnp.bfloat16)

    low = lax.broadcasted_iota(jnp.int32, (tokens, LANES), 1) < DH
    zero = jnp.zeros((tokens, LANES), jnp.bfloat16)
    one = jnp.ones((tokens, LANES), jnp.bfloat16)
    ones_two = jnp.concatenate([jnp.where(low, one, zero), jnp.where(low, zero, one)], axis=0)
    for s in range(slots):
        for m in range(2):
            mine = m * rows + s * tokens
            other = (1 - m) * rows + s * tokens
            for pair in range(width // LANES):
                lanes = slice(pair * LANES, (pair + 1) * LANES)
                queries = q_all[mine : mine + tokens, lanes]
                keys = k_all[other : other + tokens, lanes]
                values = v_all[other : other + tokens, lanes]
                keys_two = jnp.concatenate(
                    [jnp.where(low, keys, zero), jnp.where(low, zero, keys)], axis=0
                )
                values_two = jnp.concatenate(
                    [jnp.where(low, values, zero), jnp.where(low, zero, values)], axis=0
                )
                scores = lax.dot_general(
                    queries,
                    keys_two,
                    (((1,), (1,)), ((), ())),
                    preferred_element_type=jnp.float32,
                )
                powers = []
                for h in range(2):
                    part = scores[:, h * tokens : (h + 1) * tokens]
                    top = jnp.max(part, axis=-1, keepdims=True)
                    powers.append(jnp.exp((part - top) * (1.0 / DH**0.5)).astype(jnp.bfloat16))
                powers = jnp.concatenate(powers, axis=1)
                both = dot(powers, jnp.concatenate([values_two, ones_two], axis=1))
                mixed[mine : mine + tokens, lanes] = (both[:, :LANES] / both[:, LANES:]).astype(
                    jnp.bfloat16
                )

    copies[5].wait()
    for phase in range(2):
        rels = (2, 3) if phase == 0 else (1, 0)
        picks = []
        for rel in rels:
            for s in range(slots):
                slot = lax.div(position, 1) * slots + s
                depth = lax.rem((residue ^ rel) + WDEP * NWRAP - anchor_ref[slot], WDEP)
                picks.append((rel, s, slot, depth))
        base = []
        picked = []
        for m in range(2):
            for rel, s, slot, depth in picks:
                offset = pl.multiple_of(depth * cells, cells)
                base.append(tok[m, s, pl.ds(offset, cells), :])
                place = pl.multiple_of(m * rows + s * tokens + depth * cells, cells)
                picked.append(mixed[pl.ds(place, cells), :])
        mid = jnp.concatenate(base, axis=0).astype(jnp.float32) + dot(
            jnp.concatenate(picked, axis=0), wo[...]
        )
        normed_mid = rms_scale(mid, gain_ffn[...])
        if phase == 0:
            copies[6].wait()
        hidden = jax.nn.gelu(dot(normed_mid, wu[...]), approximate=True)
        half = hidden.shape[0] // 2
        hidden_sum = (hidden[:half] + hidden[half:]).astype(jnp.bfloat16)
        if phase == 0:
            copies[7].wait()
        joined = mid[:half] + mid[half:] + dot(hidden_sum, wd[...])
        for j, (rel, s, slot, depth) in enumerate(picks):
            factor = jnp.full((1, width), count_ref[slot], jnp.int32).astype(jnp.float32) * (
                1.0 / (2.0 * tokens)
            )
            outs[rel][s] = (
                joined[j * cells : (j + 1) * cells] * (factor * bell_at(depth))
            ).astype(jnp.bfloat16)


NWRAP = 1 << 20


def window_call(position, anchor, count, gains, ct_win, pet_win, weights):
    slots, tokens, width = ct_win.shape
    rows = 2 * slots * tokens
    cells = tokens // WDEP
    out = jax.ShapeDtypeStruct((slots, cells, width), jnp.bfloat16)
    token_buffer = pltpu.VMEM((2, slots, tokens, width), jnp.bfloat16)
    big = pltpu.VMEM((rows, width), jnp.bfloat16)
    return pl.pallas_call(
        window_kernel,
        out_shape=[out] * WDEP,
        in_specs=[SMEM, SMEM, SMEM, VMEM, VMEM, VMEM] + [ANY] * 8,
        out_specs=[VMEM] * WDEP,
        scratch_shapes=[token_buffer]
        + [pltpu.VMEM(w.shape, w.dtype) for w in weights]
        + [big] * 5
        + [pltpu.SemaphoreType.DMA((8,))],
        compiler_params=pltpu.CompilerParams(vmem_limit_bytes=48 * 1024 * 1024),
        name="window_layer",
    )(anchor, count, position, *gains, ct_win, pet_win, *weights)


def gather_kernel(outer, anchor_ref, place_ref, *refs):
    sources = refs[:WDEP]
    kept, sent, total = refs[WDEP], refs[WDEP + 1 : -1], refs[-1]
    slots = sources[0].shape[0]
    position = place_ref[0]
    residue = lax.rem(position, WDEP)
    block = lax.div(position, WDEP)
    total[...] = jnp.zeros_like(total)
    for rel in range(WDEP):
        for s in range(slots):
            slot = (block * WDEP + (residue ^ rel)) * slots + s
            start = anchor_ref[slot]
            depth = lax.rem(residue + WDEP * NWRAP - start, WDEP)
            target = lax.div(start + depth, WDEP)
            step = target ^ block
            total[step] += sources[rel][s].astype(jnp.float32)
    kept[...] = total[0]
    for k in range(1, outer):
        sent[k - 1][...] = total[k].astype(jnp.bfloat16)


def gather_call(outer, position, anchor, blocks):
    slots, cells, width = blocks[0].shape
    return pl.pallas_call(
        functools.partial(gather_kernel, outer),
        out_shape=[jax.ShapeDtypeStruct((cells, width), jnp.float32)]
        + [jax.ShapeDtypeStruct((cells, width), jnp.bfloat16)] * (outer - 1),
        in_specs=[SMEM, SMEM] + [VMEM] * WDEP,
        out_specs=[VMEM] * outer,
        scratch_shapes=[pltpu.VMEM((outer, cells, width), jnp.float32)],
        name="plane_sum",
    )(anchor, position, *blocks)


def upconv_kernel(tokens, place_ref, anchor_ref, count_ref, kept, *refs):
    pieces = refs[:-5]
    weight, up_ref, first_ref, second_ref, grid = refs[-5:]
    channels = up_ref.shape[-1]
    position = place_ref[0]
    shift = position - anchor_ref[...]
    inside = (shift >= 0) & (shift < WDEP)
    centred = shift.astype(jnp.float32) - (WDEP - 1) / 2.0
    spread = WDEP / 4.0
    terms = (
        count_ref[...].astype(jnp.float32)
        / (2.0 * tokens)
        * jnp.exp(-centred * centred / (2.0 * spread * spread))
    )
    total = jnp.sum(jnp.where(inside, terms, 0.0), axis=-1, keepdims=True)
    numerator = kept[...]
    for piece in pieces:
        numerator = numerator + piece[...].astype(jnp.float32)
    feature = (numerator / jnp.maximum(total, 1.0)).astype(jnp.bfloat16)
    up_rows = dot(feature, weight[...])
    for a in range(2):
        for b in range(2):
            for c in range(2):
                chunk = (a * 2 + b) * 2 + c
                for y in range(PY):
                    grid[a, 2 * y + b, pl.ds(c, PX, stride=2), :] = up_rows[
                        y * PX : (y + 1) * PX, chunk * channels : (chunk + 1) * channels
                    ]
    upsampled = grid[...].astype(jnp.bfloat16)
    up_ref[...] = upsampled
    even = lax.rem(position, 2) == 0
    active = jnp.maximum(upsampled, jnp.zeros((), jnp.bfloat16))
    first_ref[...] = jnp.where(even, active[1], active[0])
    second_ref[...] = jnp.where(even, active[0], active[1])


def upconv_call(tokens, channels, position, anchor, count, kept, pieces, weight):
    layer = (2 * PY, 2 * PX, channels)
    return pl.pallas_call(
        functools.partial(upconv_kernel, tokens),
        out_shape=[
            jax.ShapeDtypeStruct((2,) + layer, jnp.bfloat16),
            jax.ShapeDtypeStruct(layer, jnp.bfloat16),
            jax.ShapeDtypeStruct(layer, jnp.bfloat16),
        ],
        in_specs=[SMEM] + [VMEM] * (4 + len(pieces)),
        out_specs=[VMEM] * 3,
        scratch_shapes=[pltpu.VMEM((2,) + layer, jnp.float32)],
        name="upconv",
    )(position, anchor[None, :], count[None, :], kept, *pieces, weight)


def conv_kernel(place_ref, up_ref, first_ref, second_ref, weight, out_ref, padded, patches):
    depth, height, breadth, channels = up_ref.shape
    even = lax.rem(place_ref[0], 2) == 0
    padded[...] = jnp.zeros_like(padded)
    for z in range(depth + 2):
        if z == 0:
            layer = jnp.where(even, second_ref[...], first_ref[...])
        elif z == depth + 1:
            layer = jnp.where(even, first_ref[...], second_ref[...])
        else:
            layer = jnp.maximum(up_ref[z - 1], jnp.zeros((), jnp.bfloat16))
        padded[z, 1 : height + 1, 8 : 8 + breadth, :] = layer.astype(jnp.float32)
    rows = height * breadth
    for z in range(depth + 2):
        for dx in range(3):
            column = padded[z, :, 7 + dx : 7 + dx + breadth, :].astype(jnp.bfloat16)
            for dy in range(3):
                tap = dy * 3 + dx
                patches[z * rows : (z + 1) * rows, tap * channels : (tap + 1) * channels] = column[
                    dy : dy + height
                ].reshape(rows, channels)
    span = 9 * channels
    total = up_ref[...].reshape(depth * rows, channels).astype(jnp.float32)
    for dz in range(3):
        total = total + dot(
            patches[dz * rows : (dz + depth) * rows, :], weight[dz * span : (dz + 1) * span, :]
        )
    out_ref[...] = total.astype(jnp.bfloat16).reshape(out_ref.shape)


def conv_call(position, upsampled, first, second, weight):
    depth, height, breadth, channels = upsampled.shape
    return pl.pallas_call(
        conv_kernel,
        out_shape=jax.ShapeDtypeStruct(upsampled.shape, jnp.bfloat16),
        in_specs=[SMEM, VMEM, VMEM, VMEM, VMEM],
        out_specs=VMEM,
        scratch_shapes=[
            pltpu.VMEM((depth + 2, height + 2, breadth + 16, channels), jnp.float32),
            pltpu.VMEM(((depth + 2) * height * breadth, 9 * channels), jnp.bfloat16),
        ],
        name="conv",
    )(position, upsampled, first, second, weight)


def swap(values, distance, total):
    return lax.ppermute(values, "brick", [(i, i ^ distance) for i in range(total)])


def on_device(
    ct_win,
    pet_win,
    placed_anchor,
    placed_count,
    norm_ct,
    norm_pet,
    norm_ffn,
    w_query,
    w_key,
    w_value,
    w_out,
    w_up,
    w_down,
    w_upconv,
    w_conv,
):
    tokens = ct_win.shape[1]
    channels = w_conv.shape[1]
    total = lax.axis_size("brick")
    outer = total // WDEP
    position = lax.axis_index("brick").reshape(1)
    blocks = window_call(
        position,
        placed_anchor,
        placed_count,
        (norm_ct[None, :], norm_pet[None, :], norm_ffn[None, :]),
        ct_win,
        pet_win,
        (w_query, w_key, w_value, w_out, w_up, w_down),
    )
    arrived = {rel: swap(blocks[rel], rel, total) for rel in (2, 3, 1)}
    sums = gather_call(
        outer, position, placed_anchor, [blocks[0]] + [arrived[rel] for rel in range(1, WDEP)]
    )
    pieces = [swap(sums[k], k * WDEP, total) for k in range(1, outer)]
    upsampled, first, second = upconv_call(
        tokens, channels, position, placed_anchor, placed_count, sums[0], pieces, w_upconv
    )
    pairs = [(i, i + 1) for i in range(1, total - 1, 2)]
    near = swap(first, 1, total)
    far = lax.ppermute(second, "brick", pairs + [(j, i) for i, j in pairs])
    return conv_call(position, upsampled, near, far, w_conv)


def solution(mesh):
    return jax.shard_map(
        on_device,
        mesh=mesh,
        in_specs=(
            P(("groups", "brick"), None, None),
            P(("groups", "brick"), None, None),
            P("groups"),
            P("groups"),
            P(),
            P(),
            P(),
            P(),
            P(),
            P(),
            P(),
            P(),
            P(),
            P(),
            P(),
        ),
        out_specs=P(("groups", "brick"), None, None, None),
        check_vma=False,
    )
```

time: 95.9 us -> 55.6 us (0.58)
  the two profiles are of different devices: /device:TPU:16 before, /device:TPU:3 now
where the time goes in v1:
time: 55.6 us; the launch traced here: 55.1 us
  Pallas kernels  17.9 us (32%)
  waiting for transfers between devices  14.4 us (26%)
  local copies, waits for them, and re-layouts  12.9 us (23%)
  starting transfers between devices  9.79 us (18%)
    unnamed x34, local copies, waits for them, and re-layouts  10.9 us
    pallas_call x1, Pallas kernels, window_call(): pl.pallas_call(window_kernel, out_shape=[out] * WDEP, in_specs=[SMEM, SME...  10.8 us
    ppermute x7, waiting for transfers between devices, swap(): lax.ppermute(values, 'brick', [(i, i ^ distance) for i in range(total)])  9.96 us
    ppermute x7, starting transfers between devices, swap(): lax.ppermute(values, 'brick', [(i, i ^ distance) for i in range(total)])  7.89 us
    ppermute x1, waiting for transfers between devices, on_device(): far = lax.ppermute(second, 'brick', pairs + [(j, i) for i, j in pairs])  4.39 us
    pallas_call x1, Pallas kernels, upconv_call(): pl.pallas_call(functools.partial(upconv_kernel, tokens), out_shape=[jax.S...  2.69 us
    pallas_call x1, Pallas kernels, conv_call(): pl.pallas_call(conv_kernel, out_shape=jax.ShapeDtypeStruct(upsampled.shap...  2.56 us
    ppermute x1, starting transfers between devices, on_device(): far = lax.ppermute(second, 'brick', pairs + [(j, i) for i, j in pairs])  1.91 us
  transfers between devices with their start and end apart: 8, of which 5 were waited for; matrix products, arithmetic and copies ran while one was open for 0% of the time, Pallas kernels for 0%

profile of v1, /device:TPU:3, one launch (start us, length us, event | category | flops | bytes accessed | tf_op | source)
XLA Modules:
  0.0 55.1 jit_solution(13246925090851344156)
XLA Ops:
  0.0 0.7 %broadcast_in_dim.17.gain_ct = f32[1,768]{1,0:T(1,128)S(1)} reshape(f32[768]{0:T(1024)} %param.19) | data formatting | bytes 6144 | tf_op jit(solution)/shard_map/broadcast_in_dim | solution.py:353
  0.7 0.7 %broadcast_in_dim.18.gain_pet = f32[1,768]{1,0:T(1,128)S(1)} reshape(f32[768]{0:T(1024)} %param.20) | data formatting | bytes 6144 | tf_op jit(solution)/shard_map/broadcast_in_dim | solution.py:353
  1.4 0.7 %broadcast_in_dim.19.gain_ffn = f32[1,768]{1,0:T(1,128)S(1)} reshape(f32[768]{0:T(1024)} %param.21) | data formatting | bytes 6144 | tf_op jit(solution)/shard_map/broadcast_in_dim | solution.py:353
  2.1 1.3 %copy-done = bf16[768,768]{1,0:T(8,128)(2,1)S(1)} copy-done((bf16[768,768]{1,0:T(8,128)(2,1)S(1)}, bf16[768,768]{1,0:T(8,128)(2,1)}, u32[]{:S(2)}) %copy-start) | copy-done | bytes 1179672
  3.3 1.3 %copy-done.1 = bf16[768,768]{1,0:T(8,128)(2,1)S(1)} copy-done((bf16[768,768]{1,0:T(8,128)(2,1)S(1)}, bf16[768,768]{1,0:T(8,128)(2,1)}, u32[]{:S(2)}) %copy-start.1) | copy-done | bytes 1179672
  4.6 1.3 %copy-done.2 = bf16[768,768]{1,0:T(8,128)(2,1)S(1)} copy-done((bf16[768,768]{1,0:T(8,128)(2,1)S(1)}, bf16[768,768]{1,0:T(8,128)(2,1)}, u32[]{:S(2)}) %copy-start.2) | copy-done | bytes 1179672
  5.9 1.3 %copy-done.3 = bf16[768,768]{1,0:T(8,128)(2,1)S(1)} copy-done((bf16[768,768]{1,0:T(8,128)(2,1)S(1)}, bf16[768,768]{1,0:T(8,128)(2,1)}, u32[]{:S(2)}) %copy-start.3) | copy-done | bytes 1179672
  7.2 1.0 %copy-done.4 = bf16[2,128,768]{2,1,0:T(8,128)(2,1)S(1)} copy-done((bf16[2,128,768]{2,1,0:T(8,128)(2,1)S(1)}, bf16[2,128,768]{2,1,0:T(8,128)(2,1)}, u32[]{:S(2)}) %copy-start.4) | copy-done | bytes 393240
  8.2 1.0 %copy-done.5 = bf16[2,128,768]{2,1,0:T(8,128)(2,1)S(1)} copy-done((bf16[2,128,768]{2,1,0:T(8,128)(2,1)S(1)}, bf16[2,128,768]{2,1,0:T(8,128)(2,1)}, u32[]{:S(2)}) %copy-start.5) | copy-done | bytes 393240
  10.5 10.8 %window_layer.1 = (bf16[2,32,768]{2,1,0:T(8,128)(2,1)S(1)}, bf16[2,32,768]{2,1,0:T(8,128)(2,1)S(1)}, bf16[2,32,768]{2,1,0:T(8,128)(2,1)S(1)}, bf16[2,32,768]{2,1,0:T(8,128)(2,1)S(1)}) custom-call(s32[32]{0:T(128)S(1)} %copy-done.7, s32[32]{0:T(128)S(1)} %copy-done.8, s32[1]{0:T(128)} %bitcast.place_ref, f32[1,768]{1,0:T(1,128)S(1)} %broadcast_in_dim.17.gain_ct, ...), custom_call_target="tpu_custom_call" | custom-call | tf_op jit(solution)/shard_map/window_layer/pallas_call | solution.py:178
  21.9 0.7 %collective-permute-start = (bf16[2,32,768]{2,1,0:T(8,128)(2,1)S(1)}, bf16[2,32,768]{2,1,0:T(8,128)(2,1)S(1)}, u32[]{:S(2)}, u32[]{:S(2)}) collective-permute-start(bf16[2,32,768]{2,1,0:T(8,128)(2,1)S(1)} %get-tuple-element.17), channel_id=1, source_target_pairs={{0,1},{1,0},{2,3},{3,2},{4,5},{5,4},{6,7},{7,6},{8,9},{9,8},{10,11... | collective-permute-start | bytes 294920 | tf_op jit(solution)/shard_map/ppermute | solution.py:324
  22.6 1.6 %collective-permute-start.2 = (bf16[2,32,768]{2,1,0:T(8,128)(2,1)S(1)}, bf16[2,32,768]{2,1,0:T(8,128)(2,1)S(1)}, u32[]{:S(2)}, u32[]{:S(2)}) collective-permute-start(bf16[2,32,768]{2,1,0:T(8,128)(2,1)S(1)} %get-tuple-element.19), channel_id=1, source_target_pairs={{0,3},{1,2},{2,1},{3,0},{4,7},{5,6},{6,5},{7,4},{8,11},{9,10},{10,... | collective-permute-start | bytes 294920 | tf_op jit(solution)/shard_map/ppermute | solution.py:324
  24.2 2.8 %collective-permute-done.1.refs_2_ = bf16[2,32,768]{2,1,0:T(8,128)(2,1)S(1)} collective-permute-done((bf16[2,32,768]{2,1,0:T(8,128)(2,1)S(1)}, bf16[2,32,768]{2,1,0:T(8,128)(2,1)S(1)}, u32[]{:S(2)}, u32[]{:S(2)}) %collective-permute-start.1) | collective-permute-done | bytes 98336 | tf_op jit(solution)/shard_map/ppermute | solution.py:324
  27.0 2.2 %collective-permute-done.2.refs_3_ = bf16[2,32,768]{2,1,0:T(8,128)(2,1)S(1)} collective-permute-done((bf16[2,32,768]{2,1,0:T(8,128)(2,1)S(1)}, bf16[2,32,768]{2,1,0:T(8,128)(2,1)S(1)}, u32[]{:S(2)}, u32[]{:S(2)}) %collective-permute-start.2) | collective-permute-done | bytes 98336 | tf_op jit(solution)/shard_map/ppermute | solution.py:324
  29.9 1.8 %plane_sum.1 = (f32[32,768]{1,0:T(8,128)}, bf16[32,768]{1,0:T(8,128)(2,1)}, bf16[32,768]{1,0:T(8,128)(2,1)}, bf16[32,768]{1,0:T(8,128)(2,1)}) custom-call(s32[32]{0:T(128)} %anchor_ref.3, s32[1]{0:T(128)} %bitcast.place_ref, bf16[2,32,768]{2,1,0:T(8,128)(2,1)} %copy-done.6, bf16[2,32,768]{2,1,0:T(8,128)(2,1)} %copy-done.9, bf16[2,32,768]{2,1,0:T(8,128)(2,1)} %copy-done.10, ...), custom_call_target="tpu_custom_call" | custom-call | tf_op jit(solution)/shard_map/plane_sum/pallas_call | solution.py:215
  31.7 1.3 %collective-permute-start.3 = (bf16[32,768]{1,0:T(8,128)(2,1)}, bf16[32,768]{1,0:T(8,128)(2,1)S(1)}, u32[]{:S(2)}, u32[]{:S(2)}) collective-permute-start(bf16[32,768]{1,0:T(8,128)(2,1)} %get-tuple-element.21), channel_id=1, source_target_pairs={{0,4},{1,5},{2,6},{3,7},{4,0},{5,1},{6,2},{7,3},{8,12},{9,13},{10,... | collective-permute-start | bytes 147464 | tf_op jit(solution)/shard_map/ppermute | solution.py:324
  33.0 2.3 %collective-permute-start.4 = (bf16[32,768]{1,0:T(8,128)(2,1)}, bf16[32,768]{1,0:T(8,128)(2,1)S(1)}, u32[]{:S(2)}, u32[]{:S(2)}) collective-permute-start(bf16[32,768]{1,0:T(8,128)(2,1)} %get-tuple-element.22), channel_id=1, source_target_pairs={{0,8},{1,9},{2,10},{3,11},{4,12},{5,13},{6,14},{7,15},{8,0},{9,1},... | collective-permute-start | bytes 147464 | tf_op jit(solution)/shard_map/ppermute | solution.py:324
  35.3 2.1 %collective-permute-done.4.refs_1_ = bf16[32,768]{1,0:T(8,128)(2,1)S(1)} collective-permute-done((bf16[32,768]{1,0:T(8,128)(2,1)}, bf16[32,768]{1,0:T(8,128)(2,1)S(1)}, u32[]{:S(2)}, u32[]{:S(2)}) %collective-permute-start.4) | collective-permute-done | bytes 49184 | tf_op jit(solution)/shard_map/ppermute | solution.py:324
  37.4 2.9 %collective-permute-done.5.refs_2_ = bf16[32,768]{1,0:T(8,128)(2,1)S(1)} collective-permute-done((bf16[32,768]{1,0:T(8,128)(2,1)}, bf16[32,768]{1,0:T(8,128)(2,1)S(1)}, u32[]{:S(2)}, u32[]{:S(2)}) %collective-permute-start.5) | collective-permute-done | bytes 49184 | tf_op jit(solution)/shard_map/ppermute | solution.py:324
  40.9 2.7 %upconv.1 = (bf16[2,8,16,128]{3,2,1,0:T(8,128)(2,1)}, bf16[8,16,128]{2,1,0:T(8,128)(2,1)}, bf16[8,16,128]{2,1,0:T(8,128)(2,1)}) custom-call(s32[1]{0:T(128)} %bitcast.place_ref, s32[1,32]{1,0:T(1,128)} %bitcast.3, s32[1,32]{1,0:T(1,128)} %bitcast.4, f32[32,768]{1,0:T(8,128)} %get-tuple-element.20.kept, bf16[32,768]{1,0:T(8,128)(2,1)} %copy-done.12, ...), custom_call_target="tpu_custom_call" | custom-call | tf_op jit(solution)/shard_map/upconv/pallas_call | solution.py:264
  43.6 2.0 %collective-permute-start.6 = (bf16[8,16,128]{2,1,0:T(8,128)(2,1)}, bf16[8,16,128]{2,1,0:T(8,128)(2,1)S(1)}, u32[]{:S(2)}, u32[]{:S(2)}) collective-permute-start(bf16[8,16,128]{2,1,0:T(8,128)(2,1)} %get-tuple-element.25), channel_id=1, source_target_pairs={{0,1},{1,0},{2,3},{3,2},{4,5},{5,4},{6,7},{7,6},{8,9},{9,8},{10,11... | collective-permute-start | bytes 98312 | tf_op jit(solution)/shard_map/ppermute | solution.py:324
  45.6 1.9 %collective-permute-start.7 = (bf16[8,16,128]{2,1,0:T(8,128)(2,1)}, bf16[8,16,128]{2,1,0:T(8,128)(2,1)S(1)}, u32[]{:S(2)}, u32[]{:S(2)}) collective-permute-start(bf16[8,16,128]{2,1,0:T(8,128)(2,1)} %get-tuple-element.26), channel_id=1, source_target_pairs={{1,2},{3,4},{5,6},{7,8},{9,10},{11,12},{13,14},{2,1},{4,3},{6,5},{... | collective-permute-start | bytes 98312 | tf_op jit(solution)/shard_map/ppermute | solution.py:368
  47.5 4.4 %collective-permute-done.7.second_ref = bf16[8,16,128]{2,1,0:T(8,128)(2,1)S(1)} collective-permute-done((bf16[8,16,128]{2,1,0:T(8,128)(2,1)}, bf16[8,16,128]{2,1,0:T(8,128)(2,1)S(1)}, u32[]{:S(2)}, u32[]{:S(2)}) %collective-permute-start.7) | collective-permute-done | bytes 32800 | tf_op jit(solution)/shard_map/ppermute | solution.py:368
  52.5 2.6 %conv.1 = bf16[2,8,16,128]{3,2,1,0:T(8,128)(2,1)} custom-call(s32[1]{0:T(128)} %bitcast.place_ref, bf16[2,8,16,128]{3,2,1,0:T(8,128)(2,1)} %get-tuple-element.24.up_ref, bf16[8,16,128]{2,1,0:T(8,128)(2,1)} %copy-done.15, bf16[8,16,128]{2,1,0:T(8,128)(2,1)} %copy-done.16, bf16[3456,128]{1,0:T(8,128)(2,1)} %weight.1), custom_call_target="tpu_custom_call" | custom-call | tf_op jit(solution)/shard_map/conv/pallas_call | solution.py:310
  (33 shorter events, 3.8 us)
Async XLA Ops:
  2.1 1.3 %copy-start = (bf16[768,768]{1,0:T(8,128)(2,1)S(1)}, bf16[768,768]{1,0:T(8,128)(2,1)}, u32[]{:S(2)}) copy-start(bf16[768,768]{1,0:T(8,128)(2,1)} %wq_hbm.1) | copy-start | bytes 3538948
  3.3 1.3 %copy-start.1 = (bf16[768,768]{1,0:T(8,128)(2,1)S(1)}, bf16[768,768]{1,0:T(8,128)(2,1)}, u32[]{:S(2)}) copy-start(bf16[768,768]{1,0:T(8,128)(2,1)} %wk_hbm.1) | copy-start | bytes 3538948
  4.6 1.3 %copy-start.2 = (bf16[768,768]{1,0:T(8,128)(2,1)S(1)}, bf16[768,768]{1,0:T(8,128)(2,1)}, u32[]{:S(2)}) copy-start(bf16[768,768]{1,0:T(8,128)(2,1)} %wv_hbm.1) | copy-start | bytes 3538948
  5.9 1.3 %copy-start.3 = (bf16[768,768]{1,0:T(8,128)(2,1)S(1)}, bf16[768,768]{1,0:T(8,128)(2,1)}, u32[]{:S(2)}) copy-start(bf16[768,768]{1,0:T(8,128)(2,1)} %wo_hbm.1) | copy-start | bytes 3538948
  7.2 1.0 %copy-start.4 = (bf16[2,128,768]{2,1,0:T(8,128)(2,1)S(1)}, bf16[2,128,768]{2,1,0:T(8,128)(2,1)}, u32[]{:S(2)}) copy-start(bf16[2,128,768]{2,1,0:T(8,128)(2,1)} %ct_hbm.1) | copy-start | bytes 1179652
  8.1 1.0 %copy-start.5 = (bf16[2,128,768]{2,1,0:T(8,128)(2,1)S(1)}, bf16[2,128,768]{2,1,0:T(8,128)(2,1)}, u32[]{:S(2)}) copy-start(bf16[2,128,768]{2,1,0:T(8,128)(2,1)} %pet_hbm.1) | copy-start | bytes 1179652
  9.1 0.7 %copy-start.7 = (s32[32]{0:T(128)S(1)}, s32[32]{0:T(128)}, u32[]{:S(2)}) copy-start(s32[32]{0:T(128)} %anchor_ref.3) | copy-start | bytes 388
  9.8 0.7 %copy-start.8 = (s32[32]{0:T(128)S(1)}, s32[32]{0:T(128)}, u32[]{:S(2)}) copy-start(s32[32]{0:T(128)} %count_ref.1) | copy-start | bytes 388
  21.3 0.6 %copy-start.6 = (bf16[2,32,768]{2,1,0:T(8,128)(2,1)}, bf16[2,32,768]{2,1,0:T(8,128)(2,1)S(1)}, u32[]{:S(2)}) copy-start(bf16[2,32,768]{2,1,0:T(8,128)(2,1)S(1)} %get-tuple-element.16.refs_0_) | copy-start | bytes 294916
  21.9 2.3 %collective-permute-start = (bf16[2,32,768]{2,1,0:T(8,128)(2,1)S(1)}, bf16[2,32,768]{2,1,0:T(8,128)(2,1)S(1)}, u32[]{:S(2)}, u32[]{:S(2)}) collective-permute-start(bf16[2,32,768]{2,1,0:T(8,128)(2,1)S(1)} %get-tuple-element.17), channel_id=1, source_target_pairs={{0,1},{1,0},{2,3},{3,2},{4,5},{5,4},{6,7},{7,6},{8,9},{9,8},{10,11... | collective-permute-start | bytes 294920 | tf_op jit(solution)/shard_map/ppermute | solution.py:324
  22.6 4.4 %collective-permute-start.1 = (bf16[2,32,768]{2,1,0:T(8,128)(2,1)S(1)}, bf16[2,32,768]{2,1,0:T(8,128)(2,1)S(1)}, u32[]{:S(2)}, u32[]{:S(2)}) collective-permute-start(bf16[2,32,768]{2,1,0:T(8,128)(2,1)S(1)} %get-tuple-element.18), channel_id=1, source_target_pairs={{0,2},{1,3},{2,0},{3,1},{4,6},{5,7},{6,4},{7,5},{8,10},{9,11},{10,... | collective-permute-start | bytes 294920 | tf_op jit(solution)/shard_map/ppermute | solution.py:324
  22.6 6.6 %collective-permute-start.2 = (bf16[2,32,768]{2,1,0:T(8,128)(2,1)S(1)}, bf16[2,32,768]{2,1,0:T(8,128)(2,1)S(1)}, u32[]{:S(2)}, u32[]{:S(2)}) collective-permute-start(bf16[2,32,768]{2,1,0:T(8,128)(2,1)S(1)} %get-tuple-element.19), channel_id=1, source_target_pairs={{0,3},{1,2},{2,1},{3,0},{4,7},{5,6},{6,5},{7,4},{8,11},{9,10},{10,... | collective-permute-start | bytes 294920 | tf_op jit(solution)/shard_map/ppermute | solution.py:324
  24.2 5.0 %copy-start.9 = (bf16[2,32,768]{2,1,0:T(8,128)(2,1)}, bf16[2,32,768]{2,1,0:T(8,128)(2,1)S(1)}, u32[]{:S(2)}) copy-start(bf16[2,32,768]{2,1,0:T(8,128)(2,1)S(1)} %collective-permute-done.refs_1_) | copy-start | bytes 294916
  27.0 2.2 %copy-start.10 = (bf16[2,32,768]{2,1,0:T(8,128)(2,1)}, bf16[2,32,768]{2,1,0:T(8,128)(2,1)S(1)}, u32[]{:S(2)}) copy-start(bf16[2,32,768]{2,1,0:T(8,128)(2,1)S(1)} %collective-permute-done.1.refs_2_) | copy-start | bytes 294916
  29.2 0.6 %copy-start.11 = (bf16[2,32,768]{2,1,0:T(8,128)(2,1)}, bf16[2,32,768]{2,1,0:T(8,128)(2,1)S(1)}, u32[]{:S(2)}) copy-start(bf16[2,32,768]{2,1,0:T(8,128)(2,1)S(1)} %collective-permute-done.2.refs_3_) | copy-start | bytes 294916
  31.7 3.6 %collective-permute-start.3 = (bf16[32,768]{1,0:T(8,128)(2,1)}, bf16[32,768]{1,0:T(8,128)(2,1)S(1)}, u32[]{:S(2)}, u32[]{:S(2)}) collective-permute-start(bf16[32,768]{1,0:T(8,128)(2,1)} %get-tuple-element.21), channel_id=1, source_target_pairs={{0,4},{1,5},{2,6},{3,7},{4,0},{5,1},{6,2},{7,3},{8,12},{9,13},{10,... | collective-permute-start | bytes 147464 | tf_op jit(solution)/shard_map/ppermute | solution.py:324
  33.0 4.4 %collective-permute-start.4 = (bf16[32,768]{1,0:T(8,128)(2,1)}, bf16[32,768]{1,0:T(8,128)(2,1)S(1)}, u32[]{:S(2)}, u32[]{:S(2)}) collective-permute-start(bf16[32,768]{1,0:T(8,128)(2,1)} %get-tuple-element.22), channel_id=1, source_target_pairs={{0,8},{1,9},{2,10},{3,11},{4,12},{5,13},{6,14},{7,15},{8,0},{9,1},... | collective-permute-start | bytes 147464 | tf_op jit(solution)/shard_map/ppermute | solution.py:324
  35.3 5.0 %collective-permute-start.5 = (bf16[32,768]{1,0:T(8,128)(2,1)}, bf16[32,768]{1,0:T(8,128)(2,1)S(1)}, u32[]{:S(2)}, u32[]{:S(2)}) collective-permute-start(bf16[32,768]{1,0:T(8,128)(2,1)} %get-tuple-element.23), channel_id=1, source_target_pairs={{0,12},{1,13},{2,14},{3,15},{4,8},{5,9},{6,10},{7,11},{8,4},{9,5},... | collective-permute-start | bytes 147464 | tf_op jit(solution)/shard_map/ppermute | solution.py:324
  35.3 5.0 %copy-start.12 = (bf16[32,768]{1,0:T(8,128)(2,1)}, bf16[32,768]{1,0:T(8,128)(2,1)S(1)}, u32[]{:S(2)}) copy-start(bf16[32,768]{1,0:T(8,128)(2,1)S(1)} %collective-permute-done.3.refs_0_) | copy-start | bytes 147460
  37.4 2.9 %copy-start.13 = (bf16[32,768]{1,0:T(8,128)(2,1)}, bf16[32,768]{1,0:T(8,128)(2,1)S(1)}, u32[]{:S(2)}) copy-start(bf16[32,768]{1,0:T(8,128)(2,1)S(1)} %collective-permute-done.4.refs_1_) | copy-start | bytes 147460
  40.3 0.6 %copy-start.14 = (bf16[32,768]{1,0:T(8,128)(2,1)}, bf16[32,768]{1,0:T(8,128)(2,1)S(1)}, u32[]{:S(2)}) copy-start(bf16[32,768]{1,0:T(8,128)(2,1)S(1)} %collective-permute-done.5.refs_2_) | copy-start | bytes 147460
  43.6 3.9 %collective-permute-start.6 = (bf16[8,16,128]{2,1,0:T(8,128)(2,1)}, bf16[8,16,128]{2,1,0:T(8,128)(2,1)S(1)}, u32[]{:S(2)}, u32[]{:S(2)}) collective-permute-start(bf16[8,16,128]{2,1,0:T(8,128)(2,1)} %get-tuple-element.25), channel_id=1, source_target_pairs={{0,1},{1,0},{2,3},{3,2},{4,5},{5,4},{6,7},{7,6},{8,9},{9,8},{10,11... | collective-permute-start | bytes 98312 | tf_op jit(solution)/shard_map/ppermute | solution.py:324
  45.6 6.3 %collective-permute-start.7 = (bf16[8,16,128]{2,1,0:T(8,128)(2,1)}, bf16[8,16,128]{2,1,0:T(8,128)(2,1)S(1)}, u32[]{:S(2)}, u32[]{:S(2)}) collective-permute-start(bf16[8,16,128]{2,1,0:T(8,128)(2,1)} %get-tuple-element.26), channel_id=1, source_target_pairs={{1,2},{3,4},{5,6},{7,8},{9,10},{11,12},{13,14},{2,1},{4,3},{6,5},{... | collective-permute-start | bytes 98312 | tf_op jit(solution)/shard_map/ppermute | solution.py:368
  47.5 4.4 %copy-start.15 = (bf16[8,16,128]{2,1,0:T(8,128)(2,1)}, bf16[8,16,128]{2,1,0:T(8,128)(2,1)S(1)}, u32[]{:S(2)}) copy-start(bf16[8,16,128]{2,1,0:T(8,128)(2,1)S(1)} %collective-permute-done.6.first_ref) | copy-start | bytes 98308
  (1 other events, 0.6 us)

commit v2 on v1

--- a/solution.py
+++ b/solution.py
@@ -45,9 +45,9 @@
     anchor_ref,
     count_ref,
     place_ref,
-    gain_ct,
-    gain_pet,
-    gain_ffn,
+    gain_ct_hbm,
+    gain_pet_hbm,
+    gain_ffn_hbm,
     ct_hbm,
     pet_hbm,
     wq_hbm,
@@ -59,7 +59,8 @@
     *rest,
 ):
     outs = rest[:WDEP]
-    tok, wq, wk, wv, wo, wu, wd, normed, q_all, k_all, v_all, mixed, sems = rest[WDEP:]
+    gains = rest[WDEP : WDEP + 3]
+    tok, wq, wk, wv, wo, wu, wd, normed, q_all, k_all, v_all, mixed, sems = rest[WDEP + 3 :]
     slots, tokens, width = ct_hbm.shape
     rows = slots * tokens
     cells = tokens // WDEP
@@ -72,20 +73,24 @@
         (wo_hbm, wo),
         (wu_hbm, wu),
         (wd_hbm, wd),
+        (gain_ct_hbm, gains[0]),
+        (gain_pet_hbm, gains[1]),
+        (gain_ffn_hbm, gains[2]),
     ]
     copies = [pltpu.make_async_copy(src, dst, sems.at[i]) for i, (src, dst) in enumerate(sources)]
-    for copy in copies:
-        copy.start()
+    for i in (8, 9, 10, 0, 1, 2, 3, 4, 5, 6, 7):
+        copies[i].start()
     position = place_ref[0]
     residue = lax.rem(position, WDEP)
 
-    gains = (gain_ct, gain_pet)
+    for i in (8, 9, 10):
+        copies[i].wait()
     for m in range(2):
         copies[m].wait()
         for s in range(slots):
             start = m * rows + s * tokens
             normed[start : start + tokens, :] = rms_scale(
-                tok[m, s].astype(jnp.float32), gains[m][...]
+                tok[m, s].astype(jnp.float32), gains[m][...][None, :]
             )
     for i, (weight, result) in enumerate(((wq, q_all), (wk, k_all), (wv, v_all))):
         copies[2 + i].wait()
@@ -147,7 +152,7 @@
         mid = jnp.concatenate(base, axis=0).astype(jnp.float32) + dot(
             jnp.concatenate(picked, axis=0), wo[...]
         )
-        normed_mid = rms_scale(mid, gain_ffn[...])
+        normed_mid = rms_scale(mid, gains[2][...][None, :])
         if phase == 0:
             copies[6].wait()
         hidden = jax.nn.gelu(dot(normed_mid, wu[...]), approximate=True)
@@ -168,25 +173,37 @@
 NWRAP = 1 << 20
 
 
+def in_hbm(array):
+    return pltpu.with_memory_space_constraint(array, pltpu.HBM)
+
+
+def in_vmem(array):
+    return pltpu.with_memory_space_constraint(array, pltpu.VMEM)
+
+
+SMALL = pltpu.CompilerParams(vmem_limit_bytes=12 * 1024 * 1024)
+
+
 def window_call(position, anchor, count, gains, ct_win, pet_win, weights):
     slots, tokens, width = ct_win.shape
     rows = 2 * slots * tokens
     cells = tokens // WDEP
-    out = jax.ShapeDtypeStruct((slots, cells, width), jnp.bfloat16)
+    out = pltpu.VMEM((slots, cells, width), jnp.bfloat16)
     token_buffer = pltpu.VMEM((2, slots, tokens, width), jnp.bfloat16)
     big = pltpu.VMEM((rows, width), jnp.bfloat16)
     return pl.pallas_call(
         window_kernel,
         out_shape=[out] * WDEP,
-        in_specs=[SMEM, SMEM, SMEM, VMEM, VMEM, VMEM] + [ANY] * 8,
+        in_specs=[SMEM, SMEM, SMEM] + [ANY] * 11,
         out_specs=[VMEM] * WDEP,
-        scratch_shapes=[token_buffer]
+        scratch_shapes=[pltpu.VMEM((width,), jnp.float32)] * 3
+        + [token_buffer]
         + [pltpu.VMEM(w.shape, w.dtype) for w in weights]
         + [big] * 5
-        + [pltpu.SemaphoreType.DMA((8,))],
-        compiler_params=pltpu.CompilerParams(vmem_limit_bytes=48 * 1024 * 1024),
+        + [pltpu.SemaphoreType.DMA((11,))],
+        compiler_params=pltpu.CompilerParams(vmem_limit_bytes=40 * 1024 * 1024),
         name="window_layer",
-    )(anchor, count, position, *gains, ct_win, pet_win, *weights)
+    )(in_hbm(anchor), in_hbm(count), position, *map(in_hbm, (*gains, ct_win, pet_win, *weights)))
 
 
 def gather_kernel(outer, anchor_ref, place_ref, *refs):
@@ -214,13 +231,14 @@
     slots, cells, width = blocks[0].shape
     return pl.pallas_call(
         functools.partial(gather_kernel, outer),
-        out_shape=[jax.ShapeDtypeStruct((cells, width), jnp.float32)]
-        + [jax.ShapeDtypeStruct((cells, width), jnp.bfloat16)] * (outer - 1),
+        out_shape=[pltpu.VMEM((cells, width), jnp.float32)]
+        + [pltpu.VMEM((cells, width), jnp.bfloat16)] * (outer - 1),
         in_specs=[SMEM, SMEM] + [VMEM] * WDEP,
         out_specs=[VMEM] * outer,
         scratch_shapes=[pltpu.VMEM((outer, cells, width), jnp.float32)],
+        compiler_params=SMALL,
         name="plane_sum",
-    )(anchor, position, *blocks)
+    )(in_hbm(anchor), position, *map(in_vmem, blocks))
 
 
 def upconv_kernel(tokens, place_ref, anchor_ref, count_ref, kept, *refs):
@@ -264,15 +282,16 @@
     return pl.pallas_call(
         functools.partial(upconv_kernel, tokens),
         out_shape=[
-            jax.ShapeDtypeStruct((2,) + layer, jnp.bfloat16),
-            jax.ShapeDtypeStruct(layer, jnp.bfloat16),
-            jax.ShapeDtypeStruct(layer, jnp.bfloat16),
+            pltpu.VMEM((2,) + layer, jnp.bfloat16),
+            pltpu.VMEM(layer, jnp.bfloat16),
+            pltpu.VMEM(layer, jnp.bfloat16),
         ],
         in_specs=[SMEM] + [VMEM] * (4 + len(pieces)),
         out_specs=[VMEM] * 3,
         scratch_shapes=[pltpu.VMEM((2,) + layer, jnp.float32)],
+        compiler_params=SMALL,
         name="upconv",
-    )(position, anchor[None, :], count[None, :], kept, *pieces, weight)
+    )(position, in_hbm(anchor[None, :]), in_hbm(count[None, :]), *map(in_vmem, (kept, *pieces, weight)))
 
 
 def conv_kernel(place_ref, up_ref, first_ref, second_ref, weight, out_ref, padded, patches):
@@ -316,8 +335,9 @@
             pltpu.VMEM((depth + 2, height + 2, breadth + 16, channels), jnp.float32),
             pltpu.VMEM(((depth + 2) * height * breadth, 9 * channels), jnp.bfloat16),
         ],
+        compiler_params=SMALL,
         name="conv",
-    )(position, upsampled, first, second, weight)
+    )(position, *map(in_vmem, (upsampled, first, second, weight)))
 
 
 def swap(values, distance, total):
@@ -350,7 +370,7 @@
         position,
         placed_anchor,
         placed_count,
-        (norm_ct[None, :], norm_pet[None, :], norm_ffn[None, :]),
+        (norm_ct, norm_pet, norm_ffn),
         ct_win,
         pet_win,
         (w_query, w_key, w_value, w_out, w_up, w_down),

time: 55.6 us -> 38.4 us (0.69)
  the two profiles are of different devices: /device:TPU:3 before, /device:TPU:7 now
where the time goes in v2:
time: 38.4 us; the launch traced here: 38.2 us
  Pallas kernels  14.3 us (37%)
  waiting for transfers between devices  13.9 us (36%)
  starting transfers between devices  10 us (26%)
    pallas_call x1, Pallas kernels, window_call(): pl.pallas_call(window_kernel, out_shape=[out] * WDEP, in_specs=[SMEM, SME...  11 us
    ppermute x7, waiting for transfers between devices, swap(): lax.ppermute(values, 'brick', [(i, i ^ distance) for i in range(total)])  9.69 us
    ppermute x7, starting transfers between devices, swap(): lax.ppermute(values, 'brick', [(i, i ^ distance) for i in range(total)])  8.12 us
    ppermute x1, waiting for transfers between devices, on_device(): far = lax.ppermute(second, 'brick', pairs + [(j, i) for i, j in pairs])  4.19 us
    ppermute x1, starting transfers between devices, on_device(): far = lax.ppermute(second, 'brick', pairs + [(j, i) for i, j in pairs])  1.91 us
    pallas_call x1, Pallas kernels, conv_call(): pl.pallas_call(conv_kernel, out_shape=jax.ShapeDtypeStruct(upsampled.shap...  1.33 us
    pallas_call x1, Pallas kernels, upconv_call(): pl.pallas_call(functools.partial(upconv_kernel, tokens), out_shape=[pltpu...  1.13 us
    pallas_call x1, Pallas kernels, gather_call(): pl.pallas_call(functools.partial(gather_kernel, outer), out_shape=[pltpu....  0.79 us
  transfers between devices with their start and end apart: 8, of which 5 were waited for; matrix products, arithmetic and copies ran while one was open for 0% of the time, Pallas kernels for 0%

profile of v2, /device:TPU:7, one launch (start us, length us, event | category | flops | bytes accessed | tf_op | source)
XLA Modules:
  0.0 38.2 jit_solution(12598167327066517944)
XLA Ops:
  0.0 0.0 copy-start
  0.0 11.0 %window_layer.1 = (bf16[2,32,768]{2,1,0:T(8,128)(2,1)S(1)}, bf16[2,32,768]{2,1,0:T(8,128)(2,1)S(1)}, bf16[2,32,768]{2,1,0:T(8,128)(2,1)S(1)}, bf16[2,32,768]{2,1,0:T(8,128)(2,1)S(1)}) custom-call(s32[32]{0:T(128)} %anchor_ref.3, s32[32]{0:T(128)} %count_ref.1, s32[1]{0:T(128)} %bitcast.place_ref, f32[768]{0:T(1024)} %gain_ct_hbm.1, f32[768]{0:T(1024)} %gain_pet_hbm.1, ...), custom_call_target="tpu_custom_call" | custom-call | tf_op jit(solution)/shard_map/window_layer/pallas_call | solution.py:194
  11.0 0.0 copy-start.1
  11.0 0.8 %collective-permute-start = (bf16[2,32,768]{2,1,0:T(8,128)(2,1)S(1)}, bf16[2,32,768]{2,1,0:T(8,128)(2,1)S(1)}, u32[]{:S(2)}, u32[]{:S(2)}) collective-permute-start(bf16[2,32,768]{2,1,0:T(8,128)(2,1)S(1)} %get-tuple-element.17), channel_id=1, source_target_pairs={{0,1},{1,0},{2,3},{3,2},{4,5},{5,4},{6,7},{7,6},{8,9},{9,8},{10,11... | collective-permute-start | bytes 294920 | tf_op jit(solution)/shard_map/ppermute | solution.py:344
  11.8 0.3 collective-permute-start.1
  12.0 1.5 %collective-permute-start.2 = (bf16[2,32,768]{2,1,0:T(8,128)(2,1)S(1)}, bf16[2,32,768]{2,1,0:T(8,128)(2,1)S(1)}, u32[]{:S(2)}, u32[]{:S(2)}) collective-permute-start(bf16[2,32,768]{2,1,0:T(8,128)(2,1)S(1)} %get-tuple-element.19), channel_id=1, source_target_pairs={{0,3},{1,2},{2,1},{3,0},{4,7},{5,6},{6,5},{7,4},{8,11},{9,10},{10,... | collective-permute-start | bytes 294920 | tf_op jit(solution)/shard_map/ppermute | solution.py:344
  13.5 0.0 collective-permute-done.refs_1_
  13.5 2.7 %collective-permute-done.1.refs_2_ = bf16[2,32,768]{2,1,0:T(8,128)(2,1)S(1)} collective-permute-done((bf16[2,32,768]{2,1,0:T(8,128)(2,1)S(1)}, bf16[2,32,768]{2,1,0:T(8,128)(2,1)S(1)}, u32[]{:S(2)}, u32[]{:S(2)}) %collective-permute-start.1) | collective-permute-done | bytes 98336 | tf_op jit(solution)/shard_map/ppermute | solution.py:344
  16.2 2.3 %collective-permute-done.2.refs_3_ = bf16[2,32,768]{2,1,0:T(8,128)(2,1)S(1)} collective-permute-done((bf16[2,32,768]{2,1,0:T(8,128)(2,1)S(1)}, bf16[2,32,768]{2,1,0:T(8,128)(2,1)S(1)}, u32[]{:S(2)}, u32[]{:S(2)}) %collective-permute-start.2) | collective-permute-done | bytes 98336 | tf_op jit(solution)/shard_map/ppermute | solution.py:344
  18.4 0.8 %plane_sum.1 = (f32[32,768]{1,0:T(8,128)S(1)}, bf16[32,768]{1,0:T(8,128)(2,1)S(1)}, bf16[32,768]{1,0:T(8,128)(2,1)S(1)}, bf16[32,768]{1,0:T(8,128)(2,1)S(1)}) custom-call(s32[32]{0:T(128)} %anchor_ref.3, s32[1]{0:T(128)} %bitcast.place_ref, bf16[2,32,768]{2,1,0:T(8,128)(2,1)S(1)} %get-tuple-element.16.refs_0_, ...), custom_call_target="tpu_custom_call" | custom-call | tf_op jit(solution)/shard_map/plane_sum/pallas_call | solution.py:232
  19.2 1.3 %collective-permute-start.3 = (bf16[32,768]{1,0:T(8,128)(2,1)S(1)}, bf16[32,768]{1,0:T(8,128)(2,1)S(1)}, u32[]{:S(2)}, u32[]{:S(2)}) collective-permute-start(bf16[32,768]{1,0:T(8,128)(2,1)S(1)} %get-tuple-element.21), channel_id=1, source_target_pairs={{0,4},{1,5},{2,6},{3,7},{4,0},{5,1},{6,2},{7,3},{8,12},{9,13},{10,... | collective-permute-start | bytes 147464 | tf_op jit(solution)/shard_map/ppermute | solution.py:344
  20.6 2.3 %collective-permute-start.4 = (bf16[32,768]{1,0:T(8,128)(2,1)S(1)}, bf16[32,768]{1,0:T(8,128)(2,1)S(1)}, u32[]{:S(2)}, u32[]{:S(2)}) collective-permute-start(bf16[32,768]{1,0:T(8,128)(2,1)S(1)} %get-tuple-element.22), channel_id=1, source_target_pairs={{0,8},{1,9},{2,10},{3,11},{4,12},{5,13},{6,14},{7,15},{8,0},{9,1},... | collective-permute-start | bytes 147464 | tf_op jit(solution)/shard_map/ppermute | solution.py:344
  22.9 0.0 collective-permute-start.5
  22.9 0.0 collective-permute-done.3.refs_0_
  22.9 1.8 %collective-permute-done.4.refs_1_ = bf16[32,768]{1,0:T(8,128)(2,1)S(1)} collective-permute-done((bf16[32,768]{1,0:T(8,128)(2,1)S(1)}, bf16[32,768]{1,0:T(8,128)(2,1)S(1)}, u32[]{:S(2)}, u32[]{:S(2)}) %collective-permute-start.4) | collective-permute-done | bytes 49184 | tf_op jit(solution)/shard_map/ppermute | solution.py:344
  24.7 3.0 %collective-permute-done.5.refs_2_ = bf16[32,768]{1,0:T(8,128)(2,1)S(1)} collective-permute-done((bf16[32,768]{1,0:T(8,128)(2,1)S(1)}, bf16[32,768]{1,0:T(8,128)(2,1)S(1)}, u32[]{:S(2)}, u32[]{:S(2)}) %collective-permute-start.5) | collective-permute-done | bytes 49184 | tf_op jit(solution)/shard_map/ppermute | solution.py:344
  27.7 0.0 copy-done
  27.7 1.1 %upconv.1 = (bf16[2,8,16,128]{3,2,1,0:T(8,128)(2,1)S(1)}, bf16[8,16,128]{2,1,0:T(8,128)(2,1)S(1)}, bf16[8,16,128]{2,1,0:T(8,128)(2,1)S(1)}) custom-call(s32[1]{0:T(128)} %bitcast.place_ref, s32[1,32]{1,0:T(1,128)} %bitcast.3, s32[1,32]{1,0:T(1,128)} %bitcast.4, f32[32,768]{1,0:T(8,128)S(1)} %get-tuple-element.20.kept, ...), custom_call_target="tpu_custom_call" | custom-call | tf_op jit(solution)/shard_map/upconv/pallas_call | solution.py:282
  28.8 2.0 %collective-permute-start.6 = (bf16[8,16,128]{2,1,0:T(8,128)(2,1)S(1)}, bf16[8,16,128]{2,1,0:T(8,128)(2,1)S(1)}, u32[]{:S(2)}, u32[]{:S(2)}) collective-permute-start(bf16[8,16,128]{2,1,0:T(8,128)(2,1)S(1)} %get-tuple-element.25), channel_id=1, source_target_pairs={{0,1},{1,0},{2,3},{3,2},{4,5},{5,4},{6,7},{7,6},{8,9},{9,8},{10,11... | collective-permute-start | bytes 98312 | tf_op jit(solution)/shard_map/ppermute | solution.py:344
  30.8 1.9 %collective-permute-start.7 = (bf16[8,16,128]{2,1,0:T(8,128)(2,1)S(1)}, bf16[8,16,128]{2,1,0:T(8,128)(2,1)S(1)}, u32[]{:S(2)}, u32[]{:S(2)}) collective-permute-start(bf16[8,16,128]{2,1,0:T(8,128)(2,1)S(1)} %get-tuple-element.26), channel_id=1, source_target_pairs={{1,2},{3,4},{5,6},{7,8},{9,10},{11,12},{13,14},{2,1},{4,3},{6,5},{... | collective-permute-start | bytes 98312 | tf_op jit(solution)/shard_map/ppermute | solution.py:388
  32.7 0.0 collective-permute-done.6.first_ref
  32.7 4.2 %collective-permute-done.7.second_ref = bf16[8,16,128]{2,1,0:T(8,128)(2,1)S(1)} collective-permute-done((bf16[8,16,128]{2,1,0:T(8,128)(2,1)S(1)}, bf16[8,16,128]{2,1,0:T(8,128)(2,1)S(1)}, u32[]{:S(2)}, u32[]{:S(2)}) %collective-permute-start.7) | collective-permute-done | bytes 32800 | tf_op jit(solution)/shard_map/ppermute | solution.py:388
  36.9 0.0 copy-done.1
  36.9 1.3 %conv.1 = bf16[2,8,16,128]{3,2,1,0:T(8,128)(2,1)} custom-call(s32[1]{0:T(128)} %bitcast.place_ref, bf16[2,8,16,128]{3,2,1,0:T(8,128)(2,1)S(1)} %get-tuple-element.24.up_ref, bf16[8,16,128]{2,1,0:T(8,128)(2,1)S(1)} %collective-permute-done.6.first_ref, bf16[8,16,128]{2,1,0:T(8,128)(2,1)S(1)} %collective-permute-done.7.second_ref, bf16[3456,128]{1,0:T(8,128)(2,1)S(1)} %copy-done.1), custom_call_target="tpu_custom_call" | custom-call | tf_op jit(solution)/shard_map/conv/pallas_call | solution.py:329
Async XLA Ops:
  0.0 27.7 %copy-start = (bf16[768,1024]{1,0:T(8,128)(2,1)S(1)}, bf16[768,1024]{1,0:T(8,128)(2,1)}, u32[]{:S(2)}) copy-start(bf16[768,1024]{1,0:T(8,128)(2,1)} %refs_3_.1) | copy-start | bytes 4718596
  11.0 25.9 %copy-start.1 = (bf16[3456,128]{1,0:T(8,128)(2,1)S(1)}, bf16[3456,128]{1,0:T(8,128)(2,1)}, u32[]{:S(2)}) copy-start(bf16[3456,128]{1,0:T(8,128)(2,1)} %weight.1) | copy-start | bytes 2654212
  11.0 2.5 %collective-permute-start = (bf16[2,32,768]{2,1,0:T(8,128)(2,1)S(1)}, bf16[2,32,768]{2,1,0:T(8,128)(2,1)S(1)}, u32[]{:S(2)}, u32[]{:S(2)}) collective-permute-start(bf16[2,32,768]{2,1,0:T(8,128)(2,1)S(1)} %get-tuple-element.17), channel_id=1, source_target_pairs={{0,1},{1,0},{2,3},{3,2},{4,5},{5,4},{6,7},{7,6},{8,9},{9,8},{10,11... | collective-permute-start | bytes 294920 | tf_op jit(solution)/shard_map/ppermute | solution.py:344
  11.8 4.4 %collective-permute-start.1 = (bf16[2,32,768]{2,1,0:T(8,128)(2,1)S(1)}, bf16[2,32,768]{2,1,0:T(8,128)(2,1)S(1)}, u32[]{:S(2)}, u32[]{:S(2)}) collective-permute-start(bf16[2,32,768]{2,1,0:T(8,128)(2,1)S(1)} %get-tuple-element.18), channel_id=1, source_target_pairs={{0,2},{1,3},{2,0},{3,1},{4,6},{5,7},{6,4},{7,5},{8,10},{9,11},{10,... | collective-permute-start | bytes 294920 | tf_op jit(solution)/shard_map/ppermute | solution.py:344
  12.0 6.4 %collective-permute-start.2 = (bf16[2,32,768]{2,1,0:T(8,128)(2,1)S(1)}, bf16[2,32,768]{2,1,0:T(8,128)(2,1)S(1)}, u32[]{:S(2)}, u32[]{:S(2)}) collective-permute-start(bf16[2,32,768]{2,1,0:T(8,128)(2,1)S(1)} %get-tuple-element.19), channel_id=1, source_target_pairs={{0,3},{1,2},{2,1},{3,0},{4,7},{5,6},{6,5},{7,4},{8,11},{9,10},{10,... | collective-permute-start | bytes 294920 | tf_op jit(solution)/shard_map/ppermute | solution.py:344
  19.2 3.7 %collective-permute-start.3 = (bf16[32,768]{1,0:T(8,128)(2,1)S(1)}, bf16[32,768]{1,0:T(8,128)(2,1)S(1)}, u32[]{:S(2)}, u32[]{:S(2)}) collective-permute-start(bf16[32,768]{1,0:T(8,128)(2,1)S(1)} %get-tuple-element.21), channel_id=1, source_target_pairs={{0,4},{1,5},{2,6},{3,7},{4,0},{5,1},{6,2},{7,3},{8,12},{9,13},{10,... | collective-permute-start | bytes 147464 | tf_op jit(solution)/shard_map/ppermute | solution.py:344
  20.6 4.1 %collective-permute-start.4 = (bf16[32,768]{1,0:T(8,128)(2,1)S(1)}, bf16[32,768]{1,0:T(8,128)(2,1)S(1)}, u32[]{:S(2)}, u32[]{:S(2)}) collective-permute-start(bf16[32,768]{1,0:T(8,128)(2,1)S(1)} %get-tuple-element.22), channel_id=1, source_target_pairs={{0,8},{1,9},{2,10},{3,11},{4,12},{5,13},{6,14},{7,15},{8,0},{9,1},... | collective-permute-start | bytes 147464 | tf_op jit(solution)/shard_map/ppermute | solution.py:344
  22.9 4.8 %collective-permute-start.5 = (bf16[32,768]{1,0:T(8,128)(2,1)S(1)}, bf16[32,768]{1,0:T(8,128)(2,1)S(1)}, u32[]{:S(2)}, u32[]{:S(2)}) collective-permute-start(bf16[32,768]{1,0:T(8,128)(2,1)S(1)} %get-tuple-element.23), channel_id=1, source_target_pairs={{0,12},{1,13},{2,14},{3,15},{4,8},{5,9},{6,10},{7,11},{8,4},{9,5},... | collective-permute-start | bytes 147464 | tf_op jit(solution)/shard_map/ppermute | solution.py:344
  28.8 3.9 %collective-permute-start.6 = (bf16[8,16,128]{2,1,0:T(8,128)(2,1)S(1)}, bf16[8,16,128]{2,1,0:T(8,128)(2,1)S(1)}, u32[]{:S(2)}, u32[]{:S(2)}) collective-permute-start(bf16[8,16,128]{2,1,0:T(8,128)(2,1)S(1)} %get-tuple-element.25), channel_id=1, source_target_pairs={{0,1},{1,0},{2,3},{3,2},{4,5},{5,4},{6,7},{7,6},{8,9},{9,8},{10,11... | collective-permute-start | bytes 98312 | tf_op jit(solution)/shard_map/ppermute | solution.py:344
  30.8 6.1 %collective-permute-start.7 = (bf16[8,16,128]{2,1,0:T(8,128)(2,1)S(1)}, bf16[8,16,128]{2,1,0:T(8,128)(2,1)S(1)}, u32[]{:S(2)}, u32[]{:S(2)}) collective-permute-start(bf16[8,16,128]{2,1,0:T(8,128)(2,1)S(1)} %get-tuple-element.26), channel_id=1, source_target_pairs={{1,2},{3,4},{5,6},{7,8},{9,10},{11,12},{13,14},{2,1},{4,3},{6,5},{... | collective-permute-start | bytes 98312 | tf_op jit(solution)/shard_map/ppermute | solution.py:388

commit v3 on v2

--- a/solution.py
+++ b/solution.py
@@ -41,59 +41,61 @@
     return value
 
 
-def window_kernel(
-    anchor_ref,
-    count_ref,
-    place_ref,
-    gain_ct_hbm,
-    gain_pet_hbm,
-    gain_ffn_hbm,
-    ct_hbm,
-    pet_hbm,
-    wq_hbm,
-    wk_hbm,
-    wv_hbm,
-    wo_hbm,
-    wu_hbm,
-    wd_hbm,
-    *rest,
-):
-    outs = rest[:WDEP]
-    gains = rest[WDEP : WDEP + 3]
-    tok, wq, wk, wv, wo, wu, wd, normed, q_all, k_all, v_all, mixed, sems = rest[WDEP + 3 :]
-    slots, tokens, width = ct_hbm.shape
+def ffn_rows(base, mixed_rows, gain_row, wo, wu, wd, before_up=None, before_down=None):
+    mid = base.astype(jnp.float32) + dot(mixed_rows, wo[...])
+    normed_mid = rms_scale(mid, gain_row)
+    if before_up is not None:
+        before_up()
+    hidden = jax.nn.gelu(dot(normed_mid, wu[...]), approximate=True)
+    half = hidden.shape[0] // 2
+    hidden_sum = (hidden[:half] + hidden[half:]).astype(jnp.bfloat16)
+    if before_down is not None:
+        before_down()
+    return mid[:half] + mid[half:] + dot(hidden_sum, wd[...])
+
+
+def window_kernel(*refs):
+    sources, outs, scratch = refs[:13], refs[13:22], refs[22:]
+    gain_refs = (scratch[0], scratch[1], outs[8])
+    anchor_ref, count_ref, tok, wq, wk, wv, normed, q_all, k_all, v_all, mixed, sems = scratch[2:]
+    far_out = outs[:2]
+    rest_mixed, rest_base, rest_scale, wo, wu, wd = outs[2:8]
+    slots, tokens, width = sources[5].shape
     rows = slots * tokens
     cells = tokens // WDEP
-    sources = [
-        (ct_hbm, tok.at[0]),
-        (pet_hbm, tok.at[1]),
-        (wq_hbm, wq),
-        (wk_hbm, wk),
-        (wv_hbm, wv),
-        (wo_hbm, wo),
-        (wu_hbm, wu),
-        (wd_hbm, wd),
-        (gain_ct_hbm, gains[0]),
-        (gain_pet_hbm, gains[1]),
-        (gain_ffn_hbm, gains[2]),
+    targets = (
+        anchor_ref,
+        count_ref,
+        *gain_refs,
+        tok.at[0],
+        tok.at[1],
+        wq,
+        wk,
+        wv,
+        wo,
+        wu,
+        wd,
+    )
+    copies = [
+        pltpu.make_async_copy(src, dst, sems.at[i])
+        for i, (src, dst) in enumerate(zip(sources, targets, strict=True))
     ]
-    copies = [pltpu.make_async_copy(src, dst, sems.at[i]) for i, (src, dst) in enumerate(sources)]
-    for i in (8, 9, 10, 0, 1, 2, 3, 4, 5, 6, 7):
+    for i in (2, 3, 5, 6, 7, 0, 1, 4, 8, 9, 10, 11, 12):
         copies[i].start()
-    position = place_ref[0]
+    position = lax.axis_index("brick")
     residue = lax.rem(position, WDEP)
 
-    for i in (8, 9, 10):
-        copies[i].wait()
+    copies[2].wait()
+    copies[3].wait()
     for m in range(2):
-        copies[m].wait()
+        copies[5 + m].wait()
         for s in range(slots):
             start = m * rows + s * tokens
             normed[start : start + tokens, :] = rms_scale(
-                tok[m, s].astype(jnp.float32), gains[m][...][None, :]
+                tok[m, s].astype(jnp.float32), gain_refs[m][...][None, :]
             )
     for i, (weight, result) in enumerate(((wq, q_all), (wk, k_all), (wv, v_all))):
-        copies[2 + i].wait()
+        copies[7 + i].wait()
         result[...] = dot(normed[...], weight[...]).astype(jnp.bfloat16)
 
     low = lax.broadcasted_iota(jnp.int32, (tokens, LANES), 1) < DH
@@ -132,45 +134,57 @@
                     jnp.bfloat16
                 )
 
-    copies[5].wait()
-    for phase in range(2):
-        rels = (2, 3) if phase == 0 else (1, 0)
-        picks = []
+    for i in (0, 1, 4, 10):
+        copies[i].wait()
+
+    def picked(rels):
+        picks, base, chosen = [], [], []
         for rel in rels:
             for s in range(slots):
-                slot = lax.div(position, 1) * slots + s
+                slot = position * slots + s
                 depth = lax.rem((residue ^ rel) + WDEP * NWRAP - anchor_ref[slot], WDEP)
-                picks.append((rel, s, slot, depth))
-        base = []
-        picked = []
+                factor = jnp.full((1, LANES), count_ref[slot], jnp.int32).astype(jnp.float32) * (
+                    1.0 / (2.0 * tokens)
+                )
+                picks.append((s, depth, factor * bell_at(depth)))
         for m in range(2):
-            for rel, s, slot, depth in picks:
-                offset = pl.multiple_of(depth * cells, cells)
-                base.append(tok[m, s, pl.ds(offset, cells), :])
+            for s, depth, _ in picks:
+                base.append(tok[m, s, pl.ds(pl.multiple_of(depth * cells, cells), cells), :])
                 place = pl.multiple_of(m * rows + s * tokens + depth * cells, cells)
-                picked.append(mixed[pl.ds(place, cells), :])
-        mid = jnp.concatenate(base, axis=0).astype(jnp.float32) + dot(
-            jnp.concatenate(picked, axis=0), wo[...]
+                chosen.append(mixed[pl.ds(place, cells), :])
+        return (
+            [scale for _, _, scale in picks],
+            jnp.concatenate(base, axis=0),
+            jnp.concatenate(chosen, axis=0),
         )
-        normed_mid = rms_scale(mid, gains[2][...][None, :])
-        if phase == 0:
-            copies[6].wait()
-        hidden = jax.nn.gelu(dot(normed_mid, wu[...]), approximate=True)
-        half = hidden.shape[0] // 2
-        hidden_sum = (hidden[:half] + hidden[half:]).astype(jnp.bfloat16)
-        if phase == 0:
-            copies[7].wait()
-        joined = mid[:half] + mid[half:] + dot(hidden_sum, wd[...])
-        for j, (rel, s, slot, depth) in enumerate(picks):
-            factor = jnp.full((1, width), count_ref[slot], jnp.int32).astype(jnp.float32) * (
-                1.0 / (2.0 * tokens)
-            )
-            outs[rel][s] = (
-                joined[j * cells : (j + 1) * cells] * (factor * bell_at(depth))
-            ).astype(jnp.bfloat16)
+
+    scales, base, chosen = picked((1, 0))
+    rest_base[...] = base
+    rest_mixed[...] = chosen
+    for j, scale in enumerate(scales):
+        rest_scale[j * cells : (j + 1) * cells, :] = jnp.broadcast_to(scale, (cells, LANES))
+    scales, base, chosen = picked((2, 3))
+    joined = ffn_rows(
+        base, chosen, gain_refs[2][...][None, :], wo, wu, wd, copies[11].wait, copies[12].wait
+    )
+    for j, scale in enumerate(scales):
+        far_out[j // slots][j % slots] = (
+            joined[j * cells : (j + 1) * cells] * scale[:, :1]
+        ).astype(jnp.bfloat16)
+
+
+def near_kernel(rest_mixed, rest_base, rest_scale, wo, wu, wd, gain, near_out, own_out):
+    slots, cells, width = near_out.shape
+    joined = ffn_rows(rest_base[...], rest_mixed[...], gain[...][None, :], wo, wu, wd)
+    joined = (joined * rest_scale[:, :1]).astype(jnp.bfloat16)
+    for j, out in enumerate((near_out, own_out)):
+        for s in range(slots):
+            start = (j * slots + s) * cells
+            out[s] = joined[start : start + cells]
 
 
 NWRAP = 1 << 20
+ARRIVAL = (2, 3, 1, 0)
 
 
 def in_hbm(array):
@@ -184,26 +198,44 @@
 SMALL = pltpu.CompilerParams(vmem_limit_bytes=12 * 1024 * 1024)
 
 
-def window_call(position, anchor, count, gains, ct_win, pet_win, weights):
+def window_call(anchor, count, gains, ct_win, pet_win, weights):
     slots, tokens, width = ct_win.shape
     rows = 2 * slots * tokens
     cells = tokens // WDEP
+    half = slots * (WDEP // 2) * cells
     out = pltpu.VMEM((slots, cells, width), jnp.bfloat16)
-    token_buffer = pltpu.VMEM((2, slots, tokens, width), jnp.bfloat16)
+    rest = pltpu.VMEM((2 * half, width), jnp.bfloat16)
     big = pltpu.VMEM((rows, width), jnp.bfloat16)
-    return pl.pallas_call(
+    far_two, far_three, *passed = pl.pallas_call(
         window_kernel,
-        out_shape=[out] * WDEP,
-        in_specs=[SMEM, SMEM, SMEM] + [ANY] * 11,
-        out_specs=[VMEM] * WDEP,
-        scratch_shapes=[pltpu.VMEM((width,), jnp.float32)] * 3
-        + [token_buffer]
-        + [pltpu.VMEM(w.shape, w.dtype) for w in weights]
+        out_shape=[out, out, rest, rest, pltpu.VMEM((half, LANES), jnp.float32)]
+        + [pltpu.VMEM(w.shape, w.dtype) for w in weights[3:]]
+        + [pltpu.VMEM((width,), jnp.float32)],
+        in_specs=[ANY] * 13,
+        out_specs=[VMEM] * 9,
+        scratch_shapes=[pltpu.VMEM((width,), jnp.float32)] * 2
+        + [pltpu.SMEM(anchor.shape, jnp.int32)] * 2
+        + [pltpu.VMEM((2, slots, tokens, width), jnp.bfloat16)]
+        + [pltpu.VMEM(w.shape, w.dtype) for w in weights[:3]]
         + [big] * 5
-        + [pltpu.SemaphoreType.DMA((11,))],
-        compiler_params=pltpu.CompilerParams(vmem_limit_bytes=40 * 1024 * 1024),
+        + [pltpu.SemaphoreType.DMA((13,))],
+        compiler_params=pltpu.CompilerParams(vmem_limit_bytes=28 * 1024 * 1024),
         name="window_layer",
-    )(in_hbm(anchor), in_hbm(count), position, *map(in_hbm, (*gains, ct_win, pet_win, *weights)))
+    )(*map(in_hbm, (anchor, count, *gains, ct_win, pet_win, *weights)))
+    near, own = pl.pallas_call(
+        near_kernel,
+        out_shape=[out, out],
+        in_specs=[VMEM] * 7,
+        out_specs=[VMEM] * 2,
+        compiler_params=SMALL,
+        cost_estimate=pl.CostEstimate(
+            flops=2 * half * width * (2 * width + 3 * weights[4].shape[1]),
+            bytes_accessed=4 * half * width,
+            transcendentals=0,
+        ),
+        name="near_rows",
+    )(*map(in_vmem, passed))
+    return own, near, far_two, far_three
 
 
 def gather_kernel(outer, anchor_ref, place_ref, *refs):
@@ -214,14 +246,14 @@
     residue = lax.rem(position, WDEP)
     block = lax.div(position, WDEP)
     total[...] = jnp.zeros_like(total)
-    for rel in range(WDEP):
+    for source, rel in zip(sources, ARRIVAL, strict=True):
         for s in range(slots):
             slot = (block * WDEP + (residue ^ rel)) * slots + s
             start = anchor_ref[slot]
             depth = lax.rem(residue + WDEP * NWRAP - start, WDEP)
             target = lax.div(start + depth, WDEP)
             step = target ^ block
-            total[step] += sources[rel][s].astype(jnp.float32)
+            total[step] += source[s].astype(jnp.float32)
     kept[...] = total[0]
     for k in range(1, outer):
         sent[k - 1][...] = total[k].astype(jnp.bfloat16)
@@ -367,7 +399,6 @@
     outer = total // WDEP
     position = lax.axis_index("brick").reshape(1)
     blocks = window_call(
-        position,
         placed_anchor,
         placed_count,
         (norm_ct, norm_pet, norm_ffn),
@@ -375,11 +406,12 @@
         pet_win,
         (w_query, w_key, w_value, w_out, w_up, w_down),
     )
-    arrived = {rel: swap(blocks[rel], rel, total) for rel in (2, 3, 1)}
-    sums = gather_call(
-        outer, position, placed_anchor, [blocks[0]] + [arrived[rel] for rel in range(1, WDEP)]
-    )
-    pieces = [swap(sums[k], k * WDEP, total) for k in range(1, outer)]
+    own, near, far_two, far_three = blocks
+    far_two, far_three = swap(far_two, 2, total), swap(far_three, 3, total)
+    near, far_two = lax.optimization_barrier((near, far_two))
+    arrived = (far_two, far_three, swap(near, 1, total), own)
+    sums = gather_call(outer, position, placed_anchor, arrived)
+    pieces = [swap(sums[k], k * WDEP, total) for k in range(outer - 1, 0, -1)]
     upsampled, first, second = upconv_call(
         tokens, channels, position, placed_anchor, placed_count, sums[0], pieces, w_upconv
     )

time: 38.4 us -> 34.7 us (0.904)
  the two profiles are of different devices: /device:TPU:7 before, /device:TPU:3 now
where the time goes in v3:
time: 34.7 us; the launch traced here: 34.5 us
  Pallas kernels  13.9 us (40%)
  starting transfers between devices  11.4 us (33%)
  waiting for transfers between devices  9.06 us (26%)
    ppermute x7, starting transfers between devices, swap(): lax.ppermute(values, 'brick', [(i, i ^ distance) for i in range(total)])  9.42 us
    pallas_call x1, Pallas kernels, window_call(): pl.pallas_call(window_kernel, out_shape=[out, out, rest, rest, pltpu.VMEM...  8.65 us
    ppermute x7, waiting for transfers between devices, swap(): lax.ppermute(values, 'brick', [(i, i ^ distance) for i in range(total)])  4.97 us
    ppermute x1, waiting for transfers between devices, on_device(): far = lax.ppermute(second, 'brick', pairs + [(j, i) for i, j in pairs])  4.09 us
    ppermute x1, starting transfers between devices, on_device(): far = lax.ppermute(second, 'brick', pairs + [(j, i) for i, j in pairs])  2.01 us
    pallas_call x1, Pallas kernels, window_call(): pl.pallas_call(near_kernel, out_shape=[out, out], in_specs=[VMEM] * 7, ou...  1.97 us
    pallas_call x1, Pallas kernels, conv_call(): pl.pallas_call(conv_kernel, out_shape=jax.ShapeDtypeStruct(upsampled.shap...  1.32 us
    pallas_call x1, Pallas kernels, upconv_call(): pl.pallas_call(functools.partial(upconv_kernel, tokens), out_shape=[pltpu...  1.14 us
  transfers between devices with their start and end apart: 8, of which 5 were waited for; matrix products, arithmetic and copies ran while one was open for 0% of the time, Pallas kernels for 6%

profile of v3, /device:TPU:3, one launch (start us, length us, event | category | flops | bytes accessed | tf_op | source)
XLA Modules:
  0.0 34.5 jit_solution(3589347296447801481)
XLA Ops:
  0.0 8.7 %window_layer.1 = (bf16[2,32,768]{2,1,0:T(8,128)(2,1)S(1)}, bf16[2,32,768]{2,1,0:T(8,128)(2,1)S(1)}, bf16[256,768]{1,0:T(8,128)(2,1)S(1)}, bf16[256,768]{1,0:T(8...) custom-call(s32[32]{0:T(128)} %anchor_ref.1, ...), custom_call_target="tpu_custom_call" | custom-call | tf_op jit(solution)/shard_map/window_layer/pallas_call | solution.py:209
  8.7 0.1 collective-permute-start
  8.7 2.3 %collective-permute-start.1 = (bf16[2,32,768]{2,1,0:T(8,128)(2,1)S(1)}, bf16[2,32,768]{2,1,0:T(8,128)(2,1)S(1)}, u32[]{:S(2)}, u32[]{:S(2)}) collective-permute-start(bf16[2,32,768]{2,1,0:T(8,128)(2,1)S(1)} %get-tuple-element.35), channel_id=1, source_target_pairs={{0,3},{1,2},{2,1},{3,0},{4,7},{5,6},{6,5},{7,4},{8,11},{9,10},{10,... | collective-permute-start | bytes 294920 | tf_op jit(solution)/shard_map/ppermute | solution.py:376
  11.0 2.0 %near_rows.1 = (bf16[2,32,768]{2,1,0:T(8,128)(2,1)S(1)}, bf16[2,32,768]{2,1,0:T(8,128)(2,1)S(1)}) custom-call(bf16[256,768]{1,0:T(8,128)(2,1)S(1)} %get-tuple-element.25.rest_mixed, bf16[256,768]{1,0:T(8,128)(2,1)S(1)} %get-tuple-element.26.rest_base, f32[128,128]{1,0:T(8,128)S(1)} %get-tuple-element.27.rest_scale, ...), custom_call_target="tpu_custom_call" | custom-call | flops 1207959552 | bytes 393216 | tf_op jit(solution)/shard_map/near_rows/pallas_call | solution.py:225
  13.0 0.0 copy-start.1
  13.0 0.0 collective-permute-done.refs_0_
  13.0 2.0 %collective-permute-start.2 = (bf16[2,32,768]{2,1,0:T(8,128)(2,1)S(1)}, bf16[2,32,768]{2,1,0:T(8,128)(2,1)S(1)}, u32[]{:S(2)}, u32[]{:S(2)}) collective-permute-start(bf16[2,32,768]{2,1,0:T(8,128)(2,1)S(1)} %get-tuple-element.36), channel_id=1, source_target_pairs={{0,1},{1,0},{2,3},{3,2},{4,5},{5,4},{6,7},{7,6},{8,9},{9,8},{10,11... | collective-permute-start | bytes 294920 | tf_op jit(solution)/shard_map/ppermute | solution.py:376
  15.0 0.4 %collective-permute-done.1.refs_1_ = bf16[2,32,768]{2,1,0:T(8,128)(2,1)S(1)} collective-permute-done((bf16[2,32,768]{2,1,0:T(8,128)(2,1)S(1)}, bf16[2,32,768]{2,1,0:T(8,128)(2,1)S(1)}, u32[]{:S(2)}, u32[]{:S(2)}) %collective-permute-start.1) | collective-permute-done | bytes 98336 | tf_op jit(solution)/shard_map/ppermute | solution.py:376
  15.4 0.6 %collective-permute-done.2.refs_2_ = bf16[2,32,768]{2,1,0:T(8,128)(2,1)S(1)} collective-permute-done((bf16[2,32,768]{2,1,0:T(8,128)(2,1)S(1)}, bf16[2,32,768]{2,1,0:T(8,128)(2,1)S(1)}, u32[]{:S(2)}, u32[]{:S(2)}) %collective-permute-start.2) | collective-permute-done | bytes 98336 | tf_op jit(solution)/shard_map/ppermute | solution.py:376
  15.9 0.8 %plane_sum.1 = (f32[32,768]{1,0:T(8,128)S(1)}, bf16[32,768]{1,0:T(8,128)(2,1)S(1)}, bf16[32,768]{1,0:T(8,128)(2,1)S(1)}, bf16[32,768]{1,0:T(8,128)(2,1)S(1)}) custom-call(s32[32]{0:T(128)} %anchor_ref.1, s32[1]{0:T(128)} %bitcast.place_ref, bf16[2,32,768]{2,1,0:T(8,128)(2,1)S(1)} %collective-permute-done.refs_0_, ...), custom_call_target="tpu_custom_call" | custom-call | tf_op jit(solution)/shard_map/plane_sum/pallas_call | solution.py:264
  16.7 3.4 %collective-permute-start.3 = (bf16[32,768]{1,0:T(8,128)(2,1)S(1)}, bf16[32,768]{1,0:T(8,128)(2,1)S(1)}, u32[]{:S(2)}, u32[]{:S(2)}) collective-permute-start(bf16[32,768]{1,0:T(8,128)(2,1)S(1)} %get-tuple-element.39), channel_id=1, source_target_pairs={{0,12},{1,13},{2,14},{3,15},{4,8},{5,9},{6,10},{7,11},{8,4},{9,5},... | collective-permute-start | bytes 147464 | tf_op jit(solution)/shard_map/ppermute | solution.py:376
  20.2 0.0 collective-permute-start.4
  20.2 0.4 %collective-permute-start.5 = (bf16[32,768]{1,0:T(8,128)(2,1)S(1)}, bf16[32,768]{1,0:T(8,128)(2,1)S(1)}, u32[]{:S(2)}, u32[]{:S(2)}) collective-permute-start(bf16[32,768]{1,0:T(8,128)(2,1)S(1)} %get-tuple-element.41), channel_id=1, source_target_pairs={{0,4},{1,5},{2,6},{3,7},{4,0},{5,1},{6,2},{7,3},{8,12},{9,13},{10,... | collective-permute-start | bytes 147464 | tf_op jit(solution)/shard_map/ppermute | solution.py:376
  20.5 1.2 %collective-permute-done.3.refs_0_ = bf16[32,768]{1,0:T(8,128)(2,1)S(1)} collective-permute-done((bf16[32,768]{1,0:T(8,128)(2,1)S(1)}, bf16[32,768]{1,0:T(8,128)(2,1)S(1)}, u32[]{:S(2)}, u32[]{:S(2)}) %collective-permute-start.3) | collective-permute-done | bytes 49184 | tf_op jit(solution)/shard_map/ppermute | solution.py:376
  21.8 2.8 %collective-permute-done.4.refs_1_ = bf16[32,768]{1,0:T(8,128)(2,1)S(1)} collective-permute-done((bf16[32,768]{1,0:T(8,128)(2,1)S(1)}, bf16[32,768]{1,0:T(8,128)(2,1)S(1)}, u32[]{:S(2)}, u32[]{:S(2)}) %collective-permute-start.4) | collective-permute-done | bytes 49184 | tf_op jit(solution)/shard_map/ppermute | solution.py:376
  24.5 0.0 collective-permute-done.5.refs_2_
  24.5 0.0 copy-done
  24.6 1.1 %upconv.1 = (bf16[2,8,16,128]{3,2,1,0:T(8,128)(2,1)S(1)}, bf16[8,16,128]{2,1,0:T(8,128)(2,1)S(1)}, bf16[8,16,128]{2,1,0:T(8,128)(2,1)S(1)}) custom-call(s32[1]{0:T(128)} %bitcast.place_ref, s32[1,32]{1,0:T(1,128)} %bitcast.3, s32[1,32]{1,0:T(1,128)} %bitcast.4, f32[32,768]{1,0:T(8,128)S(1)} %get-tuple-element.38.kept, ...), custom_call_target="tpu_custom_call" | custom-call | tf_op jit(solution)/shard_map/upconv/pallas_call | solution.py:314
  25.7 1.3 %collective-permute-start.6 = (bf16[8,16,128]{2,1,0:T(8,128)(2,1)S(1)}, bf16[8,16,128]{2,1,0:T(8,128)(2,1)S(1)}, u32[]{:S(2)}, u32[]{:S(2)}) collective-permute-start(bf16[8,16,128]{2,1,0:T(8,128)(2,1)S(1)} %get-tuple-element.43), channel_id=1, source_target_pairs={{0,1},{1,0},{2,3},{3,2},{4,5},{5,4},{6,7},{7,6},{8,9},{9,8},{10,11... | collective-permute-start | bytes 98312 | tf_op jit(solution)/shard_map/ppermute | solution.py:376
  27.0 2.0 %collective-permute-start.7 = (bf16[8,16,128]{2,1,0:T(8,128)(2,1)S(1)}, bf16[8,16,128]{2,1,0:T(8,128)(2,1)S(1)}, u32[]{:S(2)}, u32[]{:S(2)}) collective-permute-start(bf16[8,16,128]{2,1,0:T(8,128)(2,1)S(1)} %get-tuple-element.44), channel_id=1, source_target_pairs={{1,2},{3,4},{5,6},{7,8},{9,10},{11,12},{13,14},{2,1},{4,3},{6,5},{... | collective-permute-start | bytes 98312 | tf_op jit(solution)/shard_map/ppermute | solution.py:420
  29.0 0.0 collective-permute-done.6.first_ref
  29.0 4.1 %collective-permute-done.7.second_ref = bf16[8,16,128]{2,1,0:T(8,128)(2,1)S(1)} collective-permute-done((bf16[8,16,128]{2,1,0:T(8,128)(2,1)S(1)}, bf16[8,16,128]{2,1,0:T(8,128)(2,1)S(1)}, u32[]{:S(2)}, u32[]{:S(2)}) %collective-permute-start.7) | collective-permute-done | bytes 32800 | tf_op jit(solution)/shard_map/ppermute | solution.py:420
  33.1 0.0 copy-done.1
  33.1 1.3 %conv.1 = bf16[2,8,16,128]{3,2,1,0:T(8,128)(2,1)} custom-call(s32[1]{0:T(128)} %bitcast.place_ref, bf16[2,8,16,128]{3,2,1,0:T(8,128)(2,1)S(1)} %get-tuple-element.42.up_ref, bf16[8,16,128]{2,1,0:T(8,128)(2,1)S(1)} %collective-permute-done.6.first_ref, bf16[8,16,128]{2,1,0:T(8,128)(2,1)S(1)} %collective-permute-done.7.second_ref, bf16[3456,128]{1,0:T(8,128)(2,1)S(1)} %copy-done.1), custom_call_target="tpu_custom_call" | custom-call | tf_op jit(solution)/shard_map/conv/pallas_call | solution.py:361
  (1 shorter events, 0.0 us)
Async XLA Ops:
  8.7 4.4 %collective-permute-start = (bf16[2,32,768]{2,1,0:T(8,128)(2,1)S(1)}, bf16[2,32,768]{2,1,0:T(8,128)(2,1)S(1)}, u32[]{:S(2)}, u32[]{:S(2)}) collective-permute-start(bf16[2,32,768]{2,1,0:T(8,128)(2,1)S(1)} %get-tuple-element.33), channel_id=1, source_target_pairs={{0,2},{1,3},{2,0},{3,1},{4,6},{5,7},{6,4},{7,5},{8,10},{9,11},{10,... | collective-permute-start | bytes 294920 | tf_op jit(solution)/shard_map/ppermute | solution.py:376
  8.7 6.6 %collective-permute-start.1 = (bf16[2,32,768]{2,1,0:T(8,128)(2,1)S(1)}, bf16[2,32,768]{2,1,0:T(8,128)(2,1)S(1)}, u32[]{:S(2)}, u32[]{:S(2)}) collective-permute-start(bf16[2,32,768]{2,1,0:T(8,128)(2,1)S(1)} %get-tuple-element.35), channel_id=1, source_target_pairs={{0,3},{1,2},{2,1},{3,0},{4,7},{5,6},{6,5},{7,4},{8,11},{9,10},{10,... | collective-permute-start | bytes 294920 | tf_op jit(solution)/shard_map/ppermute | solution.py:376
  11.0 13.5 %copy-start = (bf16[768,1024]{1,0:T(8,128)(2,1)S(1)}, bf16[768,1024]{1,0:T(8,128)(2,1)}, u32[]{:S(2)}) copy-start(bf16[768,1024]{1,0:T(8,128)(2,1)} %refs_3_.3) | copy-start | bytes 4718596
  13.0 20.1 %copy-start.1 = (bf16[3456,128]{1,0:T(8,128)(2,1)S(1)}, bf16[3456,128]{1,0:T(8,128)(2,1)}, u32[]{:S(2)}) copy-start(bf16[3456,128]{1,0:T(8,128)(2,1)} %weight.1) | copy-start | bytes 2654212
  13.0 2.9 %collective-permute-start.2 = (bf16[2,32,768]{2,1,0:T(8,128)(2,1)S(1)}, bf16[2,32,768]{2,1,0:T(8,128)(2,1)S(1)}, u32[]{:S(2)}, u32[]{:S(2)}) collective-permute-start(bf16[2,32,768]{2,1,0:T(8,128)(2,1)S(1)} %get-tuple-element.36), channel_id=1, source_target_pairs={{0,1},{1,0},{2,3},{3,2},{4,5},{5,4},{6,7},{7,6},{8,9},{9,8},{10,11... | collective-permute-start | bytes 294920 | tf_op jit(solution)/shard_map/ppermute | solution.py:376
  16.7 5.0 %collective-permute-start.3 = (bf16[32,768]{1,0:T(8,128)(2,1)S(1)}, bf16[32,768]{1,0:T(8,128)(2,1)S(1)}, u32[]{:S(2)}, u32[]{:S(2)}) collective-permute-start(bf16[32,768]{1,0:T(8,128)(2,1)S(1)} %get-tuple-element.39), channel_id=1, source_target_pairs={{0,12},{1,13},{2,14},{3,15},{4,8},{5,9},{6,10},{7,11},{8,4},{9,5},... | collective-permute-start | bytes 147464 | tf_op jit(solution)/shard_map/ppermute | solution.py:376
  20.2 4.4 %collective-permute-start.4 = (bf16[32,768]{1,0:T(8,128)(2,1)S(1)}, bf16[32,768]{1,0:T(8,128)(2,1)S(1)}, u32[]{:S(2)}, u32[]{:S(2)}) collective-permute-start(bf16[32,768]{1,0:T(8,128)(2,1)S(1)} %get-tuple-element.40), channel_id=1, source_target_pairs={{0,8},{1,9},{2,10},{3,11},{4,12},{5,13},{6,14},{7,15},{8,0},{9,1},... | collective-permute-start | bytes 147464 | tf_op jit(solution)/shard_map/ppermute | solution.py:376
  20.2 4.4 %collective-permute-start.5 = (bf16[32,768]{1,0:T(8,128)(2,1)S(1)}, bf16[32,768]{1,0:T(8,128)(2,1)S(1)}, u32[]{:S(2)}, u32[]{:S(2)}) collective-permute-start(bf16[32,768]{1,0:T(8,128)(2,1)S(1)} %get-tuple-element.41), channel_id=1, source_target_pairs={{0,4},{1,5},{2,6},{3,7},{4,0},{5,1},{6,2},{7,3},{8,12},{9,13},{10,... | collective-permute-start | bytes 147464 | tf_op jit(solution)/shard_map/ppermute | solution.py:376
  25.7 3.3 %collective-permute-start.6 = (bf16[8,16,128]{2,1,0:T(8,128)(2,1)S(1)}, bf16[8,16,128]{2,1,0:T(8,128)(2,1)S(1)}, u32[]{:S(2)}, u32[]{:S(2)}) collective-permute-start(bf16[8,16,128]{2,1,0:T(8,128)(2,1)S(1)} %get-tuple-element.43), channel_id=1, source_target_pairs={{0,1},{1,0},{2,3},{3,2},{4,5},{5,4},{6,7},{7,6},{8,9},{9,8},{10,11... | collective-permute-start | bytes 98312 | tf_op jit(solution)/shard_map/ppermute | solution.py:376
  27.0 6.1 %collective-permute-start.7 = (bf16[8,16,128]{2,1,0:T(8,128)(2,1)S(1)}, bf16[8,16,128]{2,1,0:T(8,128)(2,1)S(1)}, u32[]{:S(2)}, u32[]{:S(2)}) collective-permute-start(bf16[8,16,128]{2,1,0:T(8,128)(2,1)S(1)} %get-tuple-element.44), channel_id=1, source_target_pairs={{1,2},{3,4},{5,6},{7,8},{9,10},{11,12},{13,14},{2,1},{4,3},{6,5},{... | collective-permute-start | bytes 98312 | tf_op jit(solution)/shard_map/ppermute | solution.py:420

commit v4 on v3

v4 whole, which is shorter than its diff:
```python
import functools
import math

import jax
import jax.numpy as jnp
from jax import lax
from jax.experimental import pallas as pl
from jax.experimental.pallas import tpu as pltpu
from jax.sharding import PartitionSpec as P

DH = 64
PY = 4
PX = 8
WDEP = 4
LANES = 128

epsilon = 1e-06

VMEM = pl.BlockSpec(memory_space=pltpu.VMEM)
SMEM = pl.BlockSpec(memory_space=pltpu.SMEM)
ANY = pl.BlockSpec(memory_space=pl.ANY)

BELL = [
    math.exp(-((i - (WDEP - 1) / 2.0) ** 2) / (2.0 * (WDEP / 4.0) ** 2)) for i in range(WDEP)
]


def rms_scale(inputs, gain_vec):
    mean_square = jnp.mean(inputs * inputs, axis=-1, keepdims=True)
    return (inputs * lax.rsqrt(mean_square + epsilon) * gain_vec).astype(jnp.bfloat16)


def dot(left, right):
    return jnp.dot(left, right, preferred_element_type=jnp.float32)


def bell_at(depth):
    value = jnp.float32(BELL[0])
    for i in range(1, WDEP):
        value = jnp.where(depth == i, jnp.float32(BELL[i]), value)
    return value


def ffn_rows(base, mixed, gain_row, wo, wu, wd, normed, hidden, before_up=None, before_down=None):
    half = normed.shape[0] // 2
    total = jnp.zeros((half, normed.shape[1]), jnp.float32)
    for m in range(2):
        rows = slice(m * half, (m + 1) * half)
        mid = base[rows].astype(jnp.float32) + dot(mixed[rows], wo[...])
        normed[rows, :] = rms_scale(mid, gain_row)
        total = total + mid
    if before_up is not None:
        before_up()
    chunk = hidden.shape[1] // 2
    for c in range(2):
        columns = slice(c * chunk, (c + 1) * chunk)
        both = [
            jax.nn.gelu(dot(normed[m * half : (m + 1) * half, :], wu[:, columns]), approximate=True)
            for m in range(2)
        ]
        hidden[:, columns] = (both[0] + both[1]).astype(jnp.bfloat16)
    if before_down is not None:
        before_down()
    return total + dot(hidden[...], wd[...])


def attend(query_ref, key_ref, value_ref, result, place, start, tokens):
    width = query_ref.shape[1]
    low = lax.broadcasted_iota(jnp.int32, (tokens, LANES), 1) < DH
    zero = jnp.zeros((tokens, LANES), jnp.bfloat16)
    one = jnp.ones((tokens, LANES), jnp.bfloat16)
    ones_two = jnp.concatenate([jnp.where(low, one, zero), jnp.where(low, zero, one)], axis=0)
    for pair in range(width // LANES):
        lanes = slice(pair * LANES, (pair + 1) * LANES)
        keys = key_ref[start : start + tokens, lanes]
        values = value_ref[start : start + tokens, lanes]
        keys_two = jnp.concatenate(
            [jnp.where(low, keys, zero), jnp.where(low, zero, keys)], axis=0
        )
        values_two = jnp.concatenate(
            [jnp.where(low, values, zero), jnp.where(low, zero, values)], axis=0
        )
        scores = lax.dot_general(
            query_ref[place : place + tokens, lanes],
            keys_two,
            (((1,), (1,)), ((), ())),
            preferred_element_type=jnp.float32,
        )
        powers = []
        for h in range(2):
            part = scores[:, h * tokens : (h + 1) * tokens]
            top = jnp.max(part, axis=-1, keepdims=True)
            powers.append(jnp.exp((part - top) * (1.0 / DH**0.5)).astype(jnp.bfloat16))
        powers = jnp.concatenate(powers, axis=1)
        both = dot(powers, jnp.concatenate([values_two, ones_two], axis=1))
        result[place : place + tokens, lanes] = (both[:, :LANES] / both[:, LANES:]).astype(
            jnp.bfloat16
        )


def window_kernel(*refs):
    sources, outs, scratch = refs[:13], refs[13:21], refs[21:]
    far_out, rest_mixed, rest_base, rest_scale, wo, wu, wd = outs[:7]
    gain_refs = (scratch[0], scratch[1], outs[7])
    anchor_ref, count_ref, tok, wq, wk, wv, normed, q_all, k_all, v_all, mixed = scratch[2:13]
    ffn_normed, ffn_hidden, sems = scratch[13:]
    slots, tokens, width = sources[5].shape
    rows = slots * tokens
    cells = tokens // WDEP
    targets = (
        anchor_ref,
        count_ref,
        *gain_refs,
        tok.at[0],
        tok.at[1],
        wq,
        wk,
        wv,
        wo,
        wu,
        wd,
    )
    copies = [
        pltpu.make_async_copy(src, dst, sems.at[i])
        for i, (src, dst) in enumerate(zip(sources, targets, strict=True))
    ]
    for i in (2, 3, 5, 6, 7, 0, 1, 4, 8, 9, 10, 11, 12):
        copies[i].start()
    position = lax.axis_index("brick")
    residue = lax.rem(position, WDEP)

    copies[2].wait()
    copies[3].wait()
    for m in range(2):
        copies[5 + m].wait()
        for s in range(slots):
            start = m * rows + s * tokens
            normed[start : start + tokens, :] = rms_scale(
                tok[m, s].astype(jnp.float32), gain_refs[m][...][None, :]
            )
    for i, (weight, result) in enumerate(((wq, q_all), (wk, k_all), (wv, v_all))):
        copies[7 + i].wait()
        for m in range(2):
            half = slice(m * rows, (m + 1) * rows)
            result[half, :] = dot(normed[half, :], weight[...]).astype(jnp.bfloat16)
    for s in range(slots):
        for m in range(2):
            place, start = m * rows + s * tokens, (1 - m) * rows + s * tokens
            attend(q_all, k_all, v_all, mixed, place, start, tokens)
    for i in (0, 1, 4, 10):
        copies[i].wait()

    def picked(rels):
        places, scales = [], []
        for s in range(slots):
            slot = position * slots + s
            factor = jnp.full((1, LANES), count_ref[slot], jnp.int32).astype(jnp.float32) * (
                1.0 / (2.0 * tokens)
            )
            for rel in rels:
                depth = lax.rem((residue ^ rel) + WDEP * NWRAP - anchor_ref[slot], WDEP)
                places.append((s, depth))
                scales.append(factor * bell_at(depth))
        base, chosen = [], []
        for m in range(2):
            for s, depth in places:
                base.append(tok[m, s, pl.ds(pl.multiple_of(depth * cells, cells), cells), :])
                place = pl.multiple_of(m * rows + s * tokens + depth * cells, cells)
                chosen.append(mixed[pl.ds(place, cells), :])
        return scales, jnp.concatenate(base, axis=0), jnp.concatenate(chosen, axis=0)

    scales, base, chosen = picked((2, 3))
    joined = ffn_rows(
        base,
        chosen,
        gain_refs[2][...][None, :],
        wo,
        wu,
        wd,
        ffn_normed,
        ffn_hidden,
        copies[11].wait,
        copies[12].wait,
    )
    for j, scale in enumerate(scales):
        far_out[(j % 2) * slots + j // 2] = (
            joined[j * cells : (j + 1) * cells] * scale[:, :1]
        ).astype(jnp.bfloat16)
    scales, base, chosen = picked((1, 0))
    rest_base[...] = base
    rest_mixed[...] = chosen
    for j, scale in enumerate(scales):
        rest_scale[j * cells : (j + 1) * cells, :] = jnp.broadcast_to(scale, (cells, LANES))


def near_kernel(
    outer,
    tokens,
    anchor_ref,
    anchor_row,
    count_row,
    rest_mixed,
    rest_base,
    rest_scale,
    wo,
    wu,
    wd,
    gain,
    near_out,
    own_out,
    mask_out,
    bound_out,
    ffn_normed,
    ffn_hidden,
):
    slots, cells, width = near_out.shape
    position = lax.axis_index("brick")
    residue = lax.rem(position, WDEP)
    block = lax.div(position, WDEP)
    joined = ffn_rows(
        rest_base[...],
        rest_mixed[...],
        gain[...][None, :],
        wo,
        wu,
        wd,
        ffn_normed,
        ffn_hidden,
    )
    joined = (joined * rest_scale[:, :1]).astype(jnp.bfloat16)
    for s in range(slots):
        near_out[s] = joined[2 * s * cells : (2 * s + 1) * cells]
        own_out[s] = joined[(2 * s + 1) * cells : (2 * s + 2) * cells]
    for rel in range(WDEP):
        for s in range(slots):
            slot = (block * WDEP + (residue ^ rel)) * slots + s
            start = anchor_ref[slot]
            depth = lax.rem(residue + WDEP * NWRAP - start, WDEP)
            step = lax.div(start + depth, WDEP) ^ block
            for k in range(outer):
                row = k * (WDEP * slots) + rel * slots + s
                mask_out[row : row + 1, :] = jnp.full(
                    (1, LANES), jnp.where(step == k, jnp.float32(1), jnp.float32(0)), jnp.float32
                )
    shift = position - anchor_row[...]
    inside = (shift >= 0) & (shift < WDEP)
    centred = shift.astype(jnp.float32) - (WDEP - 1) / 2.0
    spread = WDEP / 4.0
    terms = (
        count_row[...].astype(jnp.float32)
        / (2.0 * tokens)
        * jnp.exp(-centred * centred / (2.0 * spread * spread))
    )
    bound = jnp.maximum(jnp.sum(jnp.where(inside, terms, 0.0), axis=-1, keepdims=True), 1.0)
    bound_out[...] = jnp.broadcast_to(bound, bound_out.shape)


NWRAP = 1 << 20


def in_hbm(array):
    return pltpu.with_memory_space_constraint(array, pltpu.HBM)


def in_vmem(array):
    return pltpu.with_memory_space_constraint(array, pltpu.VMEM)


def limit(mebibytes):
    return pltpu.CompilerParams(vmem_limit_bytes=mebibytes * 1024 * 1024)


def cost(flops, bytes_accessed):
    return pl.CostEstimate(flops=flops, bytes_accessed=bytes_accessed, transcendentals=0)


def far_call(anchor, count, gains, ct_win, pet_win, weights):
    slots, tokens, width = ct_win.shape
    rows = 2 * slots * tokens
    cells = tokens // WDEP
    half = slots * (WDEP // 2) * cells
    rest = pltpu.VMEM((2 * half, width), jnp.bfloat16)
    big = pltpu.VMEM((rows, width), jnp.bfloat16)
    far, *passed = pl.pallas_call(
        window_kernel,
        out_shape=[
            pltpu.VMEM((2 * slots, cells, width), jnp.bfloat16),
            rest,
            rest,
            pltpu.VMEM((half, LANES), jnp.float32),
        ]
        + [pltpu.VMEM(w.shape, w.dtype) for w in weights[3:]]
        + [pltpu.VMEM((width,), jnp.float32)],
        in_specs=[ANY] * 13,
        out_specs=[VMEM] * 8,
        scratch_shapes=[pltpu.VMEM((width,), jnp.float32)] * 2
        + [pltpu.SMEM(anchor.shape, jnp.int32)] * 2
        + [pltpu.VMEM((2, slots, tokens, width), jnp.bfloat16)]
        + [pltpu.VMEM(w.shape, w.dtype) for w in weights[:3]]
        + [big] * 5
        + [rest, pltpu.VMEM((half, weights[4].shape[1]), jnp.bfloat16)]
        + [pltpu.SemaphoreType.DMA((13,))],
        compiler_params=limit(24),
        name="window_far",
    )(*map(in_hbm, (anchor, count, *gains, ct_win, pet_win, *weights)))
    return far, passed


def near_call(outer, slots, tokens, anchor, count, passed):
    width = passed[0].shape[1]
    cells = tokens // WDEP
    half = slots * (WDEP // 2) * cells
    out = pltpu.VMEM((slots, cells, width), jnp.bfloat16)
    hidden = passed[4].shape[1]
    return pl.pallas_call(
        functools.partial(near_kernel, outer, tokens),
        out_shape=[
            out,
            out,
            pltpu.VMEM((outer * WDEP * slots, LANES), jnp.float32),
            pltpu.VMEM((8, LANES), jnp.float32),
        ],
        in_specs=[SMEM] + [VMEM] * 9,
        out_specs=[VMEM] * 4,
        scratch_shapes=[
            pltpu.VMEM((2 * half, width), jnp.bfloat16),
            pltpu.VMEM((half, hidden), jnp.bfloat16),
        ],
        compiler_params=limit(12),
        cost_estimate=cost(12 * half * width * width, 4 * half * width),
        name="window_near",
    )(in_hbm(anchor), in_hbm(anchor[None, :]), in_hbm(count[None, :]), *map(in_vmem, passed))


def gather_kernel(outer, mask_ref, own, near, far, forward, kept, *sent):
    slots, cells, width = own.shape
    blocks = [own[s] for s in range(slots)] + [near[s] for s in range(slots)]
    blocks += [far[s] for s in range(slots)] + [forward[s] for s in range(slots)]
    blocks = [block.astype(jnp.float32) for block in blocks]
    for k in range(outer):
        total = jnp.zeros((cells, width), jnp.float32)
        for j, block in enumerate(blocks):
            row = k * len(blocks) + j
            mask = jnp.concatenate([mask_ref[row : row + 1, :]] * (width // LANES), axis=1)
            total = total + block * mask
        if k == 0:
            kept[...] = total
        else:
            sent[k - 1][...] = total.astype(jnp.bfloat16)


def gather_call(outer, masks, own, near, far, forward):
    slots, cells, width = own.shape
    return pl.pallas_call(
        functools.partial(gather_kernel, outer),
        out_shape=[pltpu.VMEM((cells, width), jnp.float32)]
        + [pltpu.VMEM((cells, width), jnp.bfloat16)] * (outer - 1),
        in_specs=[VMEM] * 5,
        out_specs=[VMEM] * outer,
        compiler_params=limit(8),
        name="plane_sum",
    )(*map(in_vmem, (masks, own, near, far, forward)))


def upconv_kernel(bound, kept, *refs):
    pieces = refs[:-5]
    weight, up_ref, near_ref, far_ref, grid = refs[-5:]
    channels = up_ref.shape[-1]
    numerator = kept[...]
    for piece in pieces:
        numerator = numerator + piece[...].astype(jnp.float32)
    feature = (numerator / bound[:1, :1]).astype(jnp.bfloat16)
    up_rows = dot(feature, weight[...])
    for a in range(2):
        for b in range(2):
            for c in range(2):
                chunk = (a * 2 + b) * 2 + c
                for y in range(PY):
                    grid[a, 2 * y + b, pl.ds(c, PX, stride=2), :] = up_rows[
                        y * PX : (y + 1) * PX, chunk * channels : (chunk + 1) * channels
                    ]
    upsampled = grid[...].astype(jnp.bfloat16)
    up_ref[...] = upsampled
    even = lax.rem(lax.axis_index("brick"), 2) == 0
    active = jnp.maximum(upsampled, jnp.zeros((), jnp.bfloat16))
    near_ref[...] = jnp.where(even, active[1], active[0])
    far_ref[...] = jnp.where(even, active[0], active[1])


def upconv_call(channels, bound, kept, pieces, weight):
    layer = (2 * PY, 2 * PX, channels)
    return pl.pallas_call(
        upconv_kernel,
        out_shape=[
            pltpu.VMEM((2,) + layer, jnp.bfloat16),
            pltpu.VMEM(layer, jnp.bfloat16),
            pltpu.VMEM(layer, jnp.bfloat16),
        ],
        in_specs=[VMEM] * (3 + len(pieces)),
        out_specs=[VMEM] * 3,
        scratch_shapes=[pltpu.VMEM((2,) + layer, jnp.float32)],
        compiler_params=limit(8),
        name="upconv",
    )(*map(in_vmem, (bound, kept, *pieces, weight)))


def fill_patches(layers, padded, patches):
    height, breadth, channels = layers[0].shape
    rows = height * breadth
    padded[...] = jnp.zeros_like(padded)
    for z, layer in enumerate(layers):
        padded[z, 1 : height + 1, 8 : 8 + breadth, :] = layer.astype(jnp.float32)
    for z in range(len(layers)):
        for dx in range(3):
            column = padded[z, :, 7 + dx : 7 + dx + breadth, :].astype(jnp.bfloat16)
            for dy in range(3):
                tap = dy * 3 + dx
                patches[z * rows : (z + 1) * rows, tap * channels : (tap + 1) * channels] = column[
                    dy : dy + height
                ].reshape(rows, channels)


def conv_local_kernel(up_ref, weight, out_ref, padded, patches):
    depth, height, breadth, channels = up_ref.shape
    rows = height * breadth
    span = 9 * channels
    zero = jnp.zeros((), jnp.bfloat16)
    fill_patches([jnp.maximum(up_ref[z], zero) for z in range(depth)], padded, patches)
    out_ref[...] = up_ref[...].reshape(depth * rows, channels).astype(jnp.float32) + dot(
        patches[...], weight[span : 2 * span, :]
    )
    for z in range(depth - 1):
        out_ref[z * rows : (z + 1) * rows, :] += dot(
            patches[(z + 1) * rows : (z + 2) * rows, :], weight[2 * span :, :]
        )
        out_ref[(z + 1) * rows : (z + 2) * rows, :] += dot(
            patches[z * rows : (z + 1) * rows, :], weight[:span, :]
        )


def conv_halo_kernel(part_ref, near_ref, far_ref, weight, out_ref, padded, patches):
    depth, height, breadth, channels = out_ref.shape
    rows = height * breadth
    span = 9 * channels
    even = lax.rem(lax.axis_index("brick"), 2) == 0
    near, far = near_ref[...], far_ref[...]
    fill_patches([jnp.where(even, far, near), jnp.where(even, near, far)], padded, patches)
    for z in range(depth):
        total = part_ref[z * rows : (z + 1) * rows, :]
        if z == 0:
            total = total + dot(patches[:rows, :], weight[:span, :])
        if z == depth - 1:
            total = total + dot(patches[rows:, :], weight[2 * span :, :])
        out_ref[z] = total.astype(jnp.bfloat16).reshape(height, breadth, channels)


def conv_scratch(depth, height, breadth, channels):
    return [
        pltpu.VMEM((depth, height + 2, breadth + 16, channels), jnp.float32),
        pltpu.VMEM((depth * height * breadth, 9 * channels), jnp.bfloat16),
    ]


def conv_local_call(upsampled, weight):
    depth, height, breadth, channels = upsampled.shape
    rows = depth * height * breadth
    return pl.pallas_call(
        conv_local_kernel,
        out_shape=pltpu.VMEM((rows, channels), jnp.float32),
        in_specs=[VMEM] * 2,
        out_specs=VMEM,
        scratch_shapes=conv_scratch(depth, height, breadth, channels),
        compiler_params=limit(8),
        cost_estimate=cost(36 * rows * channels * channels, 12 * rows * channels),
        name="conv_local",
    )(*map(in_vmem, (upsampled, weight)))


def conv_halo_call(shape, part, near, far, weight):
    return pl.pallas_call(
        conv_halo_kernel,
        out_shape=jax.ShapeDtypeStruct(shape, jnp.bfloat16),
        in_specs=[VMEM] * 4,
        out_specs=VMEM,
        scratch_shapes=conv_scratch(2, *shape[1:]),
        compiler_params=limit(8),
        name="conv_halo",
    )(*map(in_vmem, (part, near, far, weight)))


def swap(values, distance, total):
    return lax.ppermute(values, "brick", [(i, i ^ distance) for i in range(total)])


def on_device(
    ct_win,
    pet_win,
    placed_anchor,
    placed_count,
    norm_ct,
    norm_pet,
    norm_ffn,
    w_query,
    w_key,
    w_value,
    w_out,
    w_up,
    w_down,
    w_upconv,
    w_conv,
):
    slots, tokens, _ = ct_win.shape
    channels = w_conv.shape[1]
    total = lax.axis_size("brick")
    outer = total // WDEP
    far, passed = far_call(
        placed_anchor,
        placed_count,
        (norm_ct, norm_pet, norm_ffn),
        ct_win,
        pet_win,
        (w_query, w_key, w_value, w_out, w_up, w_down),
    )
    far = swap(far, 2, total)
    near, own, masks, bound = near_call(outer, slots, tokens, placed_anchor, placed_count, passed)
    near = swap(near, 1, total)
    forward = swap(far[slots:], 1, total)
    kept, *sent = gather_call(outer, masks, own, near, far, forward)
    pieces = [swap(sent[k - 1], k * WDEP, total) for k in range(outer - 1, 0, -1)]
    upsampled, near, far = upconv_call(channels, bound, kept, pieces, w_upconv)
    pairs = [(i, i + 1) for i in range(1, total - 1, 2)]
    far = lax.ppermute(far, "brick", pairs + [(j, i) for i, j in pairs])
    part = conv_local_call(upsampled, w_conv)
    near, part = lax.optimization_barrier((near, part))
    near = swap(near, 1, total)
    return conv_halo_call(upsampled.shape, part, near, far, w_conv)


def solution(mesh):
    return jax.shard_map(
        on_device,
        mesh=mesh,
        in_specs=(
            P(("groups", "brick"), None, None),
            P(("groups", "brick"), None, None),
            P("groups"),
            P("groups"),
            P(),
            P(),
            P(),
            P(),
            P(),
            P(),
            P(),
            P(),
            P(),
            P(),
            P(),
        ),
        out_specs=P(("groups", "brick"), None, None, None),
        check_vma=False,
    )
```

time: 34.7 us -> 32.3 us (0.931)
  the two profiles are of different devices: /device:TPU:3 before, /device:TPU:0 now
where the time goes in v4:
time: 32.3 us; the launch traced here: 32.1 us
  Pallas kernels  12 us (37%)
  starting transfers between devices  11.3 us (35%)
  waiting for transfers between devices  8.77 us (27%)
    ppermute x7, starting transfers between devices, swap(): lax.ppermute(values, 'brick', [(i, i ^ distance) for i in range(total)])  10.6 us
    ppermute x7, waiting for transfers between devices, swap(): lax.ppermute(values, 'brick', [(i, i ^ distance) for i in range(total)])  8.76 us
    pallas_call x1, Pallas kernels, far_call(): pl.pallas_call(window_kernel, out_shape=[pltpu.VMEM((2 * slots, cells, wi...  7.34 us
    pallas_call x1, Pallas kernels, near_call(): pl.pallas_call(functools.partial(near_kernel, outer, tokens), out_shape=[...  2.52 us
    pallas_call x1, Pallas kernels, conv_halo_call(): pl.pallas_call(conv_halo_kernel, out_shape=jax.ShapeDtypeStruct(shape, jn...  0.97 us
    ppermute x1, starting transfers between devices, on_device(): far = lax.ppermute(far, 'brick', pairs + [(j, i) for i, j in pairs])  0.66 us
  transfers between devices with their start and end apart: 8, of which 5 were waited for; matrix products, arithmetic and copies ran while one was open for 0% of the time, Pallas kernels for 9%

profile of v4, /device:TPU:0, one launch (start us, length us, event | category | flops | bytes accessed | tf_op | source)
XLA Modules:
  0.0 32.1 jit_solution(4918978428275953784)
XLA Ops:
  0.0 7.3 %window_far.1 = (bf16[4,32,768]{2,1,0:T(8,128)(2,1)S(1)}, bf16[256,768]{1,0:T(8,128)(2,1)S(1)}, bf16[256,768]{1,0:T(8,128)(2,1)S(1)}, f32[128,128]{1,0:T(8,128)S...) custom-call(s32[32]{0:T(128)} %anchor_ref.1, ...), custom_call_target="tpu_custom_call" | custom-call | tf_op jit(solution)/shard_map/window_far/pallas_call | solution.py:284
  7.3 3.0 %collective-permute-start.1 = (bf16[4,32,768]{2,1,0:T(8,128)(2,1)S(1)}, bf16[4,32,768]{2,1,0:T(8,128)(2,1)S(1)}, u32[]{:S(2)}, u32[]{:S(2)}) collective-permute-start(bf16[4,32,768]{2,1,0:T(8,128)(2,1)S(1)} %get-tuple-element.37), channel_id=1, source_target_pairs={{0,2},{1,3},{2,0},{3,1},{4,6},{5,7},{6,4},{7,5},{8,10},{9,11},{10,... | collective-permute-start | bytes 589832 | tf_op jit(solution)/shard_map/ppermute | solution.py:492
  10.4 2.5 %window_near.1 = (bf16[2,32,768]{2,1,0:T(8,128)(2,1)S(1)}, bf16[2,32,768]{2,1,0:T(8,128)(2,1)S(1)}, f32[32,128]{1,0:T(8,128)S(1)}, f32[8,128]{1,0:T(8,128)S(1)}) custom-call(s32[32]{0:T(128)} %anchor_ref.1, s32[1,32]{1,0:T(1,128)} %bitcast.2, s32[1,32]{1,0:T(1,128)} %bitcast.3, bf16[256,768]{1,0:T(8,128)(2,1)S(1)} %get-tuple-element.26.rest_mixed, ...), custom_call_target="tpu_custom_call" | custom-call | flops 905969664 | bytes 393216 | tf_op jit(solution)/shard_map/window_near/pallas_call | solution.py:315
  12.9 0.0 copy-start
  12.9 0.1 collective-permute-start
  13.0 2.3 %collective-permute-done.1.far = bf16[4,32,768]{2,1,0:T(8,128)(2,1)S(1)} collective-permute-done((bf16[4,32,768]{2,1,0:T(8,128)(2,1)S(1)}, bf16[4,32,768]{2,1,0:T(8,128)(2,1)S(1)}, u32[]{:S(2)}, u32[]{:S(2)}) %collective-permute-start.1) | collective-permute-done | bytes 196640 | tf_op jit(solution)/shard_map/ppermute | solution.py:492
  15.3 0.1 collective-permute-start.2
  15.3 0.0 collective-permute-done.near
  15.4 1.3 %collective-permute-done.2.forward = bf16[2,32,768]{2,1,0:T(8,128)(2,1)S(1)} collective-permute-done((bf16[2,32,768]{2,1,0:T(8,128)(2,1)S(1)}, bf16[2,32,768]{2,1,0:T(8,128)(2,1)S(1)}, u32[]{:S(2)}, u32[]{:S(2)}) %collective-permute-start.2) | collective-permute-done | bytes 98336 | tf_op jit(solution)/shard_map/ppermute | solution.py:492
  16.6 0.2 plane_sum.1
  16.9 3.9 %collective-permute-start.3 = (bf16[32,768]{1,0:T(8,128)(2,1)S(1)}, bf16[32,768]{1,0:T(8,128)(2,1)S(1)}, u32[]{:S(2)}, u32[]{:S(2)}) collective-permute-start(bf16[32,768]{1,0:T(8,128)(2,1)S(1)} %get-tuple-element.39), channel_id=1, source_target_pairs={{0,12},{1,13},{2,14},{3,15},{4,8},{5,9},{6,10},{7,11},{8,4},{9,5},... | collective-permute-start | bytes 147464 | tf_op jit(solution)/shard_map/ppermute | solution.py:492
  20.8 0.0 collective-permute-start.4
  20.8 0.6 %collective-permute-start.5 = (bf16[32,768]{1,0:T(8,128)(2,1)S(1)}, bf16[32,768]{1,0:T(8,128)(2,1)S(1)}, u32[]{:S(2)}, u32[]{:S(2)}) collective-permute-start(bf16[32,768]{1,0:T(8,128)(2,1)S(1)} %get-tuple-element.41), channel_id=1, source_target_pairs={{0,4},{1,5},{2,6},{3,7},{4,0},{5,1},{6,2},{7,3},{8,12},{9,13},{10,... | collective-permute-start | bytes 147464 | tf_op jit(solution)/shard_map/ppermute | solution.py:492
  21.4 1.5 %collective-permute-done.3.refs_0_ = bf16[32,768]{1,0:T(8,128)(2,1)S(1)} collective-permute-done((bf16[32,768]{1,0:T(8,128)(2,1)S(1)}, bf16[32,768]{1,0:T(8,128)(2,1)S(1)}, u32[]{:S(2)}, u32[]{:S(2)}) %collective-permute-start.3) | collective-permute-done | bytes 49184 | tf_op jit(solution)/shard_map/ppermute | solution.py:492
  22.9 2.8 %collective-permute-done.4.refs_1_ = bf16[32,768]{1,0:T(8,128)(2,1)S(1)} collective-permute-done((bf16[32,768]{1,0:T(8,128)(2,1)S(1)}, bf16[32,768]{1,0:T(8,128)(2,1)S(1)}, u32[]{:S(2)}, u32[]{:S(2)}) %collective-permute-start.4) | collective-permute-done | bytes 49184 | tf_op jit(solution)/shard_map/ppermute | solution.py:492
  25.8 0.0 collective-permute-done.5.refs_2_
  25.8 0.4 %upconv.1 = (bf16[2,8,16,128]{3,2,1,0:T(8,128)(2,1)S(1)}, bf16[8,16,128]{2,1,0:T(8,128)(2,1)S(1)}, bf16[8,16,128]{2,1,0:T(8,128)(2,1)S(1)}) custom-call(f32[8,128]{1,0:T(8,128)S(1)} %get-tuple-element.33.bound, f32[32,768]{1,0:T(8,128)S(1)} %get-tuple-element.38.kept, bf16[32,768]{1,0:T(8,128)(2,1)S(1)} %collective-permute-done.3.refs_0_, ...), custom_call_target="tpu_custom_call" | custom-call | tf_op jit(solution)/shard_map/upconv/pallas_call | solution.py:392
  26.2 0.7 %collective-permute-start.7 = (bf16[8,16,128]{2,1,0:T(8,128)(2,1)S(1)}, bf16[8,16,128]{2,1,0:T(8,128)(2,1)S(1)}, u32[]{:S(2)}, u32[]{:S(2)}) collective-permute-start(bf16[8,16,128]{2,1,0:T(8,128)(2,1)S(1)} %get-tuple-element.46), channel_id=1, source_target_pairs={{1,2},{3,4},{5,6},{7,8},{9,10},{11,12},{13,14},{2,1},{4,3},{6,5},{... | collective-permute-start | bytes 98312 | tf_op jit(solution)/shard_map/ppermute | solution.py:532
  26.9 0.0 copy-done
  26.9 0.5 %conv_local.1.part_ref = f32[256,128]{1,0:T(8,128)S(1)} custom-call(bf16[2,8,16,128]{3,2,1,0:T(8,128)(2,1)S(1)} %get-tuple-element.43.up_ref, bf16[3456,128]{1,0:T(8,128)(2,1)S(1)} %copy-done), custom_call_target="tpu_custom_call" | custom-call | flops 150994944 | bytes 393216 | tf_op jit(solution)/shard_map/conv_local/pallas_call | solution.py:467
  27.4 2.9 %collective-permute-start.6 = (bf16[8,16,128]{2,1,0:T(8,128)(2,1)S(1)}, bf16[8,16,128]{2,1,0:T(8,128)(2,1)S(1)}, u32[]{:S(2)}, u32[]{:S(2)}) collective-permute-start(bf16[8,16,128]{2,1,0:T(8,128)(2,1)S(1)} %get-tuple-element.45), channel_id=1, source_target_pairs={{0,1},{1,0},{2,3},{3,2},{4,5},{5,4},{6,7},{7,6},{8,9},{9,8},{10,11... | collective-permute-start | bytes 98312 | tf_op jit(solution)/shard_map/ppermute | solution.py:492
  30.3 0.0 collective-permute-done.7.far_ref
  30.3 0.9 %collective-permute-done.6.near_ref = bf16[8,16,128]{2,1,0:T(8,128)(2,1)S(1)} collective-permute-done((bf16[8,16,128]{2,1,0:T(8,128)(2,1)S(1)}, bf16[8,16,128]{2,1,0:T(8,128)(2,1)S(1)}, u32[]{:S(2)}, u32[]{:S(2)}) %collective-permute-start.6) | collective-permute-done | bytes 32800 | tf_op jit(solution)/shard_map/ppermute | solution.py:492
  31.2 1.0 %conv_halo.1 = bf16[2,8,16,128]{3,2,1,0:T(8,128)(2,1)} custom-call(f32[256,128]{1,0:T(8,128)S(1)} %conv_local.1.part_ref, bf16[8,16,128]{2,1,0:T(8,128)(2,1)S(1)} %collective-permute-done.6.near_ref, bf16[8,16,128]{2,1,0:T(8,128)(2,1)S(1)} %collective-permute-done.7.far_ref, bf16[3456,128]{1,0:T(8,128)(2,1)S(1)} %copy-done), custom_call_target="tpu_custom_call" | custom-call | tf_op jit(solution)/shard_map/conv_halo/pallas_call | solution.py:480
  (3 shorter events, 0.0 us)
Async XLA Ops:
  7.3 7.9 %collective-permute-start.1 = (bf16[4,32,768]{2,1,0:T(8,128)(2,1)S(1)}, bf16[4,32,768]{2,1,0:T(8,128)(2,1)S(1)}, u32[]{:S(2)}, u32[]{:S(2)}) collective-permute-start(bf16[4,32,768]{2,1,0:T(8,128)(2,1)S(1)} %get-tuple-element.37), channel_id=1, source_target_pairs={{0,2},{1,3},{2,0},{3,1},{4,6},{5,7},{6,4},{7,5},{8,10},{9,11},{10,... | collective-permute-start | bytes 589832 | tf_op jit(solution)/shard_map/ppermute | solution.py:492
  10.4 15.4 %copy-start.1 = (bf16[768,1024]{1,0:T(8,128)(2,1)S(1)}, bf16[768,1024]{1,0:T(8,128)(2,1)}, u32[]{:S(2)}) copy-start(bf16[768,1024]{1,0:T(8,128)(2,1)} %refs_3_.3) | copy-start | bytes 4718596
  12.9 14.0 %copy-start = (bf16[3456,128]{1,0:T(8,128)(2,1)S(1)}, bf16[3456,128]{1,0:T(8,128)(2,1)}, u32[]{:S(2)}) copy-start(bf16[3456,128]{1,0:T(8,128)(2,1)} %weight.3) | copy-start | bytes 2654212
  12.9 2.5 %collective-permute-start = (bf16[2,32,768]{2,1,0:T(8,128)(2,1)S(1)}, bf16[2,32,768]{2,1,0:T(8,128)(2,1)S(1)}, u32[]{:S(2)}, u32[]{:S(2)}) collective-permute-start(bf16[2,32,768]{2,1,0:T(8,128)(2,1)S(1)} %get-tuple-element.36), channel_id=1, source_target_pairs={{0,1},{1,0},{2,3},{3,2},{4,5},{5,4},{6,7},{7,6},{8,9},{9,8},{10,11... | collective-permute-start | bytes 294920 | tf_op jit(solution)/shard_map/ppermute | solution.py:492
  15.3 1.4 %collective-permute-start.2 = (bf16[2,32,768]{2,1,0:T(8,128)(2,1)S(1)}, bf16[2,32,768]{2,1,0:T(8,128)(2,1)S(1)}, u32[]{:S(2)}, u32[]{:S(2)}) collective-permute-start(bf16[2,32,768]{2,1,0:T(8,128)(2,1)S(1)} %slice.4), channel_id=1, source_target_pairs={{0,1},{1,0},{2,3},{3,2},{4,5},{5,4},{6,7},{7,6},{8,9},{9,8},{10,11... | collective-permute-start | bytes 294920 | tf_op jit(solution)/shard_map/ppermute | solution.py:492
  16.9 6.1 %collective-permute-start.3 = (bf16[32,768]{1,0:T(8,128)(2,1)S(1)}, bf16[32,768]{1,0:T(8,128)(2,1)S(1)}, u32[]{:S(2)}, u32[]{:S(2)}) collective-permute-start(bf16[32,768]{1,0:T(8,128)(2,1)S(1)} %get-tuple-element.39), channel_id=1, source_target_pairs={{0,12},{1,13},{2,14},{3,15},{4,8},{5,9},{6,10},{7,11},{8,4},{9,5},... | collective-permute-start | bytes 147464 | tf_op jit(solution)/shard_map/ppermute | solution.py:492
  20.8 5.0 %collective-permute-start.4 = (bf16[32,768]{1,0:T(8,128)(2,1)S(1)}, bf16[32,768]{1,0:T(8,128)(2,1)S(1)}, u32[]{:S(2)}, u32[]{:S(2)}) collective-permute-start(bf16[32,768]{1,0:T(8,128)(2,1)S(1)} %get-tuple-element.40), channel_id=1, source_target_pairs={{0,8},{1,9},{2,10},{3,11},{4,12},{5,13},{6,14},{7,15},{8,0},{9,1},... | collective-permute-start | bytes 147464 | tf_op jit(solution)/shard_map/ppermute | solution.py:492
  20.8 5.0 %collective-permute-start.5 = (bf16[32,768]{1,0:T(8,128)(2,1)S(1)}, bf16[32,768]{1,0:T(8,128)(2,1)S(1)}, u32[]{:S(2)}, u32[]{:S(2)}) collective-permute-start(bf16[32,768]{1,0:T(8,128)(2,1)S(1)} %get-tuple-element.41), channel_id=1, source_target_pairs={{0,4},{1,5},{2,6},{3,7},{4,0},{5,1},{6,2},{7,3},{8,12},{9,13},{10,... | collective-permute-start | bytes 147464 | tf_op jit(solution)/shard_map/ppermute | solution.py:492
  26.2 4.1 %collective-permute-start.7 = (bf16[8,16,128]{2,1,0:T(8,128)(2,1)S(1)}, bf16[8,16,128]{2,1,0:T(8,128)(2,1)S(1)}, u32[]{:S(2)}, u32[]{:S(2)}) collective-permute-start(bf16[8,16,128]{2,1,0:T(8,128)(2,1)S(1)} %get-tuple-element.46), channel_id=1, source_target_pairs={{1,2},{3,4},{5,6},{7,8},{9,10},{11,12},{13,14},{2,1},{4,3},{6,5},{... | collective-permute-start | bytes 98312 | tf_op jit(solution)/shard_map/ppermute | solution.py:532
  27.4 3.8 %collective-permute-start.6 = (bf16[8,16,128]{2,1,0:T(8,128)(2,1)S(1)}, bf16[8,16,128]{2,1,0:T(8,128)(2,1)S(1)}, u32[]{:S(2)}, u32[]{:S(2)}) collective-permute-start(bf16[8,16,128]{2,1,0:T(8,128)(2,1)S(1)} %get-tuple-element.45), channel_id=1, source_target_pairs={{0,1},{1,0},{2,3},{3,2},{4,5},{5,4},{6,7},{7,6},{8,9},{9,8},{10,11... | collective-permute-start | bytes 98312 | tf_op jit(solution)/shard_map/ppermute | solution.py:492

commit v5 on v4

--- a/solution.py
+++ b/solution.py
@@ -99,9 +99,9 @@
 
 
 def window_kernel(*refs):
-    sources, outs, scratch = refs[:13], refs[13:21], refs[21:]
-    far_out, rest_mixed, rest_base, rest_scale, wo, wu, wd = outs[:7]
-    gain_refs = (scratch[0], scratch[1], outs[7])
+    sources, outs, scratch = refs[:13], refs[13:22], refs[22:]
+    passing_out, far_out, rest_mixed, rest_base, rest_scale, wo, wu, wd = outs[:8]
+    gain_refs = (scratch[0], scratch[1], outs[8])
     anchor_ref, count_ref, tok, wq, wk, wv, normed, q_all, k_all, v_all, mixed = scratch[2:13]
     ffn_normed, ffn_hidden, sems = scratch[13:]
     slots, tokens, width = sources[5].shape
@@ -183,9 +183,8 @@
         copies[12].wait,
     )
     for j, scale in enumerate(scales):
-        far_out[(j % 2) * slots + j // 2] = (
-            joined[j * cells : (j + 1) * cells] * scale[:, :1]
-        ).astype(jnp.bfloat16)
+        out = (far_out, passing_out)[j % 2]
+        out[j // 2] = (joined[j * cells : (j + 1) * cells] * scale[:, :1]).astype(jnp.bfloat16)
     scales, base, chosen = picked((1, 0))
     rest_base[...] = base
     rest_mixed[...] = chosen
@@ -281,10 +280,12 @@
     half = slots * (WDEP // 2) * cells
     rest = pltpu.VMEM((2 * half, width), jnp.bfloat16)
     big = pltpu.VMEM((rows, width), jnp.bfloat16)
-    far, *passed = pl.pallas_call(
+    out = pltpu.VMEM((slots, cells, width), jnp.bfloat16)
+    passing, far, *passed = pl.pallas_call(
         window_kernel,
         out_shape=[
-            pltpu.VMEM((2 * slots, cells, width), jnp.bfloat16),
+            out,
+            out,
             rest,
             rest,
             pltpu.VMEM((half, LANES), jnp.float32),
@@ -292,7 +293,7 @@
         + [pltpu.VMEM(w.shape, w.dtype) for w in weights[3:]]
         + [pltpu.VMEM((width,), jnp.float32)],
         in_specs=[ANY] * 13,
-        out_specs=[VMEM] * 8,
+        out_specs=[VMEM] * 9,
         scratch_shapes=[pltpu.VMEM((width,), jnp.float32)] * 2
         + [pltpu.SMEM(anchor.shape, jnp.int32)] * 2
         + [pltpu.VMEM((2, slots, tokens, width), jnp.bfloat16)]
@@ -303,7 +304,7 @@
         compiler_params=limit(24),
         name="window_far",
     )(*map(in_hbm, (anchor, count, *gains, ct_win, pet_win, *weights)))
-    return far, passed
+    return passing, far, passed
 
 
 def near_call(outer, slots, tokens, anchor, count, passed):
@@ -513,7 +514,7 @@
     channels = w_conv.shape[1]
     total = lax.axis_size("brick")
     outer = total // WDEP
-    far, passed = far_call(
+    passing, far, passed = far_call(
         placed_anchor,
         placed_count,
         (norm_ct, norm_pet, norm_ffn),
@@ -522,10 +523,11 @@
         (w_query, w_key, w_value, w_out, w_up, w_down),
     )
     far = swap(far, 2, total)
+    passing = swap(passing, 3, total)
     near, own, masks, bound = near_call(outer, slots, tokens, placed_anchor, placed_count, passed)
+    near, far = lax.optimization_barrier((near, far))
     near = swap(near, 1, total)
-    forward = swap(far[slots:], 1, total)
-    kept, *sent = gather_call(outer, masks, own, near, far, forward)
+    kept, *sent = gather_call(outer, masks, own, near, far, passing)
     pieces = [swap(sent[k - 1], k * WDEP, total) for k in range(outer - 1, 0, -1)]
     upsampled, near, far = upconv_call(channels, bound, kept, pieces, w_upconv)
     pairs = [(i, i + 1) for i in range(1, total - 1, 2)]

time: 32.3 us -> 31.2 us (0.966)
  waiting for transfers between devices: 8.77 us -> 7.56 us
    ppermute x7, waiting for transfers between devices: 8.76 us -> 7.56 us  [swap(): lax.ppermute(values, 'brick', [(i, i ^ distance) for i in range(total)])]
  transfers between devices with their start and end apart: 8 -> 8, of which waited for: 5 -> 5; matrix products, arithmetic and copies ran while one was open for 0% -> 0% of each run, Pallas kernels for 9% -> 10%
where the time goes in v5:
time: 31.2 us; the launch traced here: 31.1 us
  Pallas kernels  12 us (38%)
  starting transfers between devices  11.4 us (37%)
  waiting for transfers between devices  7.56 us (24%)
    ppermute x7, starting transfers between devices, swap(): lax.ppermute(values, 'brick', [(i, i ^ distance) for i in range(total)])  10.8 us
    ppermute x7, waiting for transfers between devices, swap(): lax.ppermute(values, 'brick', [(i, i ^ distance) for i in range(total)])  7.56 us
    pallas_call x1, Pallas kernels, far_call(): pl.pallas_call(window_kernel, out_shape=[out, out, rest, rest, pltpu.VMEM...  7.34 us
    pallas_call x1, Pallas kernels, near_call(): pl.pallas_call(functools.partial(near_kernel, outer, tokens), out_shape=[...  2.52 us
    pallas_call x1, Pallas kernels, conv_halo_call(): pl.pallas_call(conv_halo_kernel, out_shape=jax.ShapeDtypeStruct(shape, jn...  0.97 us
    ppermute x1, starting transfers between devices, on_device(): far = lax.ppermute(far, 'brick', pairs + [(j, i) for i, j in pairs])  0.66 us
  transfers between devices with their start and end apart: 8, of which 5 were waited for; matrix products, arithmetic and copies ran while one was open for 0% of the time, Pallas kernels for 10%

profile of v5, /device:TPU:0, one launch (start us, length us, event | category | flops | bytes accessed | tf_op | source)
XLA Modules:
  0.0 31.1 jit_solution(4211555924589217310)
XLA Ops:
  0.0 7.3 %window_far.1 = (bf16[2,32,768]{2,1,0:T(8,128)(2,1)S(1)}, bf16[2,32,768]{2,1,0:T(8,128)(2,1)S(1)}, bf16[256,768]{1,0:T(8,128)(2,1)S(1)}, bf16[256,768]{1,0:T(8,1...) custom-call(s32[32]{0:T(128)} %anchor_ref.1, ...), custom_call_target="tpu_custom_call" | custom-call | tf_op jit(solution)/shard_map/window_far/pallas_call | solution.py:284
  7.3 3.0 %collective-permute-start = (bf16[2,32,768]{2,1,0:T(8,128)(2,1)S(1)}, bf16[2,32,768]{2,1,0:T(8,128)(2,1)S(1)}, u32[]{:S(2)}, u32[]{:S(2)}) collective-permute-start(bf16[2,32,768]{2,1,0:T(8,128)(2,1)S(1)} %get-tuple-element.40), channel_id=1, source_target_pairs={{0,2},{1,3},{2,0},{3,1},{4,6},{5,7},{6,4},{7,5},{8,10},{9,11},{10,... | collective-permute-start | bytes 294920 | tf_op jit(solution)/shard_map/ppermute | solution.py:493
  10.4 0.0 collective-permute-start.2
  10.4 2.5 %window_near.1 = (bf16[2,32,768]{2,1,0:T(8,128)(2,1)S(1)}, bf16[2,32,768]{2,1,0:T(8,128)(2,1)S(1)}, f32[32,128]{1,0:T(8,128)S(1)}, f32[8,128]{1,0:T(8,128)S(1)}) custom-call(s32[32]{0:T(128)} %anchor_ref.1, s32[1,32]{1,0:T(1,128)} %bitcast.2, s32[1,32]{1,0:T(1,128)} %bitcast.3, bf16[256,768]{1,0:T(8,128)(2,1)S(1)} %get-tuple-element.29.rest_mixed, ...), custom_call_target="tpu_custom_call" | custom-call | flops 905969664 | bytes 393216 | tf_op jit(solution)/shard_map/window_near/pallas_call | solution.py:316
  12.9 0.0 copy-start
  12.9 0.6 %collective-permute-done.far = bf16[2,32,768]{2,1,0:T(8,128)(2,1)S(1)} collective-permute-done((bf16[2,32,768]{2,1,0:T(8,128)(2,1)S(1)}, bf16[2,32,768]{2,1,0:T(8,128)(2,1)S(1)}, u32[]{:S(2)}, u32[]{:S(2)}) %collective-permute-start) | collective-permute-done | bytes 98336 | tf_op jit(solution)/shard_map/ppermute | solution.py:493
  13.5 0.0 collective-permute-start.1
  13.5 1.8 %collective-permute-done.2.forward = bf16[2,32,768]{2,1,0:T(8,128)(2,1)S(1)} collective-permute-done((bf16[2,32,768]{2,1,0:T(8,128)(2,1)S(1)}, bf16[2,32,768]{2,1,0:T(8,128)(2,1)S(1)}, u32[]{:S(2)}, u32[]{:S(2)}) %collective-permute-start.2) | collective-permute-done | bytes 98336 | tf_op jit(solution)/shard_map/ppermute | solution.py:493
  15.3 0.0 collective-permute-done.1.near
  15.3 0.2 plane_sum.1
  15.5 3.8 %collective-permute-start.3 = (bf16[32,768]{1,0:T(8,128)(2,1)S(1)}, bf16[32,768]{1,0:T(8,128)(2,1)S(1)}, u32[]{:S(2)}, u32[]{:S(2)}) collective-permute-start(bf16[32,768]{1,0:T(8,128)(2,1)S(1)} %get-tuple-element.45), channel_id=1, source_target_pairs={{0,12},{1,13},{2,14},{3,15},{4,8},{5,9},{6,10},{7,11},{8,4},{9,5},... | collective-permute-start | bytes 147464 | tf_op jit(solution)/shard_map/ppermute | solution.py:493
  19.3 0.0 collective-permute-start.4
  19.3 0.6 %collective-permute-start.5 = (bf16[32,768]{1,0:T(8,128)(2,1)S(1)}, bf16[32,768]{1,0:T(8,128)(2,1)S(1)}, u32[]{:S(2)}, u32[]{:S(2)}) collective-permute-start(bf16[32,768]{1,0:T(8,128)(2,1)S(1)} %get-tuple-element.47), channel_id=1, source_target_pairs={{0,4},{1,5},{2,6},{3,7},{4,0},{5,1},{6,2},{7,3},{8,12},{9,13},{10,... | collective-permute-start | bytes 147464 | tf_op jit(solution)/shard_map/ppermute | solution.py:493
  20.0 1.5 %collective-permute-done.3.refs_0_ = bf16[32,768]{1,0:T(8,128)(2,1)S(1)} collective-permute-done((bf16[32,768]{1,0:T(8,128)(2,1)S(1)}, bf16[32,768]{1,0:T(8,128)(2,1)S(1)}, u32[]{:S(2)}, u32[]{:S(2)}) %collective-permute-start.3) | collective-permute-done | bytes 49184 | tf_op jit(solution)/shard_map/ppermute | solution.py:493
  21.5 2.8 %collective-permute-done.4.refs_1_ = bf16[32,768]{1,0:T(8,128)(2,1)S(1)} collective-permute-done((bf16[32,768]{1,0:T(8,128)(2,1)S(1)}, bf16[32,768]{1,0:T(8,128)(2,1)S(1)}, u32[]{:S(2)}, u32[]{:S(2)}) %collective-permute-start.4) | collective-permute-done | bytes 49184 | tf_op jit(solution)/shard_map/ppermute | solution.py:493
  24.3 0.0 collective-permute-done.5.refs_2_
  24.3 0.0 copy-done.1
  24.3 0.4 %upconv.1 = (bf16[2,8,16,128]{3,2,1,0:T(8,128)(2,1)S(1)}, bf16[8,16,128]{2,1,0:T(8,128)(2,1)S(1)}, bf16[8,16,128]{2,1,0:T(8,128)(2,1)S(1)}) custom-call(f32[8,128]{1,0:T(8,128)S(1)} %get-tuple-element.36.bound, f32[32,768]{1,0:T(8,128)S(1)} %get-tuple-element.44.kept, bf16[32,768]{1,0:T(8,128)(2,1)S(1)} %collective-permute-done.3.refs_0_, ...), custom_call_target="tpu_custom_call" | custom-call | tf_op jit(solution)/shard_map/upconv/pallas_call | solution.py:393
  24.7 0.7 %collective-permute-start.7 = (bf16[8,16,128]{2,1,0:T(8,128)(2,1)S(1)}, bf16[8,16,128]{2,1,0:T(8,128)(2,1)S(1)}, u32[]{:S(2)}, u32[]{:S(2)}) collective-permute-start(bf16[8,16,128]{2,1,0:T(8,128)(2,1)S(1)} %get-tuple-element.52), channel_id=1, source_target_pairs={{1,2},{3,4},{5,6},{7,8},{9,10},{11,12},{13,14},{2,1},{4,3},{6,5},{... | collective-permute-start | bytes 98312 | tf_op jit(solution)/shard_map/ppermute | solution.py:534
  25.4 0.5 %conv_local.1.part_ref = f32[256,128]{1,0:T(8,128)S(1)} custom-call(bf16[2,8,16,128]{3,2,1,0:T(8,128)(2,1)S(1)} %get-tuple-element.49.up_ref, bf16[3456,128]{1,0:T(8,128)(2,1)S(1)} %copy-done), custom_call_target="tpu_custom_call" | custom-call | flops 150994944 | bytes 393216 | tf_op jit(solution)/shard_map/conv_local/pallas_call | solution.py:468
  25.9 3.3 %collective-permute-start.6 = (bf16[8,16,128]{2,1,0:T(8,128)(2,1)S(1)}, bf16[8,16,128]{2,1,0:T(8,128)(2,1)S(1)}, u32[]{:S(2)}, u32[]{:S(2)}) collective-permute-start(bf16[8,16,128]{2,1,0:T(8,128)(2,1)S(1)} %get-tuple-element.51), channel_id=1, source_target_pairs={{0,1},{1,0},{2,3},{3,2},{4,5},{5,4},{6,7},{7,6},{8,9},{9,8},{10,11... | collective-permute-start | bytes 98312 | tf_op jit(solution)/shard_map/ppermute | solution.py:493
  29.2 0.0 collective-permute-done.7.far_ref
  29.2 0.9 %collective-permute-done.6.near_ref = bf16[8,16,128]{2,1,0:T(8,128)(2,1)S(1)} collective-permute-done((bf16[8,16,128]{2,1,0:T(8,128)(2,1)S(1)}, bf16[8,16,128]{2,1,0:T(8,128)(2,1)S(1)}, u32[]{:S(2)}, u32[]{:S(2)}) %collective-permute-start.6) | collective-permute-done | bytes 32800 | tf_op jit(solution)/shard_map/ppermute | solution.py:493
  30.1 1.0 %conv_halo.1 = bf16[2,8,16,128]{3,2,1,0:T(8,128)(2,1)} custom-call(f32[256,128]{1,0:T(8,128)S(1)} %conv_local.1.part_ref, bf16[8,16,128]{2,1,0:T(8,128)(2,1)S(1)} %collective-permute-done.6.near_ref, bf16[8,16,128]{2,1,0:T(8,128)(2,1)S(1)} %collective-permute-done.7.far_ref, bf16[3456,128]{1,0:T(8,128)(2,1)S(1)} %copy-done), custom_call_target="tpu_custom_call" | custom-call | tf_op jit(solution)/shard_map/conv_halo/pallas_call | solution.py:481
  (2 shorter events, 0.0 us)
Async XLA Ops:
  7.3 6.1 %collective-permute-start = (bf16[2,32,768]{2,1,0:T(8,128)(2,1)S(1)}, bf16[2,32,768]{2,1,0:T(8,128)(2,1)S(1)}, u32[]{:S(2)}, u32[]{:S(2)}) collective-permute-start(bf16[2,32,768]{2,1,0:T(8,128)(2,1)S(1)} %get-tuple-element.40), channel_id=1, source_target_pairs={{0,2},{1,3},{2,0},{3,1},{4,6},{5,7},{6,4},{7,5},{8,10},{9,11},{10,... | collective-permute-start | bytes 294920 | tf_op jit(solution)/shard_map/ppermute | solution.py:493
  10.4 4.9 %collective-permute-start.2 = (bf16[2,32,768]{2,1,0:T(8,128)(2,1)S(1)}, bf16[2,32,768]{2,1,0:T(8,128)(2,1)S(1)}, u32[]{:S(2)}, u32[]{:S(2)}) collective-permute-start(bf16[2,32,768]{2,1,0:T(8,128)(2,1)S(1)} %get-tuple-element.43), channel_id=1, source_target_pairs={{0,3},{1,2},{2,1},{3,0},{4,7},{5,6},{6,5},{7,4},{8,11},{9,10},{10,... | collective-permute-start | bytes 294920 | tf_op jit(solution)/shard_map/ppermute | solution.py:493
  10.4 14.0 %copy-start.1 = (bf16[768,1024]{1,0:T(8,128)(2,1)S(1)}, bf16[768,1024]{1,0:T(8,128)(2,1)}, u32[]{:S(2)}) copy-start(bf16[768,1024]{1,0:T(8,128)(2,1)} %refs_3_.3) | copy-start | bytes 4718596
  12.9 12.5 %copy-start = (bf16[3456,128]{1,0:T(8,128)(2,1)S(1)}, bf16[3456,128]{1,0:T(8,128)(2,1)}, u32[]{:S(2)}) copy-start(bf16[3456,128]{1,0:T(8,128)(2,1)} %weight.3) | copy-start | bytes 2654212
  13.5 1.8 %collective-permute-start.1 = (bf16[2,32,768]{2,1,0:T(8,128)(2,1)S(1)}, bf16[2,32,768]{2,1,0:T(8,128)(2,1)S(1)}, u32[]{:S(2)}, u32[]{:S(2)}) collective-permute-start(bf16[2,32,768]{2,1,0:T(8,128)(2,1)S(1)} %get-tuple-element.41), channel_id=1, source_target_pairs={{0,1},{1,0},{2,3},{3,2},{4,5},{5,4},{6,7},{7,6},{8,9},{9,8},{10,11... | collective-permute-start | bytes 294920 | tf_op jit(solution)/shard_map/ppermute | solution.py:493
  15.5 6.0 %collective-permute-start.3 = (bf16[32,768]{1,0:T(8,128)(2,1)S(1)}, bf16[32,768]{1,0:T(8,128)(2,1)S(1)}, u32[]{:S(2)}, u32[]{:S(2)}) collective-permute-start(bf16[32,768]{1,0:T(8,128)(2,1)S(1)} %get-tuple-element.45), channel_id=1, source_target_pairs={{0,12},{1,13},{2,14},{3,15},{4,8},{5,9},{6,10},{7,11},{8,4},{9,5},... | collective-permute-start | bytes 147464 | tf_op jit(solution)/shard_map/ppermute | solution.py:493
  19.3 5.0 %collective-permute-start.4 = (bf16[32,768]{1,0:T(8,128)(2,1)S(1)}, bf16[32,768]{1,0:T(8,128)(2,1)S(1)}, u32[]{:S(2)}, u32[]{:S(2)}) collective-permute-start(bf16[32,768]{1,0:T(8,128)(2,1)S(1)} %get-tuple-element.46), channel_id=1, source_target_pairs={{0,8},{1,9},{2,10},{3,11},{4,12},{5,13},{6,14},{7,15},{8,0},{9,1},... | collective-permute-start | bytes 147464 | tf_op jit(solution)/shard_map/ppermute | solution.py:493
  19.3 5.0 %collective-permute-start.5 = (bf16[32,768]{1,0:T(8,128)(2,1)S(1)}, bf16[32,768]{1,0:T(8,128)(2,1)S(1)}, u32[]{:S(2)}, u32[]{:S(2)}) collective-permute-start(bf16[32,768]{1,0:T(8,128)(2,1)S(1)} %get-tuple-element.47), channel_id=1, source_target_pairs={{0,4},{1,5},{2,6},{3,7},{4,0},{5,1},{6,2},{7,3},{8,12},{9,13},{10,... | collective-permute-start | bytes 147464 | tf_op jit(solution)/shard_map/ppermute | solution.py:493
  24.7 4.5 %collective-permute-start.7 = (bf16[8,16,128]{2,1,0:T(8,128)(2,1)S(1)}, bf16[8,16,128]{2,1,0:T(8,128)(2,1)S(1)}, u32[]{:S(2)}, u32[]{:S(2)}) collective-permute-start(bf16[8,16,128]{2,1,0:T(8,128)(2,1)S(1)} %get-tuple-element.52), channel_id=1, source_target_pairs={{1,2},{3,4},{5,6},{7,8},{9,10},{11,12},{13,14},{2,1},{4,3},{6,5},{... | collective-permute-start | bytes 98312 | tf_op jit(solution)/shard_map/ppermute | solution.py:534
  25.9 4.1 %collective-permute-start.6 = (bf16[8,16,128]{2,1,0:T(8,128)(2,1)S(1)}, bf16[8,16,128]{2,1,0:T(8,128)(2,1)S(1)}, u32[]{:S(2)}, u32[]{:S(2)}) collective-permute-start(bf16[8,16,128]{2,1,0:T(8,128)(2,1)S(1)} %get-tuple-element.51), channel_id=1, source_target_pairs={{0,1},{1,0},{2,3},{3,2},{4,5},{5,4},{6,7},{7,6},{8,9},{9,8},{10,11... | collective-permute-start | bytes 98312 | tf_op jit(solution)/shard_map/ppermute | solution.py:493

commit v6 on v5

--- a/solution.py
+++ b/solution.py
@@ -41,7 +41,7 @@
     return value
 
 
-def ffn_rows(base, mixed, gain_row, wo, wu, wd, normed, hidden, before_up=None, before_down=None):
+def ffn_rows(base, mixed, gain_row, wo, wu, wd, normed, hidden):
     half = normed.shape[0] // 2
     total = jnp.zeros((half, normed.shape[1]), jnp.float32)
     for m in range(2):
@@ -49,8 +49,6 @@
         mid = base[rows].astype(jnp.float32) + dot(mixed[rows], wo[...])
         normed[rows, :] = rms_scale(mid, gain_row)
         total = total + mid
-    if before_up is not None:
-        before_up()
     chunk = hidden.shape[1] // 2
     for c in range(2):
         columns = slice(c * chunk, (c + 1) * chunk)
@@ -59,8 +57,6 @@
             for m in range(2)
         ]
         hidden[:, columns] = (both[0] + both[1]).astype(jnp.bfloat16)
-    if before_down is not None:
-        before_down()
     return total + dot(hidden[...], wd[...])
 
 
@@ -124,7 +120,7 @@
         pltpu.make_async_copy(src, dst, sems.at[i])
         for i, (src, dst) in enumerate(zip(sources, targets, strict=True))
     ]
-    for i in (2, 3, 5, 6, 7, 0, 1, 4, 8, 9, 10, 11, 12):
+    for i in (5, 2, 6, 3, 7, 8, 9, 10, 11, 12, 0, 1, 4):
         copies[i].start()
     position = lax.axis_index("brick")
     residue = lax.rem(position, WDEP)
@@ -139,7 +135,8 @@
                 tok[m, s].astype(jnp.float32), gain_refs[m][...][None, :]
             )
     for i, (weight, result) in enumerate(((wq, q_all), (wk, k_all), (wv, v_all))):
-        copies[7 + i].wait()
+        for n in ((7,), (8, 9), ())[i]:
+            copies[n].wait()
         for m in range(2):
             half = slice(m * rows, (m + 1) * rows)
             result[half, :] = dot(normed[half, :], weight[...]).astype(jnp.bfloat16)
@@ -147,7 +144,7 @@
         for m in range(2):
             place, start = m * rows + s * tokens, (1 - m) * rows + s * tokens
             attend(q_all, k_all, v_all, mixed, place, start, tokens)
-    for i in (0, 1, 4, 10):
+    for i in (0, 1, 4, 10, 11, 12):
         copies[i].wait()
 
     def picked(rels):
@@ -179,8 +176,6 @@
         wd,
         ffn_normed,
         ffn_hidden,
-        copies[11].wait,
-        copies[12].wait,
     )
     for j, scale in enumerate(scales):
         out = (far_out, passing_out)[j % 2]

time: 31.2 us -> 30.7 us (0.984)
  Pallas kernels: 12 us -> 11.5 us
    pallas_call x1, Pallas kernels: 7.34 us -> 6.86 us  [far_call(): pl.pallas_call(window_kernel, out_shape=[out, out, rest, rest, pltpu.VMEM...]
where the time goes in v6:
time: 30.7 us; the launch traced here: 30.6 us
  Pallas kernels  11.5 us (37%)
  starting transfers between devices  11.4 us (37%)
  waiting for transfers between devices  7.58 us (25%)
    ppermute x7, starting transfers between devices, swap(): lax.ppermute(values, 'brick', [(i, i ^ distance) for i in range(total)])  10.8 us
    ppermute x7, waiting for transfers between devices, swap(): lax.ppermute(values, 'brick', [(i, i ^ distance) for i in range(total)])  7.57 us
    pallas_call x1, Pallas kernels, far_call(): pl.pallas_call(window_kernel, out_shape=[out, out, rest, rest, pltpu.VMEM...  6.86 us
    pallas_call x1, Pallas kernels, near_call(): pl.pallas_call(functools.partial(near_kernel, outer, tokens), out_shape=[...  2.51 us
    pallas_call x1, Pallas kernels, conv_halo_call(): pl.pallas_call(conv_halo_kernel, out_shape=jax.ShapeDtypeStruct(shape, jn...  0.97 us
    ppermute x1, starting transfers between devices, on_device(): far = lax.ppermute(far, 'brick', pairs + [(j, i) for i, j in pairs])  0.66 us
  transfers between devices with their start and end apart: 8, of which 5 were waited for; matrix products, arithmetic and copies ran while one was open for 0% of the time, Pallas kernels for 10%

profile of v6, /device:TPU:0, one launch (start us, length us, event | category | flops | bytes accessed | tf_op | source)
XLA Modules:
  0.0 30.6 jit_solution(14237390532133466868)
XLA Ops:
  0.0 6.9 %window_far.1 = (bf16[2,32,768]{2,1,0:T(8,128)(2,1)S(1)}, bf16[2,32,768]{2,1,0:T(8,128)(2,1)S(1)}, bf16[256,768]{1,0:T(8,128)(2,1)S(1)}, bf16[256,768]{1,0:T(8,1...) custom-call(s32[32]{0:T(128)} %anchor_ref.1, ...), custom_call_target="tpu_custom_call" | custom-call | tf_op jit(solution)/shard_map/window_far/pallas_call | solution.py:279
  6.9 3.0 %collective-permute-start = (bf16[2,32,768]{2,1,0:T(8,128)(2,1)S(1)}, bf16[2,32,768]{2,1,0:T(8,128)(2,1)S(1)}, u32[]{:S(2)}, u32[]{:S(2)}) collective-permute-start(bf16[2,32,768]{2,1,0:T(8,128)(2,1)S(1)} %get-tuple-element.40), channel_id=1, source_target_pairs={{0,2},{1,3},{2,0},{3,1},{4,6},{5,7},{6,4},{7,5},{8,10},{9,11},{10,... | collective-permute-start | bytes 294920 | tf_op jit(solution)/shard_map/ppermute | solution.py:488
  9.9 0.0 collective-permute-start.2
  9.9 2.5 %window_near.1 = (bf16[2,32,768]{2,1,0:T(8,128)(2,1)S(1)}, bf16[2,32,768]{2,1,0:T(8,128)(2,1)S(1)}, f32[32,128]{1,0:T(8,128)S(1)}, f32[8,128]{1,0:T(8,128)S(1)}) custom-call(s32[32]{0:T(128)} %anchor_ref.1, s32[1,32]{1,0:T(1,128)} %bitcast.2, s32[1,32]{1,0:T(1,128)} %bitcast.3, bf16[256,768]{1,0:T(8,128)(2,1)S(1)} %get-tuple-element.29.rest_mixed, ...), custom_call_target="tpu_custom_call" | custom-call | flops 905969664 | bytes 393216 | tf_op jit(solution)/shard_map/window_near/pallas_call | solution.py:311
  12.4 0.0 copy-start
  12.4 0.6 %collective-permute-done.far = bf16[2,32,768]{2,1,0:T(8,128)(2,1)S(1)} collective-permute-done((bf16[2,32,768]{2,1,0:T(8,128)(2,1)S(1)}, bf16[2,32,768]{2,1,0:T(8,128)(2,1)S(1)}, u32[]{:S(2)}, u32[]{:S(2)}) %collective-permute-start) | collective-permute-done | bytes 98336 | tf_op jit(solution)/shard_map/ppermute | solution.py:488
  13.0 0.0 collective-permute-start.1
  13.0 1.8 %collective-permute-done.2.forward = bf16[2,32,768]{2,1,0:T(8,128)(2,1)S(1)} collective-permute-done((bf16[2,32,768]{2,1,0:T(8,128)(2,1)S(1)}, bf16[2,32,768]{2,1,0:T(8,128)(2,1)S(1)}, u32[]{:S(2)}, u32[]{:S(2)}) %collective-permute-start.2) | collective-permute-done | bytes 98336 | tf_op jit(solution)/shard_map/ppermute | solution.py:488
  14.8 0.0 collective-permute-done.1.near
  14.8 0.2 plane_sum.1
  15.0 3.8 %collective-permute-start.3 = (bf16[32,768]{1,0:T(8,128)(2,1)S(1)}, bf16[32,768]{1,0:T(8,128)(2,1)S(1)}, u32[]{:S(2)}, u32[]{:S(2)}) collective-permute-start(bf16[32,768]{1,0:T(8,128)(2,1)S(1)} %get-tuple-element.45), channel_id=1, source_target_pairs={{0,12},{1,13},{2,14},{3,15},{4,8},{5,9},{6,10},{7,11},{8,4},{9,5},... | collective-permute-start | bytes 147464 | tf_op jit(solution)/shard_map/ppermute | solution.py:488
  18.8 0.0 collective-permute-start.4
  18.8 0.6 %collective-permute-start.5 = (bf16[32,768]{1,0:T(8,128)(2,1)S(1)}, bf16[32,768]{1,0:T(8,128)(2,1)S(1)}, u32[]{:S(2)}, u32[]{:S(2)}) collective-permute-start(bf16[32,768]{1,0:T(8,128)(2,1)S(1)} %get-tuple-element.47), channel_id=1, source_target_pairs={{0,4},{1,5},{2,6},{3,7},{4,0},{5,1},{6,2},{7,3},{8,12},{9,13},{10,... | collective-permute-start | bytes 147464 | tf_op jit(solution)/shard_map/ppermute | solution.py:488
  19.5 1.5 %collective-permute-done.3.refs_0_ = bf16[32,768]{1,0:T(8,128)(2,1)S(1)} collective-permute-done((bf16[32,768]{1,0:T(8,128)(2,1)S(1)}, bf16[32,768]{1,0:T(8,128)(2,1)S(1)}, u32[]{:S(2)}, u32[]{:S(2)}) %collective-permute-start.3) | collective-permute-done | bytes 49184 | tf_op jit(solution)/shard_map/ppermute | solution.py:488
  21.0 2.8 %collective-permute-done.4.refs_1_ = bf16[32,768]{1,0:T(8,128)(2,1)S(1)} collective-permute-done((bf16[32,768]{1,0:T(8,128)(2,1)S(1)}, bf16[32,768]{1,0:T(8,128)(2,1)S(1)}, u32[]{:S(2)}, u32[]{:S(2)}) %collective-permute-start.4) | collective-permute-done | bytes 49184 | tf_op jit(solution)/shard_map/ppermute | solution.py:488
  23.8 0.0 collective-permute-done.5.refs_2_
  23.8 0.0 copy-done.1
  23.8 0.4 %upconv.1 = (bf16[2,8,16,128]{3,2,1,0:T(8,128)(2,1)S(1)}, bf16[8,16,128]{2,1,0:T(8,128)(2,1)S(1)}, bf16[8,16,128]{2,1,0:T(8,128)(2,1)S(1)}) custom-call(f32[8,128]{1,0:T(8,128)S(1)} %get-tuple-element.36.bound, f32[32,768]{1,0:T(8,128)S(1)} %get-tuple-element.44.kept, bf16[32,768]{1,0:T(8,128)(2,1)S(1)} %collective-permute-done.3.refs_0_, ...), custom_call_target="tpu_custom_call" | custom-call | tf_op jit(solution)/shard_map/upconv/pallas_call | solution.py:388
  24.3 0.7 %collective-permute-start.7 = (bf16[8,16,128]{2,1,0:T(8,128)(2,1)S(1)}, bf16[8,16,128]{2,1,0:T(8,128)(2,1)S(1)}, u32[]{:S(2)}, u32[]{:S(2)}) collective-permute-start(bf16[8,16,128]{2,1,0:T(8,128)(2,1)S(1)} %get-tuple-element.52), channel_id=1, source_target_pairs={{1,2},{3,4},{5,6},{7,8},{9,10},{11,12},{13,14},{2,1},{4,3},{6,5},{... | collective-permute-start | bytes 98312 | tf_op jit(solution)/shard_map/ppermute | solution.py:529
  24.9 0.5 %conv_local.1.part_ref = f32[256,128]{1,0:T(8,128)S(1)} custom-call(bf16[2,8,16,128]{3,2,1,0:T(8,128)(2,1)S(1)} %get-tuple-element.49.up_ref, bf16[3456,128]{1,0:T(8,128)(2,1)S(1)} %copy-done), custom_call_target="tpu_custom_call" | custom-call | flops 150994944 | bytes 393216 | tf_op jit(solution)/shard_map/conv_local/pallas_call | solution.py:463
  25.4 3.3 %collective-permute-start.6 = (bf16[8,16,128]{2,1,0:T(8,128)(2,1)S(1)}, bf16[8,16,128]{2,1,0:T(8,128)(2,1)S(1)}, u32[]{:S(2)}, u32[]{:S(2)}) collective-permute-start(bf16[8,16,128]{2,1,0:T(8,128)(2,1)S(1)} %get-tuple-element.51), channel_id=1, source_target_pairs={{0,1},{1,0},{2,3},{3,2},{4,5},{5,4},{6,7},{7,6},{8,9},{9,8},{10,11... | collective-permute-start | bytes 98312 | tf_op jit(solution)/shard_map/ppermute | solution.py:488
  28.7 0.0 collective-permute-done.7.far_ref
  28.7 0.9 %collective-permute-done.6.near_ref = bf16[8,16,128]{2,1,0:T(8,128)(2,1)S(1)} collective-permute-done((bf16[8,16,128]{2,1,0:T(8,128)(2,1)S(1)}, bf16[8,16,128]{2,1,0:T(8,128)(2,1)S(1)}, u32[]{:S(2)}, u32[]{:S(2)}) %collective-permute-start.6) | collective-permute-done | bytes 32800 | tf_op jit(solution)/shard_map/ppermute | solution.py:488
  29.6 1.0 %conv_halo.1 = bf16[2,8,16,128]{3,2,1,0:T(8,128)(2,1)} custom-call(f32[256,128]{1,0:T(8,128)S(1)} %conv_local.1.part_ref, bf16[8,16,128]{2,1,0:T(8,128)(2,1)S(1)} %collective-permute-done.6.near_ref, bf16[8,16,128]{2,1,0:T(8,128)(2,1)S(1)} %collective-permute-done.7.far_ref, bf16[3456,128]{1,0:T(8,128)(2,1)S(1)} %copy-done), custom_call_target="tpu_custom_call" | custom-call | tf_op jit(solution)/shard_map/conv_halo/pallas_call | solution.py:476
  (2 shorter events, 0.0 us)
Async XLA Ops:
  6.9 6.1 %collective-permute-start = (bf16[2,32,768]{2,1,0:T(8,128)(2,1)S(1)}, bf16[2,32,768]{2,1,0:T(8,128)(2,1)S(1)}, u32[]{:S(2)}, u32[]{:S(2)}) collective-permute-start(bf16[2,32,768]{2,1,0:T(8,128)(2,1)S(1)} %get-tuple-element.40), channel_id=1, source_target_pairs={{0,2},{1,3},{2,0},{3,1},{4,6},{5,7},{6,4},{7,5},{8,10},{9,11},{10,... | collective-permute-start | bytes 294920 | tf_op jit(solution)/shard_map/ppermute | solution.py:488
  9.9 4.9 %collective-permute-start.2 = (bf16[2,32,768]{2,1,0:T(8,128)(2,1)S(1)}, bf16[2,32,768]{2,1,0:T(8,128)(2,1)S(1)}, u32[]{:S(2)}, u32[]{:S(2)}) collective-permute-start(bf16[2,32,768]{2,1,0:T(8,128)(2,1)S(1)} %get-tuple-element.43), channel_id=1, source_target_pairs={{0,3},{1,2},{2,1},{3,0},{4,7},{5,6},{6,5},{7,4},{8,11},{9,10},{10,... | collective-permute-start | bytes 294920 | tf_op jit(solution)/shard_map/ppermute | solution.py:488
  9.9 14.0 %copy-start.1 = (bf16[768,1024]{1,0:T(8,128)(2,1)S(1)}, bf16[768,1024]{1,0:T(8,128)(2,1)}, u32[]{:S(2)}) copy-start(bf16[768,1024]{1,0:T(8,128)(2,1)} %refs_3_.3) | copy-start | bytes 4718596
  12.4 12.5 %copy-start = (bf16[3456,128]{1,0:T(8,128)(2,1)S(1)}, bf16[3456,128]{1,0:T(8,128)(2,1)}, u32[]{:S(2)}) copy-start(bf16[3456,128]{1,0:T(8,128)(2,1)} %weight.3) | copy-start | bytes 2654212
  13.0 1.8 %collective-permute-start.1 = (bf16[2,32,768]{2,1,0:T(8,128)(2,1)S(1)}, bf16[2,32,768]{2,1,0:T(8,128)(2,1)S(1)}, u32[]{:S(2)}, u32[]{:S(2)}) collective-permute-start(bf16[2,32,768]{2,1,0:T(8,128)(2,1)S(1)} %get-tuple-element.41), channel_id=1, source_target_pairs={{0,1},{1,0},{2,3},{3,2},{4,5},{5,4},{6,7},{7,6},{8,9},{9,8},{10,11... | collective-permute-start | bytes 294920 | tf_op jit(solution)/shard_map/ppermute | solution.py:488
  15.0 6.0 %collective-permute-start.3 = (bf16[32,768]{1,0:T(8,128)(2,1)S(1)}, bf16[32,768]{1,0:T(8,128)(2,1)S(1)}, u32[]{:S(2)}, u32[]{:S(2)}) collective-permute-start(bf16[32,768]{1,0:T(8,128)(2,1)S(1)} %get-tuple-element.45), channel_id=1, source_target_pairs={{0,12},{1,13},{2,14},{3,15},{4,8},{5,9},{6,10},{7,11},{8,4},{9,5},... | collective-permute-start | bytes 147464 | tf_op jit(solution)/shard_map/ppermute | solution.py:488
  18.8 5.0 %collective-permute-start.4 = (bf16[32,768]{1,0:T(8,128)(2,1)S(1)}, bf16[32,768]{1,0:T(8,128)(2,1)S(1)}, u32[]{:S(2)}, u32[]{:S(2)}) collective-permute-start(bf16[32,768]{1,0:T(8,128)(2,1)S(1)} %get-tuple-element.46), channel_id=1, source_target_pairs={{0,8},{1,9},{2,10},{3,11},{4,12},{5,13},{6,14},{7,15},{8,0},{9,1},... | collective-permute-start | bytes 147464 | tf_op jit(solution)/shard_map/ppermute | solution.py:488
  18.8 5.0 %collective-permute-start.5 = (bf16[32,768]{1,0:T(8,128)(2,1)S(1)}, bf16[32,768]{1,0:T(8,128)(2,1)S(1)}, u32[]{:S(2)}, u32[]{:S(2)}) collective-permute-start(bf16[32,768]{1,0:T(8,128)(2,1)S(1)} %get-tuple-element.47), channel_id=1, source_target_pairs={{0,4},{1,5},{2,6},{3,7},{4,0},{5,1},{6,2},{7,3},{8,12},{9,13},{10,... | collective-permute-start | bytes 147464 | tf_op jit(solution)/shard_map/ppermute | solution.py:488
  24.3 4.5 %collective-permute-start.7 = (bf16[8,16,128]{2,1,0:T(8,128)(2,1)S(1)}, bf16[8,16,128]{2,1,0:T(8,128)(2,1)S(1)}, u32[]{:S(2)}, u32[]{:S(2)}) collective-permute-start(bf16[8,16,128]{2,1,0:T(8,128)(2,1)S(1)} %get-tuple-element.52), channel_id=1, source_target_pairs={{1,2},{3,4},{5,6},{7,8},{9,10},{11,12},{13,14},{2,1},{4,3},{6,5},{... | collective-permute-start | bytes 98312 | tf_op jit(solution)/shard_map/ppermute | solution.py:529
  25.4 4.1 %collective-permute-start.6 = (bf16[8,16,128]{2,1,0:T(8,128)(2,1)S(1)}, bf16[8,16,128]{2,1,0:T(8,128)(2,1)S(1)}, u32[]{:S(2)}, u32[]{:S(2)}) collective-permute-start(bf16[8,16,128]{2,1,0:T(8,128)(2,1)S(1)} %get-tuple-element.51), channel_id=1, source_target_pairs={{0,1},{1,0},{2,3},{3,2},{4,5},{5,4},{6,7},{7,6},{8,9},{9,8},{10,11... | collective-permute-start | bytes 98312 | tf_op jit(solution)/shard_map/ppermute | solution.py:488

commit v7 on v6

--- a/solution.py
+++ b/solution.py
@@ -438,8 +438,11 @@
     depth, height, breadth, channels = out_ref.shape
     rows = height * breadth
     span = 9 * channels
-    even = lax.rem(lax.axis_index("brick"), 2) == 0
+    position = lax.axis_index("brick")
+    even = lax.rem(position, 2) == 0
+    edge = (position == 0) | (position == lax.axis_size("brick") - 1)
     near, far = near_ref[...], far_ref[...]
+    far = jnp.where(edge, jnp.zeros_like(far), far)
     fill_patches([jnp.where(even, far, near), jnp.where(even, near, far)], padded, patches)
     for z in range(depth):
         total = part_ref[z * rows : (z + 1) * rows, :]
@@ -486,6 +489,16 @@
 
 def swap(values, distance, total):
     return lax.ppermute(values, "brick", [(i, i ^ distance) for i in range(total)])
+
+
+def far_pairs(groups, total):
+    pairs = []
+    for g in range(groups):
+        for i in range(1, total - 1, 2):
+            pairs += [(g * total + i, g * total + i + 1), (g * total + i + 1, g * total + i)]
+        other = (g ^ 1) if groups % 2 == 0 else g
+        pairs += [(g * total + end, other * total + end) for end in (0, total - 1)]
+    return pairs
 
 
 def on_device(
@@ -525,8 +538,7 @@
     kept, *sent = gather_call(outer, masks, own, near, far, passing)
     pieces = [swap(sent[k - 1], k * WDEP, total) for k in range(outer - 1, 0, -1)]
     upsampled, near, far = upconv_call(channels, bound, kept, pieces, w_upconv)
-    pairs = [(i, i + 1) for i in range(1, total - 1, 2)]
-    far = lax.ppermute(far, "brick", pairs + [(j, i) for i, j in pairs])
+    far = lax.ppermute(far, ("groups", "brick"), far_pairs(lax.axis_size("groups"), total))
     part = conv_local_call(upsampled, w_conv)
     near, part = lax.optimization_barrier((near, part))
     near = swap(near, 1, total)

time: 30.7 us -> 29.4 us (0.958)
  starting transfers between devices: 11.4 us -> 9.59 us
  waiting for transfers between devices: 7.58 us -> 8.09 us
    ppermute x7, starting transfers between devices: 10.8 us -> 8.01 us  [swap(): lax.ppermute(values, 'brick', [(i, i ^ distance) for i in range(total)])]
    ppermute x1, waiting for transfers between devices: 0.01 us -> 1.37 us  [on_device(): lax.ppermute(far, ('groups', 'brick'), far_pairs(lax.axis_size('groups'),...]
    ppermute x1, starting transfers between devices: 0.66 us -> 1.58 us  [on_device(): lax.ppermute(far, ('groups', 'brick'), far_pairs(lax.axis_size('groups'),...]
    ppermute x7, waiting for transfers between devices: 7.57 us -> 6.72 us  [swap(): lax.ppermute(values, 'brick', [(i, i ^ distance) for i in range(total)])]
where the time goes in v7:
time: 29.4 us; the launch traced here: 29.2 us
  Pallas kernels  11.5 us (39%)
  starting transfers between devices  9.59 us (33%)
  waiting for transfers between devices  8.09 us (28%)
    ppermute x7, starting transfers between devices, swap(): lax.ppermute(values, 'brick', [(i, i ^ distance) for i in range(total)])  8.01 us
    pallas_call x1, Pallas kernels, far_call(): pl.pallas_call(window_kernel, out_shape=[out, out, rest, rest, pltpu.VMEM...  6.86 us
    ppermute x7, waiting for transfers between devices, swap(): lax.ppermute(values, 'brick', [(i, i ^ distance) for i in range(total)])  6.72 us
    pallas_call x1, Pallas kernels, near_call(): pl.pallas_call(functools.partial(near_kernel, outer, tokens), out_shape=[...  2.51 us
    ppermute x1, starting transfers between devices, on_device(): lax.ppermute(far, ('groups', 'brick'), far_pairs(lax.axis_size('groups'),...  1.58 us
    ppermute x1, waiting for transfers between devices, on_device(): lax.ppermute(far, ('groups', 'brick'), far_pairs(lax.axis_size('groups'),...  1.37 us
    pallas_call x1, Pallas kernels, conv_halo_call(): pl.pallas_call(conv_halo_kernel, out_shape=jax.ShapeDtypeStruct(shape, jn...  0.98 us
  transfers between devices with their start and end apart: 8, of which 5 were waited for; matrix products, arithmetic and copies ran while one was open for 0% of the time, Pallas kernels for 10%

profile of v7, /device:TPU:0, one launch (start us, length us, event | category | flops | bytes accessed | tf_op | source)
XLA Modules:
  0.0 29.2 jit_solution(3485862204966276613)
XLA Ops:
  0.0 6.9 %window_far.1 = (bf16[2,32,768]{2,1,0:T(8,128)(2,1)S(1)}, bf16[2,32,768]{2,1,0:T(8,128)(2,1)S(1)}, bf16[256,768]{1,0:T(8,128)(2,1)S(1)}, bf16[256,768]{1,0:T(8,1...) custom-call(s32[32]{0:T(128)} %anchor_ref.1, ...), custom_call_target="tpu_custom_call" | custom-call | tf_op jit(solution)/shard_map/window_far/pallas_call | solution.py:279
  6.9 3.0 %collective-permute-start = (bf16[2,32,768]{2,1,0:T(8,128)(2,1)S(1)}, bf16[2,32,768]{2,1,0:T(8,128)(2,1)S(1)}, u32[]{:S(2)}, u32[]{:S(2)}) collective-permute-start(bf16[2,32,768]{2,1,0:T(8,128)(2,1)S(1)} %get-tuple-element.40), channel_id=1, source_target_pairs={{0,2},{1,3},{2,0},{3,1},{4,6},{5,7},{6,4},{7,5},{8,10},{9,11},{10,... | collective-permute-start | bytes 294920 | tf_op jit(solution)/shard_map/ppermute | solution.py:491
  9.9 0.0 collective-permute-start.2
  9.9 2.5 %window_near.1 = (bf16[2,32,768]{2,1,0:T(8,128)(2,1)S(1)}, bf16[2,32,768]{2,1,0:T(8,128)(2,1)S(1)}, f32[32,128]{1,0:T(8,128)S(1)}, f32[8,128]{1,0:T(8,128)S(1)}) custom-call(s32[32]{0:T(128)} %anchor_ref.1, s32[1,32]{1,0:T(1,128)} %bitcast.2, s32[1,32]{1,0:T(1,128)} %bitcast.3, bf16[256,768]{1,0:T(8,128)(2,1)S(1)} %get-tuple-element.29.rest_mixed, ...), custom_call_target="tpu_custom_call" | custom-call | flops 905969664 | bytes 393216 | tf_op jit(solution)/shard_map/window_near/pallas_call | solution.py:311
  12.4 0.0 copy-start
  12.4 0.6 %collective-permute-done.far = bf16[2,32,768]{2,1,0:T(8,128)(2,1)S(1)} collective-permute-done((bf16[2,32,768]{2,1,0:T(8,128)(2,1)S(1)}, bf16[2,32,768]{2,1,0:T(8,128)(2,1)S(1)}, u32[]{:S(2)}, u32[]{:S(2)}) %collective-permute-start) | collective-permute-done | bytes 98336 | tf_op jit(solution)/shard_map/ppermute | solution.py:491
  13.0 0.0 collective-permute-start.1
  13.0 1.8 %collective-permute-done.2.forward = bf16[2,32,768]{2,1,0:T(8,128)(2,1)S(1)} collective-permute-done((bf16[2,32,768]{2,1,0:T(8,128)(2,1)S(1)}, bf16[2,32,768]{2,1,0:T(8,128)(2,1)S(1)}, u32[]{:S(2)}, u32[]{:S(2)}) %collective-permute-start.2) | collective-permute-done | bytes 98336 | tf_op jit(solution)/shard_map/ppermute | solution.py:491
  14.8 0.0 collective-permute-done.1.near
  14.8 0.2 plane_sum.1
  15.0 3.8 %collective-permute-start.3 = (bf16[32,768]{1,0:T(8,128)(2,1)S(1)}, bf16[32,768]{1,0:T(8,128)(2,1)S(1)}, u32[]{:S(2)}, u32[]{:S(2)}) collective-permute-start(bf16[32,768]{1,0:T(8,128)(2,1)S(1)} %get-tuple-element.45), channel_id=1, source_target_pairs={{0,12},{1,13},{2,14},{3,15},{4,8},{5,9},{6,10},{7,11},{8,4},{9,5},... | collective-permute-start | bytes 147464 | tf_op jit(solution)/shard_map/ppermute | solution.py:491
  18.8 0.0 collective-permute-start.4
  18.8 0.6 %collective-permute-start.5 = (bf16[32,768]{1,0:T(8,128)(2,1)S(1)}, bf16[32,768]{1,0:T(8,128)(2,1)S(1)}, u32[]{:S(2)}, u32[]{:S(2)}) collective-permute-start(bf16[32,768]{1,0:T(8,128)(2,1)S(1)} %get-tuple-element.47), channel_id=1, source_target_pairs={{0,4},{1,5},{2,6},{3,7},{4,0},{5,1},{6,2},{7,3},{8,12},{9,13},{10,... | collective-permute-start | bytes 147464 | tf_op jit(solution)/shard_map/ppermute | solution.py:491
  19.5 1.5 %collective-permute-done.3.refs_0_ = bf16[32,768]{1,0:T(8,128)(2,1)S(1)} collective-permute-done((bf16[32,768]{1,0:T(8,128)(2,1)S(1)}, bf16[32,768]{1,0:T(8,128)(2,1)S(1)}, u32[]{:S(2)}, u32[]{:S(2)}) %collective-permute-start.3) | collective-permute-done | bytes 49184 | tf_op jit(solution)/shard_map/ppermute | solution.py:491
  21.0 2.8 %collective-permute-done.4.refs_1_ = bf16[32,768]{1,0:T(8,128)(2,1)S(1)} collective-permute-done((bf16[32,768]{1,0:T(8,128)(2,1)S(1)}, bf16[32,768]{1,0:T(8,128)(2,1)S(1)}, u32[]{:S(2)}, u32[]{:S(2)}) %collective-permute-start.4) | collective-permute-done | bytes 49184 | tf_op jit(solution)/shard_map/ppermute | solution.py:491
  23.8 0.0 collective-permute-done.5.refs_2_
  23.8 0.0 copy-done.1
  23.8 0.4 %upconv.1 = (bf16[2,8,16,128]{3,2,1,0:T(8,128)(2,1)S(1)}, bf16[8,16,128]{2,1,0:T(8,128)(2,1)S(1)}, bf16[8,16,128]{2,1,0:T(8,128)(2,1)S(1)}) custom-call(f32[8,128]{1,0:T(8,128)S(1)} %get-tuple-element.36.bound, f32[32,768]{1,0:T(8,128)S(1)} %get-tuple-element.44.kept, bf16[32,768]{1,0:T(8,128)(2,1)S(1)} %collective-permute-done.3.refs_0_, ...), custom_call_target="tpu_custom_call" | custom-call | tf_op jit(solution)/shard_map/upconv/pallas_call | solution.py:388
  24.3 1.6 %collective-permute-start.7 = (bf16[8,16,128]{2,1,0:T(8,128)(2,1)S(1)}, bf16[8,16,128]{2,1,0:T(8,128)(2,1)S(1)}, u32[]{:S(2)}, u32[]{:S(2)}) collective-permute-start(bf16[8,16,128]{2,1,0:T(8,128)(2,1)S(1)} %get-tuple-element.52), channel_id=1, source_target_pairs={{1,2},{2,1},{3,4},{4,3},{5,6},{6,5},{7,8},{8,7},{9,10},{10,9},{11,... | collective-permute-start | bytes 98312 | tf_op jit(solution)/shard_map/ppermute | solution.py:541
  25.8 0.5 %conv_local.1.part_ref = f32[256,128]{1,0:T(8,128)S(1)} custom-call(bf16[2,8,16,128]{3,2,1,0:T(8,128)(2,1)S(1)} %get-tuple-element.49.up_ref, bf16[3456,128]{1,0:T(8,128)(2,1)S(1)} %copy-done), custom_call_target="tpu_custom_call" | custom-call | flops 150994944 | bytes 393216 | tf_op jit(solution)/shard_map/conv_local/pallas_call | solution.py:466
  26.3 0.5 %collective-permute-start.6 = (bf16[8,16,128]{2,1,0:T(8,128)(2,1)S(1)}, bf16[8,16,128]{2,1,0:T(8,128)(2,1)S(1)}, u32[]{:S(2)}, u32[]{:S(2)}) collective-permute-start(bf16[8,16,128]{2,1,0:T(8,128)(2,1)S(1)} %get-tuple-element.51), channel_id=1, source_target_pairs={{0,1},{1,0},{2,3},{3,2},{4,5},{5,4},{6,7},{7,6},{8,9},{9,8},{10,11... | collective-permute-start | bytes 98312 | tf_op jit(solution)/shard_map/ppermute | solution.py:491
  26.9 1.4 %collective-permute-done.7.far_ref = bf16[8,16,128]{2,1,0:T(8,128)(2,1)S(1)} collective-permute-done((bf16[8,16,128]{2,1,0:T(8,128)(2,1)S(1)}, bf16[8,16,128]{2,1,0:T(8,128)(2,1)S(1)}, u32[]{:S(2)}, u32[]{:S(2)}) %collective-permute-start.7) | collective-permute-done | bytes 32800 | tf_op jit(solution)/shard_map/ppermute | solution.py:541
  28.2 0.0 collective-permute-done.6.near_ref
  28.2 1.0 %conv_halo.1 = bf16[2,8,16,128]{3,2,1,0:T(8,128)(2,1)} custom-call(f32[256,128]{1,0:T(8,128)S(1)} %conv_local.1.part_ref, bf16[8,16,128]{2,1,0:T(8,128)(2,1)S(1)} %collective-permute-done.6.near_ref, bf16[8,16,128]{2,1,0:T(8,128)(2,1)S(1)} %collective-permute-done.7.far_ref, bf16[3456,128]{1,0:T(8,128)(2,1)S(1)} %copy-done), custom_call_target="tpu_custom_call" | custom-call | tf_op jit(solution)/shard_map/conv_halo/pallas_call | solution.py:479
  (2 shorter events, 0.0 us)
Async XLA Ops:
  6.9 6.1 %collective-permute-start = (bf16[2,32,768]{2,1,0:T(8,128)(2,1)S(1)}, bf16[2,32,768]{2,1,0:T(8,128)(2,1)S(1)}, u32[]{:S(2)}, u32[]{:S(2)}) collective-permute-start(bf16[2,32,768]{2,1,0:T(8,128)(2,1)S(1)} %get-tuple-element.40), channel_id=1, source_target_pairs={{0,2},{1,3},{2,0},{3,1},{4,6},{5,7},{6,4},{7,5},{8,10},{9,11},{10,... | collective-permute-start | bytes 294920 | tf_op jit(solution)/shard_map/ppermute | solution.py:491
  9.9 4.9 %collective-permute-start.2 = (bf16[2,32,768]{2,1,0:T(8,128)(2,1)S(1)}, bf16[2,32,768]{2,1,0:T(8,128)(2,1)S(1)}, u32[]{:S(2)}, u32[]{:S(2)}) collective-permute-start(bf16[2,32,768]{2,1,0:T(8,128)(2,1)S(1)} %get-tuple-element.43), channel_id=1, source_target_pairs={{0,3},{1,2},{2,1},{3,0},{4,7},{5,6},{6,5},{7,4},{8,11},{9,10},{10,... | collective-permute-start | bytes 294920 | tf_op jit(solution)/shard_map/ppermute | solution.py:491
  9.9 14.0 %copy-start.1 = (bf16[768,1024]{1,0:T(8,128)(2,1)S(1)}, bf16[768,1024]{1,0:T(8,128)(2,1)}, u32[]{:S(2)}) copy-start(bf16[768,1024]{1,0:T(8,128)(2,1)} %refs_3_.3) | copy-start | bytes 4718596
  12.4 13.5 %copy-start = (bf16[3456,128]{1,0:T(8,128)(2,1)S(1)}, bf16[3456,128]{1,0:T(8,128)(2,1)}, u32[]{:S(2)}) copy-start(bf16[3456,128]{1,0:T(8,128)(2,1)} %weight.3) | copy-start | bytes 2654212
  13.0 1.8 %collective-permute-start.1 = (bf16[2,32,768]{2,1,0:T(8,128)(2,1)S(1)}, bf16[2,32,768]{2,1,0:T(8,128)(2,1)S(1)}, u32[]{:S(2)}, u32[]{:S(2)}) collective-permute-start(bf16[2,32,768]{2,1,0:T(8,128)(2,1)S(1)} %get-tuple-element.41), channel_id=1, source_target_pairs={{0,1},{1,0},{2,3},{3,2},{4,5},{5,4},{6,7},{7,6},{8,9},{9,8},{10,11... | collective-permute-start | bytes 294920 | tf_op jit(solution)/shard_map/ppermute | solution.py:491
  15.0 6.0 %collective-permute-start.3 = (bf16[32,768]{1,0:T(8,128)(2,1)S(1)}, bf16[32,768]{1,0:T(8,128)(2,1)S(1)}, u32[]{:S(2)}, u32[]{:S(2)}) collective-permute-start(bf16[32,768]{1,0:T(8,128)(2,1)S(1)} %get-tuple-element.45), channel_id=1, source_target_pairs={{0,12},{1,13},{2,14},{3,15},{4,8},{5,9},{6,10},{7,11},{8,4},{9,5},... | collective-permute-start | bytes 147464 | tf_op jit(solution)/shard_map/ppermute | solution.py:491
  18.8 5.0 %collective-permute-start.4 = (bf16[32,768]{1,0:T(8,128)(2,1)S(1)}, bf16[32,768]{1,0:T(8,128)(2,1)S(1)}, u32[]{:S(2)}, u32[]{:S(2)}) collective-permute-start(bf16[32,768]{1,0:T(8,128)(2,1)S(1)} %get-tuple-element.46), channel_id=1, source_target_pairs={{0,8},{1,9},{2,10},{3,11},{4,12},{5,13},{6,14},{7,15},{8,0},{9,1},... | collective-permute-start | bytes 147464 | tf_op jit(solution)/shard_map/ppermute | solution.py:491
  18.8 5.0 %collective-permute-start.5 = (bf16[32,768]{1,0:T(8,128)(2,1)S(1)}, bf16[32,768]{1,0:T(8,128)(2,1)S(1)}, u32[]{:S(2)}, u32[]{:S(2)}) collective-permute-start(bf16[32,768]{1,0:T(8,128)(2,1)S(1)} %get-tuple-element.47), channel_id=1, source_target_pairs={{0,4},{1,5},{2,6},{3,7},{4,0},{5,1},{6,2},{7,3},{8,12},{9,13},{10,... | collective-permute-start | bytes 147464 | tf_op jit(solution)/shard_map/ppermute | solution.py:491
  24.3 4.0 %collective-permute-start.7 = (bf16[8,16,128]{2,1,0:T(8,128)(2,1)S(1)}, bf16[8,16,128]{2,1,0:T(8,128)(2,1)S(1)}, u32[]{:S(2)}, u32[]{:S(2)}) collective-permute-start(bf16[8,16,128]{2,1,0:T(8,128)(2,1)S(1)} %get-tuple-element.52), channel_id=1, source_target_pairs={{1,2},{2,1},{3,4},{4,3},{5,6},{6,5},{7,8},{8,7},{9,10},{10,9},{11,... | collective-permute-start | bytes 98312 | tf_op jit(solution)/shard_map/ppermute | solution.py:541
  26.3 1.9 %collective-permute-start.6 = (bf16[8,16,128]{2,1,0:T(8,128)(2,1)S(1)}, bf16[8,16,128]{2,1,0:T(8,128)(2,1)S(1)}, u32[]{:S(2)}, u32[]{:S(2)}) collective-permute-start(bf16[8,16,128]{2,1,0:T(8,128)(2,1)S(1)} %get-tuple-element.51), channel_id=1, source_target_pairs={{0,1},{1,0},{2,3},{3,2},{4,5},{5,4},{6,7},{7,6},{8,9},{9,8},{10,11... | collective-permute-start | bytes 98312 | tf_op jit(solution)/shard_map/ppermute | solution.py:491

commit v8 on v7

--- a/solution.py
+++ b/solution.py
@@ -358,45 +358,42 @@
     )(*map(in_vmem, (masks, own, near, far, forward)))
 
 
-def upconv_kernel(bound, kept, *refs):
-    pieces = refs[:-5]
-    weight, up_ref, near_ref, far_ref, grid = refs[-5:]
-    channels = up_ref.shape[-1]
+def up_layer(feature, weight, start, grid):
+    half = weight.shape[1] // 2
+    channels = half // 4
+    up_rows = dot(feature, weight[:, pl.ds(pl.multiple_of(start * half, half), half)])
+    for b in range(2):
+        for c in range(2):
+            chunk = b * 2 + c
+            for y in range(PY):
+                grid[2 * y + b, pl.ds(c, PX, stride=2), :] = up_rows[
+                    y * PX : (y + 1) * PX, chunk * channels : (chunk + 1) * channels
+                ]
+    return grid[...].astype(jnp.bfloat16)
+
+
+def up_far_kernel(bound, kept, *refs):
+    pieces = refs[:-4]
+    weight, feature_ref, far_ref, grid = refs[-4:]
     numerator = kept[...]
     for piece in pieces:
         numerator = numerator + piece[...].astype(jnp.float32)
     feature = (numerator / bound[:1, :1]).astype(jnp.bfloat16)
-    up_rows = dot(feature, weight[...])
-    for a in range(2):
-        for b in range(2):
-            for c in range(2):
-                chunk = (a * 2 + b) * 2 + c
-                for y in range(PY):
-                    grid[a, 2 * y + b, pl.ds(c, PX, stride=2), :] = up_rows[
-                        y * PX : (y + 1) * PX, chunk * channels : (chunk + 1) * channels
-                    ]
-    upsampled = grid[...].astype(jnp.bfloat16)
-    up_ref[...] = upsampled
-    even = lax.rem(lax.axis_index("brick"), 2) == 0
-    active = jnp.maximum(upsampled, jnp.zeros((), jnp.bfloat16))
-    near_ref[...] = jnp.where(even, active[1], active[0])
-    far_ref[...] = jnp.where(even, active[0], active[1])
-
-
-def upconv_call(channels, bound, kept, pieces, weight):
+    feature_ref[...] = feature
+    odd = lax.rem(lax.axis_index("brick"), 2)
+    far_ref[...] = up_layer(feature, weight, odd, grid)
+
+
+def up_far_call(channels, bound, kept, pieces, weight):
     layer = (2 * PY, 2 * PX, channels)
     return pl.pallas_call(
-        upconv_kernel,
-        out_shape=[
-            pltpu.VMEM((2,) + layer, jnp.bfloat16),
-            pltpu.VMEM(layer, jnp.bfloat16),
-            pltpu.VMEM(layer, jnp.bfloat16),
-        ],
+        up_far_kernel,
+        out_shape=[pltpu.VMEM(kept.shape, jnp.bfloat16), pltpu.VMEM(layer, jnp.bfloat16)],
         in_specs=[VMEM] * (3 + len(pieces)),
-        out_specs=[VMEM] * 3,
-        scratch_shapes=[pltpu.VMEM((2,) + layer, jnp.float32)],
+        out_specs=[VMEM] * 2,
+        scratch_shapes=[pltpu.VMEM(layer, jnp.float32)],
         compiler_params=limit(8),
-        name="upconv",
+        name="up_far",
     )(*map(in_vmem, (bound, kept, *pieces, weight)))
 
 
@@ -416,22 +413,23 @@
                 ].reshape(rows, channels)
 
 
-def conv_local_kernel(up_ref, weight, out_ref, padded, patches):
-    depth, height, breadth, channels = up_ref.shape
+def conv_local_kernel(
+    feature_ref, far_ref, w_up, weight, near_ref, out_ref, grid, padded, patches
+):
+    height, breadth, channels = near_ref.shape
     rows = height * breadth
     span = 9 * channels
+    even = lax.rem(lax.axis_index("brick"), 2) == 0
+    odd = lax.rem(lax.axis_index("brick"), 2)
+    near, far = up_layer(feature_ref[...], w_up, 1 - odd, grid), far_ref[...]
+    near_ref[...] = near
+    layers = [jnp.where(even, far, near), jnp.where(even, near, far)]
     zero = jnp.zeros((), jnp.bfloat16)
-    fill_patches([jnp.maximum(up_ref[z], zero) for z in range(depth)], padded, patches)
-    out_ref[...] = up_ref[...].reshape(depth * rows, channels).astype(jnp.float32) + dot(
-        patches[...], weight[span : 2 * span, :]
-    )
-    for z in range(depth - 1):
-        out_ref[z * rows : (z + 1) * rows, :] += dot(
-            patches[(z + 1) * rows : (z + 2) * rows, :], weight[2 * span :, :]
-        )
-        out_ref[(z + 1) * rows : (z + 2) * rows, :] += dot(
-            patches[z * rows : (z + 1) * rows, :], weight[:span, :]
-        )
+    fill_patches([jnp.maximum(layer, zero) for layer in layers], padded, patches)
+    both = jnp.concatenate([layer.reshape(rows, channels) for layer in layers], axis=0)
+    out_ref[...] = both.astype(jnp.float32) + dot(patches[...], weight[span : 2 * span, :])
+    out_ref[:rows, :] += dot(patches[rows:, :], weight[2 * span :, :])
+    out_ref[rows:, :] += dot(patches[:rows, :], weight[:span, :])
 
 
 def conv_halo_kernel(part_ref, near_ref, far_ref, weight, out_ref, padded, patches):
@@ -442,7 +440,8 @@
     even = lax.rem(position, 2) == 0
     edge = (position == 0) | (position == lax.axis_size("brick") - 1)
     near, far = near_ref[...], far_ref[...]
-    far = jnp.where(edge, jnp.zeros_like(far), far)
+    near = jnp.maximum(near, jnp.zeros((), jnp.bfloat16))
+    far = jnp.where(edge, jnp.zeros_like(far), jnp.maximum(far, jnp.zeros((), jnp.bfloat16)))
     fill_patches([jnp.where(even, far, near), jnp.where(even, near, far)], padded, patches)
     for z in range(depth):
         total = part_ref[z * rows : (z + 1) * rows, :]
@@ -460,19 +459,23 @@
     ]
 
 
-def conv_local_call(upsampled, weight):
-    depth, height, breadth, channels = upsampled.shape
-    rows = depth * height * breadth
+def conv_local_call(feature, far, w_up, weight):
+    height, breadth, channels = far.shape
+    rows = 2 * height * breadth
     return pl.pallas_call(
         conv_local_kernel,
-        out_shape=pltpu.VMEM((rows, channels), jnp.float32),
-        in_specs=[VMEM] * 2,
-        out_specs=VMEM,
-        scratch_shapes=conv_scratch(depth, height, breadth, channels),
+        out_shape=[
+            pltpu.VMEM(far.shape, jnp.bfloat16),
+            pltpu.VMEM((rows, channels), jnp.float32),
+        ],
+        in_specs=[VMEM] * 4,
+        out_specs=[VMEM] * 2,
+        scratch_shapes=[pltpu.VMEM(far.shape, jnp.float32)]
+        + conv_scratch(2, height, breadth, channels),
         compiler_params=limit(8),
         cost_estimate=cost(36 * rows * channels * channels, 12 * rows * channels),
         name="conv_local",
-    )(*map(in_vmem, (upsampled, weight)))
+    )(*map(in_vmem, (feature, far, w_up, weight)))
 
 
 def conv_halo_call(shape, part, near, far, weight):
@@ -537,12 +540,10 @@
     near = swap(near, 1, total)
     kept, *sent = gather_call(outer, masks, own, near, far, passing)
     pieces = [swap(sent[k - 1], k * WDEP, total) for k in range(outer - 1, 0, -1)]
-    upsampled, near, far = upconv_call(channels, bound, kept, pieces, w_upconv)
-    far = lax.ppermute(far, ("groups", "brick"), far_pairs(lax.axis_size("groups"), total))
-    part = conv_local_call(upsampled, w_conv)
-    near, part = lax.optimization_barrier((near, part))
-    near = swap(near, 1, total)
-    return conv_halo_call(upsampled.shape, part, near, far, w_conv)
+    feature, far = up_far_call(channels, bound, kept, pieces, w_upconv)
+    arrived = lax.ppermute(far, ("groups", "brick"), far_pairs(lax.axis_size("groups"), total))
+    near, part = conv_local_call(feature, far, w_upconv, w_conv)
+    return conv_halo_call((2, *far.shape), part, swap(near, 1, total), arrived, w_conv)
 
 
 def solution(mesh):

time: 29.4 us -> 29.2 us (level)
  transfers between devices with their start and end apart: 8 -> 8, of which waited for: 5 -> 5; matrix products, arithmetic and copies ran while one was open for 0% -> 0% of each run, Pallas kernels for 10% -> 11%
where the time goes in v8:
time: 29.2 us; the launch traced here: 29.1 us
  Pallas kernels  11.6 us (40%)
  starting transfers between devices  9.59 us (33%)
  waiting for transfers between devices  7.85 us (27%)
    ppermute x7, starting transfers between devices, swap(): lax.ppermute(values, 'brick', [(i, i ^ distance) for i in range(total)])  8.01 us
    pallas_call x1, Pallas kernels, far_call(): pl.pallas_call(window_kernel, out_shape=[out, out, rest, rest, pltpu.VMEM...  6.86 us
    ppermute x7, waiting for transfers between devices, swap(): lax.ppermute(values, 'brick', [(i, i ^ distance) for i in range(total)])  6.72 us
    pallas_call x1, Pallas kernels, near_call(): pl.pallas_call(functools.partial(near_kernel, outer, tokens), out_shape=[...  2.51 us
    ppermute x1, starting transfers between devices, on_device(): lax.ppermute(far, ('groups', 'brick'), far_pairs(lax.axis_size('groups'),...  1.58 us
    ppermute x1, waiting for transfers between devices, on_device(): lax.ppermute(far, ('groups', 'brick'), far_pairs(lax.axis_size('groups'),...  1.13 us
    pallas_call x1, Pallas kernels, conv_halo_call(): pl.pallas_call(conv_halo_kernel, out_shape=jax.ShapeDtypeStruct(shape, jn...  0.97 us
    pallas_call x1, Pallas kernels, conv_local_call(): pl.pallas_call(conv_local_kernel, out_shape=[pltpu.VMEM(far.shape, jnp.bf...  0.74 us
  transfers between devices with their start and end apart: 8, of which 5 were waited for; matrix products, arithmetic and copies ran while one was open for 0% of the time, Pallas kernels for 11%

profile of v8, /device:TPU:0, one launch (start us, length us, event | category | flops | bytes accessed | tf_op | source)
XLA Modules:
  0.0 29.1 jit_solution(17560313505482096887)
XLA Ops:
  0.0 6.9 %window_far.1 = (bf16[2,32,768]{2,1,0:T(8,128)(2,1)S(1)}, bf16[2,32,768]{2,1,0:T(8,128)(2,1)S(1)}, bf16[256,768]{1,0:T(8,128)(2,1)S(1)}, bf16[256,768]{1,0:T(8,1...) custom-call(s32[32]{0:T(128)} %anchor_ref.1, ...), custom_call_target="tpu_custom_call" | custom-call | tf_op jit(solution)/shard_map/window_far/pallas_call | solution.py:279
  6.9 3.0 %collective-permute-start = (bf16[2,32,768]{2,1,0:T(8,128)(2,1)S(1)}, bf16[2,32,768]{2,1,0:T(8,128)(2,1)S(1)}, u32[]{:S(2)}, u32[]{:S(2)}) collective-permute-start(bf16[2,32,768]{2,1,0:T(8,128)(2,1)S(1)} %get-tuple-element.39), channel_id=1, source_target_pairs={{0,2},{1,3},{2,0},{3,1},{4,6},{5,7},{6,4},{7,5},{8,10},{9,11},{10,... | collective-permute-start | bytes 294920 | tf_op jit(solution)/shard_map/ppermute | solution.py:494
  9.9 0.0 collective-permute-start.2
  9.9 2.5 %window_near.1 = (bf16[2,32,768]{2,1,0:T(8,128)(2,1)S(1)}, bf16[2,32,768]{2,1,0:T(8,128)(2,1)S(1)}, f32[32,128]{1,0:T(8,128)S(1)}, f32[8,128]{1,0:T(8,128)S(1)}) custom-call(s32[32]{0:T(128)} %anchor_ref.1, s32[1,32]{1,0:T(1,128)} %bitcast.2, s32[1,32]{1,0:T(1,128)} %bitcast.3, bf16[256,768]{1,0:T(8,128)(2,1)S(1)} %get-tuple-element.28.rest_mixed, ...), custom_call_target="tpu_custom_call" | custom-call | flops 905969664 | bytes 393216 | tf_op jit(solution)/shard_map/window_near/pallas_call | solution.py:311
  12.4 0.0 copy-start.1
  12.4 0.6 %collective-permute-done.far = bf16[2,32,768]{2,1,0:T(8,128)(2,1)S(1)} collective-permute-done((bf16[2,32,768]{2,1,0:T(8,128)(2,1)S(1)}, bf16[2,32,768]{2,1,0:T(8,128)(2,1)S(1)}, u32[]{:S(2)}, u32[]{:S(2)}) %collective-permute-start) | collective-permute-done | bytes 98336 | tf_op jit(solution)/shard_map/ppermute | solution.py:494
  13.0 0.0 collective-permute-start.1
  13.0 1.8 %collective-permute-done.2.forward = bf16[2,32,768]{2,1,0:T(8,128)(2,1)S(1)} collective-permute-done((bf16[2,32,768]{2,1,0:T(8,128)(2,1)S(1)}, bf16[2,32,768]{2,1,0:T(8,128)(2,1)S(1)}, u32[]{:S(2)}, u32[]{:S(2)}) %collective-permute-start.2) | collective-permute-done | bytes 98336 | tf_op jit(solution)/shard_map/ppermute | solution.py:494
  14.8 0.0 collective-permute-done.1.near
  14.8 0.2 plane_sum.1
  15.0 3.8 %collective-permute-start.3 = (bf16[32,768]{1,0:T(8,128)(2,1)S(1)}, bf16[32,768]{1,0:T(8,128)(2,1)S(1)}, u32[]{:S(2)}, u32[]{:S(2)}) collective-permute-start(bf16[32,768]{1,0:T(8,128)(2,1)S(1)} %get-tuple-element.44), channel_id=1, source_target_pairs={{0,12},{1,13},{2,14},{3,15},{4,8},{5,9},{6,10},{7,11},{8,4},{9,5},... | collective-permute-start | bytes 147464 | tf_op jit(solution)/shard_map/ppermute | solution.py:494
  18.8 0.0 collective-permute-start.4
  18.8 0.6 %collective-permute-start.5 = (bf16[32,768]{1,0:T(8,128)(2,1)S(1)}, bf16[32,768]{1,0:T(8,128)(2,1)S(1)}, u32[]{:S(2)}, u32[]{:S(2)}) collective-permute-start(bf16[32,768]{1,0:T(8,128)(2,1)S(1)} %get-tuple-element.46), channel_id=1, source_target_pairs={{0,4},{1,5},{2,6},{3,7},{4,0},{5,1},{6,2},{7,3},{8,12},{9,13},{10,... | collective-permute-start | bytes 147464 | tf_op jit(solution)/shard_map/ppermute | solution.py:494
  19.5 1.5 %collective-permute-done.3.refs_0_ = bf16[32,768]{1,0:T(8,128)(2,1)S(1)} collective-permute-done((bf16[32,768]{1,0:T(8,128)(2,1)S(1)}, bf16[32,768]{1,0:T(8,128)(2,1)S(1)}, u32[]{:S(2)}, u32[]{:S(2)}) %collective-permute-start.3) | collective-permute-done | bytes 49184 | tf_op jit(solution)/shard_map/ppermute | solution.py:494
  21.0 2.8 %collective-permute-done.4.refs_1_ = bf16[32,768]{1,0:T(8,128)(2,1)S(1)} collective-permute-done((bf16[32,768]{1,0:T(8,128)(2,1)S(1)}, bf16[32,768]{1,0:T(8,128)(2,1)S(1)}, u32[]{:S(2)}, u32[]{:S(2)}) %collective-permute-start.4) | collective-permute-done | bytes 49184 | tf_op jit(solution)/shard_map/ppermute | solution.py:494
  23.8 0.0 collective-permute-done.5.refs_2_
  23.8 0.0 copy-done
  23.8 0.3 up_far.1
  24.1 1.6 %collective-permute-start.7 = (bf16[8,16,128]{2,1,0:T(8,128)(2,1)S(1)}, bf16[8,16,128]{2,1,0:T(8,128)(2,1)S(1)}, u32[]{:S(2)}, u32[]{:S(2)}) collective-permute-start(bf16[8,16,128]{2,1,0:T(8,128)(2,1)S(1)} %get-tuple-element.48.far_ref), channel_id=1, source_target_pairs={{1,2},{2,1},{3,4},{4,3},{5,6},{6,5},{7,8},{8,7},{9,10},{10,9},{11,... | collective-permute-start | bytes 98312 | tf_op jit(solution)/shard_map/ppermute | solution.py:544
  25.7 0.7 %conv_local.1 = (bf16[8,16,128]{2,1,0:T(8,128)(2,1)S(1)}, f32[256,128]{1,0:T(8,128)S(1)}) custom-call(bf16[32,768]{1,0:T(8,128)(2,1)S(1)} %get-tuple-element.47.feature_ref, bf16[8,16,128]{2,1,0:T(8,128)(2,1)S(1)} %get-tuple-element.48.far_ref, bf16[768,1024]{1,0:T(8,128)(2,1)S(1)} %copy-done, bf16[3456,128]{1,0:T(8,128)(2,1)S(1)} %copy-done.1), custom_call_target="tpu_custom_call" | custom-call | flops 150994944 | bytes 393216 | tf_op jit(solution)/shard_map/conv_local/pallas_call | solution.py:465
  26.4 0.5 %collective-permute-start.6 = (bf16[8,16,128]{2,1,0:T(8,128)(2,1)S(1)}, bf16[8,16,128]{2,1,0:T(8,128)(2,1)S(1)}, u32[]{:S(2)}, u32[]{:S(2)}) collective-permute-start(bf16[8,16,128]{2,1,0:T(8,128)(2,1)S(1)} %get-tuple-element.50), channel_id=1, source_target_pairs={{0,1},{1,0},{2,3},{3,2},{4,5},{5,4},{6,7},{7,6},{8,9},{9,8},{10,11... | collective-permute-start | bytes 98312 | tf_op jit(solution)/shard_map/ppermute | solution.py:494
  27.0 1.1 %collective-permute-done.7.far_ref = bf16[8,16,128]{2,1,0:T(8,128)(2,1)S(1)} collective-permute-done((bf16[8,16,128]{2,1,0:T(8,128)(2,1)S(1)}, bf16[8,16,128]{2,1,0:T(8,128)(2,1)S(1)}, u32[]{:S(2)}, u32[]{:S(2)}) %collective-permute-start.7) | collective-permute-done | bytes 32800 | tf_op jit(solution)/shard_map/ppermute | solution.py:544
  28.1 0.0 collective-permute-done.6.near_ref
  28.1 1.0 %conv_halo.1 = bf16[2,8,16,128]{3,2,1,0:T(8,128)(2,1)} custom-call(f32[256,128]{1,0:T(8,128)S(1)} %get-tuple-element.49.part_ref, bf16[8,16,128]{2,1,0:T(8,128)(2,1)S(1)} %collective-permute-done.6.near_ref, bf16[8,16,128]{2,1,0:T(8,128)(2,1)S(1)} %collective-permute-done.7.far_ref, bf16[3456,128]{1,0:T(8,128)(2,1)S(1)} %copy-done.1), custom_call_target="tpu_custom_call" | custom-call | tf_op jit(solution)/shard_map/conv_halo/pallas_call | solution.py:482
  (2 shorter events, 0.0 us)
Async XLA Ops:
  6.9 6.1 %collective-permute-start = (bf16[2,32,768]{2,1,0:T(8,128)(2,1)S(1)}, bf16[2,32,768]{2,1,0:T(8,128)(2,1)S(1)}, u32[]{:S(2)}, u32[]{:S(2)}) collective-permute-start(bf16[2,32,768]{2,1,0:T(8,128)(2,1)S(1)} %get-tuple-element.39), channel_id=1, source_target_pairs={{0,2},{1,3},{2,0},{3,1},{4,6},{5,7},{6,4},{7,5},{8,10},{9,11},{10,... | collective-permute-start | bytes 294920 | tf_op jit(solution)/shard_map/ppermute | solution.py:494
  9.9 4.9 %collective-permute-start.2 = (bf16[2,32,768]{2,1,0:T(8,128)(2,1)S(1)}, bf16[2,32,768]{2,1,0:T(8,128)(2,1)S(1)}, u32[]{:S(2)}, u32[]{:S(2)}) collective-permute-start(bf16[2,32,768]{2,1,0:T(8,128)(2,1)S(1)} %get-tuple-element.42), channel_id=1, source_target_pairs={{0,3},{1,2},{2,1},{3,0},{4,7},{5,6},{6,5},{7,4},{8,11},{9,10},{10,... | collective-permute-start | bytes 294920 | tf_op jit(solution)/shard_map/ppermute | solution.py:494
  9.9 14.0 %copy-start = (bf16[768,1024]{1,0:T(8,128)(2,1)S(1)}, bf16[768,1024]{1,0:T(8,128)(2,1)}, u32[]{:S(2)}) copy-start(bf16[768,1024]{1,0:T(8,128)(2,1)} %w_up.1) | copy-start | bytes 4718596
  12.4 13.3 %copy-start.1 = (bf16[3456,128]{1,0:T(8,128)(2,1)S(1)}, bf16[3456,128]{1,0:T(8,128)(2,1)}, u32[]{:S(2)}) copy-start(bf16[3456,128]{1,0:T(8,128)(2,1)} %weight.3) | copy-start | bytes 2654212
  13.0 1.8 %collective-permute-start.1 = (bf16[2,32,768]{2,1,0:T(8,128)(2,1)S(1)}, bf16[2,32,768]{2,1,0:T(8,128)(2,1)S(1)}, u32[]{:S(2)}, u32[]{:S(2)}) collective-permute-start(bf16[2,32,768]{2,1,0:T(8,128)(2,1)S(1)} %get-tuple-element.40), channel_id=1, source_target_pairs={{0,1},{1,0},{2,3},{3,2},{4,5},{5,4},{6,7},{7,6},{8,9},{9,8},{10,11... | collective-permute-start | bytes 294920 | tf_op jit(solution)/shard_map/ppermute | solution.py:494
  15.0 6.0 %collective-permute-start.3 = (bf16[32,768]{1,0:T(8,128)(2,1)S(1)}, bf16[32,768]{1,0:T(8,128)(2,1)S(1)}, u32[]{:S(2)}, u32[]{:S(2)}) collective-permute-start(bf16[32,768]{1,0:T(8,128)(2,1)S(1)} %get-tuple-element.44), channel_id=1, source_target_pairs={{0,12},{1,13},{2,14},{3,15},{4,8},{5,9},{6,10},{7,11},{8,4},{9,5},... | collective-permute-start | bytes 147464 | tf_op jit(solution)/shard_map/ppermute | solution.py:494
  18.8 5.0 %collective-permute-start.4 = (bf16[32,768]{1,0:T(8,128)(2,1)S(1)}, bf16[32,768]{1,0:T(8,128)(2,1)S(1)}, u32[]{:S(2)}, u32[]{:S(2)}) collective-permute-start(bf16[32,768]{1,0:T(8,128)(2,1)S(1)} %get-tuple-element.45), channel_id=1, source_target_pairs={{0,8},{1,9},{2,10},{3,11},{4,12},{5,13},{6,14},{7,15},{8,0},{9,1},... | collective-permute-start | bytes 147464 | tf_op jit(solution)/shard_map/ppermute | solution.py:494
  18.8 5.0 %collective-permute-start.5 = (bf16[32,768]{1,0:T(8,128)(2,1)S(1)}, bf16[32,768]{1,0:T(8,128)(2,1)S(1)}, u32[]{:S(2)}, u32[]{:S(2)}) collective-permute-start(bf16[32,768]{1,0:T(8,128)(2,1)S(1)} %get-tuple-element.46), channel_id=1, source_target_pairs={{0,4},{1,5},{2,6},{3,7},{4,0},{5,1},{6,2},{7,3},{8,12},{9,13},{10,... | collective-permute-start | bytes 147464 | tf_op jit(solution)/shard_map/ppermute | solution.py:494
  24.1 4.0 %collective-permute-start.7 = (bf16[8,16,128]{2,1,0:T(8,128)(2,1)S(1)}, bf16[8,16,128]{2,1,0:T(8,128)(2,1)S(1)}, u32[]{:S(2)}, u32[]{:S(2)}) collective-permute-start(bf16[8,16,128]{2,1,0:T(8,128)(2,1)S(1)} %get-tuple-element.48.far_ref), channel_id=1, source_target_pairs={{1,2},{2,1},{3,4},{4,3},{5,6},{6,5},{7,8},{8,7},{9,10},{10,9},{11,... | collective-permute-start | bytes 98312 | tf_op jit(solution)/shard_map/ppermute | solution.py:544
  26.4 1.7 %collective-permute-start.6 = (bf16[8,16,128]{2,1,0:T(8,128)(2,1)S(1)}, bf16[8,16,128]{2,1,0:T(8,128)(2,1)S(1)}, u32[]{:S(2)}, u32[]{:S(2)}) collective-permute-start(bf16[8,16,128]{2,1,0:T(8,128)(2,1)S(1)} %get-tuple-element.50), channel_id=1, source_target_pairs={{0,1},{1,0},{2,3},{3,2},{4,5},{5,4},{6,7},{7,6},{8,9},{9,8},{10,11... | collective-permute-start | bytes 98312 | tf_op jit(solution)/shard_map/ppermute | solution.py:494

commit v9 on v8

--- a/solution.py
+++ b/solution.py
@@ -94,12 +94,37 @@
         )
 
 
+def picked(rels, anchor_ref, count_ref, tok, mixed):
+    slots, tokens = tok.shape[1:3]
+    rows = slots * tokens
+    cells = tokens // WDEP
+    position = lax.axis_index("brick")
+    residue = lax.rem(position, WDEP)
+    places, scales = [], []
+    for s in range(slots):
+        slot = position * slots + s
+        factor = jnp.full((1, LANES), count_ref[slot], jnp.int32).astype(jnp.float32) * (
+            1.0 / (2.0 * tokens)
+        )
+        for rel in rels:
+            depth = lax.rem((residue ^ rel) + WDEP * NWRAP - anchor_ref[slot], WDEP)
+            places.append((s, depth))
+            scales.append(factor * bell_at(depth))
+    base, chosen = [], []
+    for m in range(2):
+        for s, depth in places:
+            base.append(tok[m, s, pl.ds(pl.multiple_of(depth * cells, cells), cells), :])
+            place = pl.multiple_of(m * rows + s * tokens + depth * cells, cells)
+            chosen.append(mixed[pl.ds(place, cells), :])
+    return scales, jnp.concatenate(base, axis=0), jnp.concatenate(chosen, axis=0)
+
+
 def window_kernel(*refs):
-    sources, outs, scratch = refs[:13], refs[13:22], refs[22:]
-    passing_out, far_out, rest_mixed, rest_base, rest_scale, wo, wu, wd = outs[:8]
-    gain_refs = (scratch[0], scratch[1], outs[8])
-    anchor_ref, count_ref, tok, wq, wk, wv, normed, q_all, k_all, v_all, mixed = scratch[2:13]
-    ffn_normed, ffn_hidden, sems = scratch[13:]
+    sources, outs, scratch = refs[:13], refs[13:21], refs[21:]
+    passing_out, far_out, mixed, tok, wo, wu, wd = outs[:7]
+    gain_refs = (scratch[0], scratch[1], outs[7])
+    anchor_ref, count_ref, wq, wk, wv, normed, q_all, k_all, v_all = scratch[2:11]
+    ffn_normed, ffn_hidden, sems = scratch[11:]
     slots, tokens, width = sources[5].shape
     rows = slots * tokens
     cells = tokens // WDEP
@@ -122,8 +147,6 @@
     ]
     for i in (5, 2, 6, 3, 7, 8, 9, 10, 11, 12, 0, 1, 4):
         copies[i].start()
-    position = lax.axis_index("brick")
-    residue = lax.rem(position, WDEP)
 
     copies[2].wait()
     copies[3].wait()
@@ -147,26 +170,7 @@
     for i in (0, 1, 4, 10, 11, 12):
         copies[i].wait()
 
-    def picked(rels):
-        places, scales = [], []
-        for s in range(slots):
-            slot = position * slots + s
-            factor = jnp.full((1, LANES), count_ref[slot], jnp.int32).astype(jnp.float32) * (
-                1.0 / (2.0 * tokens)
-            )
-            for rel in rels:
-                depth = lax.rem((residue ^ rel) + WDEP * NWRAP - anchor_ref[slot], WDEP)
-                places.append((s, depth))
-                scales.append(factor * bell_at(depth))
-        base, chosen = [], []
-        for m in range(2):
-            for s, depth in places:
-                base.append(tok[m, s, pl.ds(pl.multiple_of(depth * cells, cells), cells), :])
-                place = pl.multiple_of(m * rows + s * tokens + depth * cells, cells)
-                chosen.append(mixed[pl.ds(place, cells), :])
-        return scales, jnp.concatenate(base, axis=0), jnp.concatenate(chosen, axis=0)
-
-    scales, base, chosen = picked((2, 3))
+    scales, base, chosen = picked((2, 3), anchor_ref, count_ref, tok, mixed)
     joined = ffn_rows(
         base,
         chosen,
@@ -180,22 +184,17 @@
     for j, scale in enumerate(scales):
         out = (far_out, passing_out)[j % 2]
         out[j // 2] = (joined[j * cells : (j + 1) * cells] * scale[:, :1]).astype(jnp.bfloat16)
-    scales, base, chosen = picked((1, 0))
-    rest_base[...] = base
-    rest_mixed[...] = chosen
-    for j, scale in enumerate(scales):
-        rest_scale[j * cells : (j + 1) * cells, :] = jnp.broadcast_to(scale, (cells, LANES))
 
 
 def near_kernel(
     outer,
     tokens,
     anchor_ref,
+    count_ref,
     anchor_row,
     count_row,
-    rest_mixed,
-    rest_base,
-    rest_scale,
+    all_mixed,
+    tok,
     wo,
     wu,
     wd,
@@ -211,9 +210,10 @@
     position = lax.axis_index("brick")
     residue = lax.rem(position, WDEP)
     block = lax.div(position, WDEP)
+    scales, base, chosen = picked((1, 0), anchor_ref, count_ref, tok, all_mixed)
     joined = ffn_rows(
-        rest_base[...],
-        rest_mixed[...],
+        base,
+        chosen,
         gain[...][None, :],
         wo,
         wu,
@@ -221,10 +221,9 @@
         ffn_normed,
         ffn_hidden,
     )
-    joined = (joined * rest_scale[:, :1]).astype(jnp.bfloat16)
-    for s in range(slots):
-        near_out[s] = joined[2 * s * cells : (2 * s + 1) * cells]
-        own_out[s] = joined[(2 * s + 1) * cells : (2 * s + 2) * cells]
+    for j, scale in enumerate(scales):
+        out = (near_out, own_out)[j % 2]
+        out[j // 2] = (joined[j * cells : (j + 1) * cells] * scale[:, :1]).astype(jnp.bfloat16)
     for rel in range(WDEP):
         for s in range(slots):
             slot = (block * WDEP + (residue ^ rel)) * slots + s
@@ -281,19 +280,17 @@
         out_shape=[
             out,
             out,
-            rest,
-            rest,
-            pltpu.VMEM((half, LANES), jnp.float32),
+            big,
+            pltpu.VMEM((2, slots, tokens, width), jnp.bfloat16),
         ]
         + [pltpu.VMEM(w.shape, w.dtype) for w in weights[3:]]
         + [pltpu.VMEM((width,), jnp.float32)],
         in_specs=[ANY] * 13,
-        out_specs=[VMEM] * 9,
+        out_specs=[VMEM] * 8,
         scratch_shapes=[pltpu.VMEM((width,), jnp.float32)] * 2
         + [pltpu.SMEM(anchor.shape, jnp.int32)] * 2
-        + [pltpu.VMEM((2, slots, tokens, width), jnp.bfloat16)]
         + [pltpu.VMEM(w.shape, w.dtype) for w in weights[:3]]
-        + [big] * 5
+        + [big] * 4
         + [rest, pltpu.VMEM((half, weights[4].shape[1]), jnp.bfloat16)]
         + [pltpu.SemaphoreType.DMA((13,))],
         compiler_params=limit(24),
@@ -307,7 +304,7 @@
     cells = tokens // WDEP
     half = slots * (WDEP // 2) * cells
     out = pltpu.VMEM((slots, cells, width), jnp.bfloat16)
-    hidden = passed[4].shape[1]
+    hidden = passed[3].shape[1]
     return pl.pallas_call(
         functools.partial(near_kernel, outer, tokens),
         out_shape=[
@@ -316,7 +313,7 @@
             pltpu.VMEM((outer * WDEP * slots, LANES), jnp.float32),
             pltpu.VMEM((8, LANES), jnp.float32),
         ],
-        in_specs=[SMEM] + [VMEM] * 9,
+        in_specs=[SMEM] * 2 + [VMEM] * 8,
         out_specs=[VMEM] * 4,
         scratch_shapes=[
             pltpu.VMEM((2 * half, width), jnp.bfloat16),
@@ -325,7 +322,13 @@
         compiler_params=limit(12),
         cost_estimate=cost(12 * half * width * width, 4 * half * width),
         name="window_near",
-    )(in_hbm(anchor), in_hbm(anchor[None, :]), in_hbm(count[None, :]), *map(in_vmem, passed))
+    )(
+        in_hbm(anchor),
+        in_hbm(count),
+        in_hbm(anchor[None, :]),
+        in_hbm(count[None, :]),
+        *map(in_vmem, passed),
+    )
 
 
 def gather_kernel(outer, mask_ref, own, near, far, forward, kept, *sent):
@@ -539,7 +542,7 @@
     near, far = lax.optimization_barrier((near, far))
     near = swap(near, 1, total)
     kept, *sent = gather_call(outer, masks, own, near, far, passing)
-    pieces = [swap(sent[k - 1], k * WDEP, total) for k in range(outer - 1, 0, -1)]
+    pieces = [swap(sent[k - 1], k * WDEP, total) for k in sorted(range(1, outer), key=lambda k: (abs(2 * k - outer), -k))]
     feature, far = up_far_call(channels, bound, kept, pieces, w_upconv)
     arrived = lax.ppermute(far, ("groups", "brick"), far_pairs(lax.axis_size("groups"), total))
     near, part = conv_local_call(feature, far, w_upconv, w_conv)

time: 29.2 us -> 29.1 us (level)
  no operation moved by 1% of the time
where the time goes in v9:
time: 29.1 us; the launch traced here: 29 us
  Pallas kernels  11.5 us (40%)
  starting transfers between devices  9.51 us (33%)
  waiting for transfers between devices  7.87 us (27%)
    ppermute x7, starting transfers between devices, swap(): lax.ppermute(values, 'brick', [(i, i ^ distance) for i in range(total)])  7.93 us
    pallas_call x1, Pallas kernels, far_call(): pl.pallas_call(window_kernel, out_shape=[out, out, big, pltpu.VMEM((2, sl...  6.76 us
    ppermute x7, waiting for transfers between devices, swap(): lax.ppermute(values, 'brick', [(i, i ^ distance) for i in range(total)])  6.72 us
    pallas_call x1, Pallas kernels, near_call(): pl.pallas_call(functools.partial(near_kernel, outer, tokens), out_shape=[...  2.54 us
    ppermute x1, starting transfers between devices, on_device(): lax.ppermute(far, ('groups', 'brick'), far_pairs(lax.axis_size('groups'),...  1.58 us
    ppermute x1, waiting for transfers between devices, on_device(): lax.ppermute(far, ('groups', 'brick'), far_pairs(lax.axis_size('groups'),...  1.15 us
    pallas_call x1, Pallas kernels, conv_halo_call(): pl.pallas_call(conv_halo_kernel, out_shape=jax.ShapeDtypeStruct(shape, jn...  0.97 us
    pallas_call x1, Pallas kernels, conv_local_call(): pl.pallas_call(conv_local_kernel, out_shape=[pltpu.VMEM(far.shape, jnp.bf...  0.74 us
  transfers between devices with their start and end apart: 8, of which 5 were waited for; matrix products, arithmetic and copies ran while one was open for 0% of the time, Pallas kernels for 11%

profile of v9, /device:TPU:0, one launch (start us, length us, event | category | flops | bytes accessed | tf_op | source)
XLA Modules:
  0.0 29.0 jit_solution(14657495225140125652)
XLA Ops:
  0.0 6.8 %window_far.1 = (bf16[2,32,768]{2,1,0:T(8,128)(2,1)S(1)}, bf16[2,32,768]{2,1,0:T(8,128)(2,1)S(1)}, bf16[512,768]{1,0:T(8,128)(2,1)S(1)}, bf16[2,2,128,768]{3,2,1...) custom-call(s32[32]{0:T(128)} %anchor_ref.1, ...), custom_call_target="tpu_custom_call" | custom-call | tf_op jit(solution)/shard_map/window_far/pallas_call | solution.py:278
  6.8 3.0 %collective-permute-start = (bf16[2,32,768]{2,1,0:T(8,128)(2,1)S(1)}, bf16[2,32,768]{2,1,0:T(8,128)(2,1)S(1)}, u32[]{:S(2)}, u32[]{:S(2)}) collective-permute-start(bf16[2,32,768]{2,1,0:T(8,128)(2,1)S(1)} %get-tuple-element.37), channel_id=1, source_target_pairs={{0,2},{1,3},{2,0},{3,1},{4,6},{5,7},{6,4},{7,5},{8,10},{9,11},{10,... | collective-permute-start | bytes 294920 | tf_op jit(solution)/shard_map/ppermute | solution.py:497
  9.8 0.0 collective-permute-start.2
  9.8 2.5 %window_near.1 = (bf16[2,32,768]{2,1,0:T(8,128)(2,1)S(1)}, bf16[2,32,768]{2,1,0:T(8,128)(2,1)S(1)}, f32[32,128]{1,0:T(8,128)S(1)}, f32[8,128]{1,0:T(8,128)S(1)}) custom-call(s32[32]{0:T(128)} %anchor_ref.1, s32[32]{0:T(128)} %count_ref.1, s32[1,32]{1,0:T(1,128)} %bitcast.2, s32[1,32]{1,0:T(1,128)} %bitcast.3, ...), custom_call_target="tpu_custom_call" | custom-call | flops 905969664 | bytes 393216 | tf_op jit(solution)/shard_map/window_near/pallas_call | solution.py:308
  12.3 0.0 copy-start.1
  12.3 0.5 %collective-permute-done.far = bf16[2,32,768]{2,1,0:T(8,128)(2,1)S(1)} collective-permute-done((bf16[2,32,768]{2,1,0:T(8,128)(2,1)S(1)}, bf16[2,32,768]{2,1,0:T(8,128)(2,1)S(1)}, u32[]{:S(2)}, u32[]{:S(2)}) %collective-permute-start) | collective-permute-done | bytes 98336 | tf_op jit(solution)/shard_map/ppermute | solution.py:497
  12.9 0.0 collective-permute-start.1
  12.9 1.8 %collective-permute-done.2.forward = bf16[2,32,768]{2,1,0:T(8,128)(2,1)S(1)} collective-permute-done((bf16[2,32,768]{2,1,0:T(8,128)(2,1)S(1)}, bf16[2,32,768]{2,1,0:T(8,128)(2,1)S(1)}, u32[]{:S(2)}, u32[]{:S(2)}) %collective-permute-start.2) | collective-permute-done | bytes 98336 | tf_op jit(solution)/shard_map/ppermute | solution.py:497
  14.7 0.0 collective-permute-done.1.near
  14.7 0.2 plane_sum.1
  14.9 2.8 %collective-permute-start.3 = (bf16[32,768]{1,0:T(8,128)(2,1)S(1)}, bf16[32,768]{1,0:T(8,128)(2,1)S(1)}, u32[]{:S(2)}, u32[]{:S(2)}) collective-permute-start(bf16[32,768]{1,0:T(8,128)(2,1)S(1)} %get-tuple-element.42), channel_id=1, source_target_pairs={{0,8},{1,9},{2,10},{3,11},{4,12},{5,13},{6,14},{7,15},{8,0},{9,1},... | collective-permute-start | bytes 147464 | tf_op jit(solution)/shard_map/ppermute | solution.py:497
  17.7 1.4 %collective-permute-start.4 = (bf16[32,768]{1,0:T(8,128)(2,1)S(1)}, bf16[32,768]{1,0:T(8,128)(2,1)S(1)}, u32[]{:S(2)}, u32[]{:S(2)}) collective-permute-start(bf16[32,768]{1,0:T(8,128)(2,1)S(1)} %get-tuple-element.43), channel_id=1, source_target_pairs={{0,12},{1,13},{2,14},{3,15},{4,8},{5,9},{6,10},{7,11},{8,4},{9,5},... | collective-permute-start | bytes 147464 | tf_op jit(solution)/shard_map/ppermute | solution.py:497
  19.1 0.2 collective-permute-start.5
  19.3 1.2 %collective-permute-done.3.refs_0_ = bf16[32,768]{1,0:T(8,128)(2,1)S(1)} collective-permute-done((bf16[32,768]{1,0:T(8,128)(2,1)S(1)}, bf16[32,768]{1,0:T(8,128)(2,1)S(1)}, u32[]{:S(2)}, u32[]{:S(2)}) %collective-permute-start.3) | collective-permute-done | bytes 49184 | tf_op jit(solution)/shard_map/ppermute | solution.py:497
  20.5 3.2 %collective-permute-done.4.refs_1_ = bf16[32,768]{1,0:T(8,128)(2,1)S(1)} collective-permute-done((bf16[32,768]{1,0:T(8,128)(2,1)S(1)}, bf16[32,768]{1,0:T(8,128)(2,1)S(1)}, u32[]{:S(2)}, u32[]{:S(2)}) %collective-permute-start.4) | collective-permute-done | bytes 49184 | tf_op jit(solution)/shard_map/ppermute | solution.py:497
  23.7 0.0 collective-permute-done.5.refs_2_
  23.7 0.0 copy-done
  23.7 0.3 up_far.1
  24.0 1.6 %collective-permute-start.7 = (bf16[8,16,128]{2,1,0:T(8,128)(2,1)S(1)}, bf16[8,16,128]{2,1,0:T(8,128)(2,1)S(1)}, u32[]{:S(2)}, u32[]{:S(2)}) collective-permute-start(bf16[8,16,128]{2,1,0:T(8,128)(2,1)S(1)} %get-tuple-element.46.far_ref), channel_id=1, source_target_pairs={{1,2},{2,1},{3,4},{4,3},{5,6},{6,5},{7,8},{8,7},{9,10},{10,9},{11,... | collective-permute-start | bytes 98312 | tf_op jit(solution)/shard_map/ppermute | solution.py:547
  25.6 0.7 %conv_local.1 = (bf16[8,16,128]{2,1,0:T(8,128)(2,1)S(1)}, f32[256,128]{1,0:T(8,128)S(1)}) custom-call(bf16[32,768]{1,0:T(8,128)(2,1)S(1)} %get-tuple-element.45.feature_ref, bf16[8,16,128]{2,1,0:T(8,128)(2,1)S(1)} %get-tuple-element.46.far_ref, bf16[768,1024]{1,0:T(8,128)(2,1)S(1)} %copy-done, bf16[3456,128]{1,0:T(8,128)(2,1)S(1)} %copy-done.1), custom_call_target="tpu_custom_call" | custom-call | flops 150994944 | bytes 393216 | tf_op jit(solution)/shard_map/conv_local/pallas_call | solution.py:468
  26.3 0.5 %collective-permute-start.6 = (bf16[8,16,128]{2,1,0:T(8,128)(2,1)S(1)}, bf16[8,16,128]{2,1,0:T(8,128)(2,1)S(1)}, u32[]{:S(2)}, u32[]{:S(2)}) collective-permute-start(bf16[8,16,128]{2,1,0:T(8,128)(2,1)S(1)} %get-tuple-element.48), channel_id=1, source_target_pairs={{0,1},{1,0},{2,3},{3,2},{4,5},{5,4},{6,7},{7,6},{8,9},{9,8},{10,11... | collective-permute-start | bytes 98312 | tf_op jit(solution)/shard_map/ppermute | solution.py:497
  26.8 1.1 %collective-permute-done.7.far_ref = bf16[8,16,128]{2,1,0:T(8,128)(2,1)S(1)} collective-permute-done((bf16[8,16,128]{2,1,0:T(8,128)(2,1)S(1)}, bf16[8,16,128]{2,1,0:T(8,128)(2,1)S(1)}, u32[]{:S(2)}, u32[]{:S(2)}) %collective-permute-start.7) | collective-permute-done | bytes 32800 | tf_op jit(solution)/shard_map/ppermute | solution.py:547
  28.0 0.0 collective-permute-done.6.near_ref
  28.0 1.0 %conv_halo.1 = bf16[2,8,16,128]{3,2,1,0:T(8,128)(2,1)} custom-call(f32[256,128]{1,0:T(8,128)S(1)} %get-tuple-element.47.part_ref, bf16[8,16,128]{2,1,0:T(8,128)(2,1)S(1)} %collective-permute-done.6.near_ref, bf16[8,16,128]{2,1,0:T(8,128)(2,1)S(1)} %collective-permute-done.7.far_ref, bf16[3456,128]{1,0:T(8,128)(2,1)S(1)} %copy-done.1), custom_call_target="tpu_custom_call" | custom-call | tf_op jit(solution)/shard_map/conv_halo/pallas_call | solution.py:485
  (2 shorter events, 0.0 us)
Async XLA Ops:
  6.8 6.1 %collective-permute-start = (bf16[2,32,768]{2,1,0:T(8,128)(2,1)S(1)}, bf16[2,32,768]{2,1,0:T(8,128)(2,1)S(1)}, u32[]{:S(2)}, u32[]{:S(2)}) collective-permute-start(bf16[2,32,768]{2,1,0:T(8,128)(2,1)S(1)} %get-tuple-element.37), channel_id=1, source_target_pairs={{0,2},{1,3},{2,0},{3,1},{4,6},{5,7},{6,4},{7,5},{8,10},{9,11},{10,... | collective-permute-start | bytes 294920 | tf_op jit(solution)/shard_map/ppermute | solution.py:497
  9.8 4.9 %collective-permute-start.2 = (bf16[2,32,768]{2,1,0:T(8,128)(2,1)S(1)}, bf16[2,32,768]{2,1,0:T(8,128)(2,1)S(1)}, u32[]{:S(2)}, u32[]{:S(2)}) collective-permute-start(bf16[2,32,768]{2,1,0:T(8,128)(2,1)S(1)} %get-tuple-element.40), channel_id=1, source_target_pairs={{0,3},{1,2},{2,1},{3,0},{4,7},{5,6},{6,5},{7,4},{8,11},{9,10},{10,... | collective-permute-start | bytes 294920 | tf_op jit(solution)/shard_map/ppermute | solution.py:497
  9.8 13.9 %copy-start = (bf16[768,1024]{1,0:T(8,128)(2,1)S(1)}, bf16[768,1024]{1,0:T(8,128)(2,1)}, u32[]{:S(2)}) copy-start(bf16[768,1024]{1,0:T(8,128)(2,1)} %w_up.1) | copy-start | bytes 4718596
  12.3 13.3 %copy-start.1 = (bf16[3456,128]{1,0:T(8,128)(2,1)S(1)}, bf16[3456,128]{1,0:T(8,128)(2,1)}, u32[]{:S(2)}) copy-start(bf16[3456,128]{1,0:T(8,128)(2,1)} %weight.3) | copy-start | bytes 2654212
  12.9 1.8 %collective-permute-start.1 = (bf16[2,32,768]{2,1,0:T(8,128)(2,1)S(1)}, bf16[2,32,768]{2,1,0:T(8,128)(2,1)S(1)}, u32[]{:S(2)}, u32[]{:S(2)}) collective-permute-start(bf16[2,32,768]{2,1,0:T(8,128)(2,1)S(1)} %get-tuple-element.38), channel_id=1, source_target_pairs={{0,1},{1,0},{2,3},{3,2},{4,5},{5,4},{6,7},{7,6},{8,9},{9,8},{10,11... | collective-permute-start | bytes 294920 | tf_op jit(solution)/shard_map/ppermute | solution.py:497
  14.9 5.6 %collective-permute-start.3 = (bf16[32,768]{1,0:T(8,128)(2,1)S(1)}, bf16[32,768]{1,0:T(8,128)(2,1)S(1)}, u32[]{:S(2)}, u32[]{:S(2)}) collective-permute-start(bf16[32,768]{1,0:T(8,128)(2,1)S(1)} %get-tuple-element.42), channel_id=1, source_target_pairs={{0,8},{1,9},{2,10},{3,11},{4,12},{5,13},{6,14},{7,15},{8,0},{9,1},... | collective-permute-start | bytes 147464 | tf_op jit(solution)/shard_map/ppermute | solution.py:497
  17.7 6.0 %collective-permute-start.4 = (bf16[32,768]{1,0:T(8,128)(2,1)S(1)}, bf16[32,768]{1,0:T(8,128)(2,1)S(1)}, u32[]{:S(2)}, u32[]{:S(2)}) collective-permute-start(bf16[32,768]{1,0:T(8,128)(2,1)S(1)} %get-tuple-element.43), channel_id=1, source_target_pairs={{0,12},{1,13},{2,14},{3,15},{4,8},{5,9},{6,10},{7,11},{8,4},{9,5},... | collective-permute-start | bytes 147464 | tf_op jit(solution)/shard_map/ppermute | solution.py:497
  19.1 4.6 %collective-permute-start.5 = (bf16[32,768]{1,0:T(8,128)(2,1)S(1)}, bf16[32,768]{1,0:T(8,128)(2,1)S(1)}, u32[]{:S(2)}, u32[]{:S(2)}) collective-permute-start(bf16[32,768]{1,0:T(8,128)(2,1)S(1)} %get-tuple-element.44), channel_id=1, source_target_pairs={{0,4},{1,5},{2,6},{3,7},{4,0},{5,1},{6,2},{7,3},{8,12},{9,13},{10,... | collective-permute-start | bytes 147464 | tf_op jit(solution)/shard_map/ppermute | solution.py:497
  24.0 4.0 %collective-permute-start.7 = (bf16[8,16,128]{2,1,0:T(8,128)(2,1)S(1)}, bf16[8,16,128]{2,1,0:T(8,128)(2,1)S(1)}, u32[]{:S(2)}, u32[]{:S(2)}) collective-permute-start(bf16[8,16,128]{2,1,0:T(8,128)(2,1)S(1)} %get-tuple-element.46.far_ref), channel_id=1, source_target_pairs={{1,2},{2,1},{3,4},{4,3},{5,6},{6,5},{7,8},{8,7},{9,10},{10,9},{11,... | collective-permute-start | bytes 98312 | tf_op jit(solution)/shard_map/ppermute | solution.py:547
  26.3 1.7 %collective-permute-start.6 = (bf16[8,16,128]{2,1,0:T(8,128)(2,1)S(1)}, bf16[8,16,128]{2,1,0:T(8,128)(2,1)S(1)}, u32[]{:S(2)}, u32[]{:S(2)}) collective-permute-start(bf16[8,16,128]{2,1,0:T(8,128)(2,1)S(1)} %get-tuple-element.48), channel_id=1, source_target_pairs={{0,1},{1,0},{2,3},{3,2},{4,5},{5,4},{6,7},{7,6},{8,9},{9,8},{10,11... | collective-permute-start | bytes 98312 | tf_op jit(solution)/shard_map/ppermute | solution.py:497
